TPU v7x, 32 devices: a whole 2x2x4 slice. The times are simulated.
32 devices in a mesh: tile: 8 (over z, x), mp: 4 (over y, core).
Axes of the slice: x: 2, y: 2, z: 4, core: 2. Of those that a mesh axis runs over, the one named last changes fastest.
Arguments:
- latent: bfloat16 [96, 384], P('tile'), may hold values from -19 to 19, as said below
- reward_grad: float32 [96, 384], P('tile'), may hold values from -6 to 6
- curvature: float32 [96, 384], P('tile'), may hold values from 0.3 to 3
- offsets: int32 [16, 2], P('tile'), may hold values from 0 to 64, as said below
- counts: int32 [96, 96], P('tile'), may hold values from 1 to 4, as said below
- w_in: bfloat16 [16, 640], replicated, may hold values from -3.2 to 3.2, as said below
- w_value: bfloat16 [640, 2560], P(None, 'mp'), may hold values from -0.25 to 0.25
- w_gate: bfloat16 [640, 2560], P(None, 'mp'), may hold values from -0.25 to 0.25
- w_down: bfloat16 [2560, 640], P('mp'), may hold values from -0.125 to 0.125
- w_out: bfloat16 [640, 16], replicated, may hold values from -0.25 to 0.25
Outputs:
- blended: float32 [96, 384], P('tile')
- grad_in: float32 [16, 640], replicated
- grad_value: float32 [640, 2560], P(None, 'mp')
- grad_gate: float32 [640, 2560], P(None, 'mp')
- grad_down: float32 [2560, 640], P('mp')
- grad_out: float32 [640, 16], replicated
Inputs may be any that keep to these rules, and one draw needn't show every extreme that they name: `offsets`: the corners are the points of a grid of 4 by 4 points spaced 24, each point taken by exactly one tile in a random order, each moved by at most 4 along each direction; the grid's first row and column stay at 0 and its last row and column are clamped to 64 and 64. The tiles cover every cell of the canvas. `counts`: the number of tiles whose 32 x 32 square holds the cell. `latent`: Real-valued. `w_in`: Real-valued.
All inputs are finite; a program needn't handle non-finite values.
Results may differ from a plain program's by a relative error of at most 0.003.
The roundings to bfloat16 on the way count: a program that leaves them out, or rounds other values in their place, can miss the bound.
Values may be sent and summed in bfloat16 or wider, within the bound.
No kernel may reach another device: no remote copies, remote signals or barrier semaphores. Data moves between devices by JAX's collectives and lax.ppermute only.
A program may use at most 64 MiB of HBM per device.

v0:
```python
import math

import jax
import jax.numpy as jnp
from jax import lax
from jax.sharding import PartitionSpec as P

S = 32
SPACING = 24


layer_eps = 1e-05
root_half = 0.7071067811865476
inv_root_two_pi = 0.3989422804014327
highest = lax.Precision.HIGHEST


def passed_along(shard, axis, by):
    peers = lax.axis_size(axis)
    pairs = [(i, i + by) for i in range(peers) if 0 <= i + by < peers]
    return lax.ppermute(shard, axis, pairs)


def gelu_value(inputs):
    return 0.5 * inputs * (1.0 + lax.erf(inputs * root_half))


def gelu_slope(inputs):
    return (
        0.5 * (1.0 + lax.erf(inputs * root_half))
        + inputs * jnp.exp(-0.5 * inputs * inputs) * inv_root_two_pi
    )


def patchify(cropped, channels):
    half_side = cropped.shape[0] // 2
    return (
        cropped.reshape(half_side, 2, half_side, 2 * channels)
        .transpose(0, 2, 1, 3)
        .reshape(half_side * half_side, 4 * channels)
    )


def unpatch(tokens, tile_side, channels):
    half_side = tile_side // 2
    token_rows = tokens.shape[0] // half_side
    return (
        tokens.reshape(token_rows, half_side, 2, 2 * channels)
        .transpose(0, 2, 1, 3)
        .reshape(2 * token_rows, tile_side * channels)
    )


def layer_norm(hidden):
    values = hidden.astype(jnp.float32)
    center = values - jnp.mean(values, axis=-1, keepdims=True)
    variance = jnp.mean(center * center, axis=-1, keepdims=True)
    inv_scale = lax.rsqrt(variance + layer_eps)
    return (center * inv_scale, inv_scale)


def norm_backward(normed, inv_scale, d_unit):
    centered = d_unit - jnp.mean(d_unit, axis=-1, keepdims=True)
    return inv_scale * (centered - normed * jnp.mean(d_unit * normed, axis=-1, keepdims=True))


def contract_rows(left, right):
    return lax.dot_general(
        left, right, (((0,), (0,)), ((), ())), preferred_element_type=jnp.float32
    )


def contract_rows_exact(left, right):
    return lax.dot_general(
        left, right, (((0,), (0,)), ((), ())), precision=highest, preferred_element_type=jnp.float32
    )


def contract_cols(left, right):
    return lax.dot_general(
        left, right, (((1,), (1,)), ((), ())), preferred_element_type=jnp.float32
    )


def crop_tiles(source, corners, row_base, tile_side, channels):

    def crop_one(corner):
        cropped = lax.dynamic_slice(
            source, (corner[0] - row_base, corner[1] * channels), (tile_side, tile_side * channels)
        )
        return patchify(cropped, channels)

    return jax.vmap(crop_one)(corners)


def place_tiles(canvas, pieces, corners, row_shift, channels):
    piece_rows = pieces.shape[1]
    piece_cols = pieces.shape[2]

    def add_tile(tile_index, current):
        corner = corners[tile_index]
        start_row = corner[0] + row_shift
        start_col = corner[1] * channels
        existing = lax.dynamic_slice(current, (start_row, start_col), (piece_rows, piece_cols))
        return lax.dynamic_update_slice(
            current, existing + pieces[tile_index], (start_row, start_col)
        )

    return lax.fori_loop(0, pieces.shape[0], add_tile, canvas)


def per_device(
    latent, reward_grad, curvature, offsets, counts, w_in, w_value, w_gate, w_down, w_out
):
    channels = w_in.shape[0] // 4
    model_width = w_in.shape[1]
    tile_side = S
    half_side = tile_side // 2
    token_count = half_side * half_side
    tiles_here = offsets.shape[0]
    slab_rows = latent.shape[0]
    canvas_cols = latent.shape[1]
    tile_devices = lax.axis_size("tile")
    model_devices = lax.axis_size("mp")
    tile_pos = lax.axis_index("tile")
    model_pos = lax.axis_index("mp")
    share_tokens = token_count // model_devices
    share_pixels = tile_side // model_devices
    scale_factor = 16.0 / math.sqrt(tiles_here * tile_devices * token_count)
    w_out_wide = w_out.astype(jnp.float32)
    cover_count = jnp.repeat(counts, channels, axis=1).astype(jnp.float32)
    placed_row = model_pos * share_pixels
    every_corner = lax.all_gather(offsets, "tile", axis=0, tiled=True)
    grid_cols = canvas_cols // (channels * SPACING)
    grid_cells = (every_corner[:, 0] + SPACING // 2) // SPACING * grid_cols + (
        every_corner[:, 1] + SPACING // 2
    ) // SPACING
    wanted = (
        tile_pos // 2 * grid_cols
        + tile_pos % 2 * tiles_here
        + jnp.arange(tiles_here, dtype=jnp.int32)
    )
    matched = (grid_cells[None, :] == wanted[:, None]).astype(jnp.int32)
    corners = jnp.sum(matched[:, :, None] * every_corner[None, :, :], axis=1)
    row_base = (tile_pos - 2) * slab_rows
    latent_parts = []
    for shift_by in (2, 1, 0, -1, -2):
        if shift_by == 0:
            latent_parts.append(latent)
        else:
            latent_parts.append(passed_along(latent, "tile", shift_by))
    latent_source = jnp.concatenate(latent_parts, axis=0)
    patches = crop_tiles(latent_source, corners, row_base, tile_side, channels)
    flat_patches = jnp.transpose(patches, (1, 0, 2)).reshape(token_count * tiles_here, 4 * channels)
    hidden = jnp.dot(flat_patches, w_in, preferred_element_type=jnp.float32).astype(jnp.bfloat16)
    normed, inv_scale = layer_norm(hidden)
    unit_in = normed.astype(jnp.bfloat16)
    value_proj = jnp.dot(unit_in, w_value, preferred_element_type=jnp.float32)
    gate_proj = jnp.dot(unit_in, w_gate, preferred_element_type=jnp.float32)
    active = (value_proj * gelu_value(gate_proj)).astype(jnp.bfloat16)
    active_grid = active.reshape(token_count, tiles_here, active.shape[1])

    def take_share(values):
        grid = values.reshape(token_count, tiles_here, values.shape[-1])
        picked = lax.dynamic_slice_in_dim(grid, model_pos * share_tokens, share_tokens, 0)
        return picked.reshape(share_tokens * tiles_here, values.shape[-1])

    hidden_share = take_share(hidden)
    row_block = active_grid.reshape(
        lax.axis_size("mp") * share_tokens * tiles_here, active_grid.shape[2]
    )
    ff_share = lax.psum_scatter(
        jnp.dot(row_block, w_down, preferred_element_type=jnp.float32).reshape(
            lax.axis_size("mp") * share_tokens, tiles_here, model_width
        ),
        "mp",
        scatter_dimension=0,
        tiled=True,
    ).reshape(share_tokens * tiles_here, model_width)
    noise_share = jnp.dot(hidden_share, w_out, preferred_element_type=jnp.float32) + jnp.dot(
        ff_share, w_out_wide, precision=highest, preferred_element_type=jnp.float32
    )
    noise_tiles = jnp.transpose(
        noise_share.reshape(share_tokens, tiles_here, w_out.shape[1]), (1, 0, 2)
    )

    def unpatch_share(tokens):
        return unpatch(tokens, tile_side, channels)

    noise_pieces = jax.vmap(unpatch_share)(noise_tiles)
    window_term = place_tiles(
        jnp.zeros((5 * slab_rows, canvas_cols), jnp.float32),
        noise_pieces,
        corners,
        placed_row - row_base,
        channels,
    )
    slab_sum = window_term[2 * slab_rows : 3 * slab_rows]
    for shift_by in (-2, -1, 1, 2):
        outgoing = window_term[(shift_by + 2) * slab_rows : (shift_by + 3) * slab_rows]
        slab_sum = slab_sum + passed_along(outgoing, "tile", shift_by)
    blend_total = lax.psum(slab_sum, "mp")
    blended = blend_total / cover_count
    cotangent = ((reward_grad - curvature * blended) / cover_count * scale_factor).astype(
        jnp.bfloat16
    )
    cot_parts = []
    for shift_by in (2, 1, 0, -1, -2):
        if shift_by == 0:
            cot_parts.append(cotangent)
        else:
            cot_parts.append(passed_along(cotangent, "tile", shift_by))
    cot_source = jnp.concatenate(cot_parts, axis=0)
    cot_patches = crop_tiles(cot_source, corners, row_base, tile_side, channels)
    cot_flat = jnp.transpose(cot_patches, (1, 0, 2)).reshape(token_count * tiles_here, 4 * channels)
    cot_share = take_share(cot_flat)
    d_feat = contract_cols(cot_flat, w_out)
    d_feat_b = d_feat.astype(jnp.bfloat16)
    d_active = contract_cols(d_feat_b, w_down)
    down_term = contract_rows(active, d_feat_b)
    d_value = (d_active * gelu_value(gate_proj)).astype(jnp.bfloat16)
    d_gate = (d_active * value_proj * gelu_slope(gate_proj)).astype(jnp.bfloat16)
    value_term = contract_rows(unit_in, d_value)
    gate_term = contract_rows(unit_in, d_gate)
    d_value_grid = d_value.reshape(token_count, tiles_here, d_value.shape[1])
    d_gate_grid = d_gate.reshape(token_count, tiles_here, d_gate.shape[1])
    value_block = d_value_grid.reshape(
        share_tokens * lax.axis_size("mp") * tiles_here, d_value.shape[1]
    )
    gate_block = d_gate_grid.reshape(
        share_tokens * lax.axis_size("mp") * tiles_here, d_gate.shape[1]
    )
    summed = contract_cols(value_block, w_value) + contract_cols(gate_block, w_gate)
    d_unit_share = (
        lax.psum_scatter(
            summed.reshape(share_tokens * lax.axis_size("mp"), tiles_here, model_width).astype(
                jnp.bfloat16
            ),
            "mp",
            scatter_dimension=0,
            tiled=True,
        )
        .astype(jnp.float32)
        .reshape(share_tokens * tiles_here, model_width)
    )
    d_hidden = (
        take_share(d_feat) + norm_backward(take_share(normed), take_share(inv_scale), d_unit_share)
    ).astype(jnp.bfloat16)
    in_term = contract_rows(take_share(flat_patches), d_hidden)
    out_term = contract_rows(hidden_share, cot_share) + contract_rows_exact(
        ff_share, cot_share.astype(jnp.float32)
    )
    grad_in, grad_out = lax.psum((in_term, out_term), ("tile", "mp"))
    grad_value, grad_gate, grad_down = lax.psum((value_term, gate_term, down_term), "tile")
    return (blended, grad_in, grad_value, grad_gate, grad_down, grad_out)


def solution(mesh):
    return jax.shard_map(
        per_device,
        mesh=mesh,
        in_specs=(
            P("tile", None),
            P("tile", None),
            P("tile", None),
            P("tile", None),
            P("tile", None),
            P(),
            P(None, "mp"),
            P(None, "mp"),
            P("mp", None),
            P(),
        ),
        out_specs=(P("tile", None), P(), P(None, "mp"), P(None, "mp"), P("mp", None), P()),
        check_vma=False,
    )
```

profile of v0, /device:TPU:0, one launch (start us, length us, event | category | flops | bytes accessed | tf_op | source)
XLA Modules:
  0.0 512.2 jit_solution(112543032347929282)
XLA Ops:
  7.2 1.4 collective-permute-start.2
  8.7 5.5 %collective-permute-start.1 = (bf16[12,384]{1,0:T(8,128)(2,1)}, bf16[12,384]{1,0:T(8,128)(2,1)S(1)}, u32[]{:S(2)}, u32[]{:S(2)}) collective-permute-start(bf16[12,384]{1,0:T(8,128)(2,1)} %param.12), channel_id=1, source_target_pairs={{0,4},{4,8},{8,12},{12,16},{16,20},{20,24},{24,28},{1,5},{5,9},{9,... | collective-permute-start | bytes 27656 | tf_op jit(solution)/shard_map/ppermute | solution.py:21
  14.2 4.0 collective-permute-start
  18.2 1.3 collective-permute-start.3
  19.5 21.4 %all-gather = s32[8,2,2]{2,1,0:T(2,128)S(1)} all-gather(s32[1,2,2]{2,1,0:T(2,128)} %bitcast.120), channel_id=1, replica_groups=mesh['tile'=8,'mp'=4] {'tile'}, dimensions={0}, use_global_device_ids=true | all-gather | bytes 144 | tf_op jit(solution)/shard_map/all_gather | solution.py:133
  41.5 1.0 concatenate.10
  42.4 4.0 while.16
  43.1 1.4 bitcast_dynamic-update-slice_fusion.4
  45.0 1.4 bitcast_dynamic-update-slice_fusion.4
  49.1 0.8 fusion.38
  50.2 1.9 multiply_convert_fusion.1
  52.8 1.8 reshape.228
  57.6 33.5 %all-reduce.7.cloned.1.call-done = f32[256,2,640]{2,1,0:T(2,128)} async-done(((f32[256,2,640]{2,1,0:T(2,128)}), f32[256,2,640]{2,1,0:T(2,128)}) %all-reduce.7.cloned.1.call-update) | async-done | bytes 1310736
  91.1 1.0 constant_dynamic-slice_fusion.7
  93.2 5.1 while.15
  98.9 0.8 copy.111
  99.7 0.8 copy.115
  100.7 0.8 copy.113
  101.5 1.3 collective-permute-start.5
  102.8 4.6 collective-permute-start.6
  107.4 3.4 collective-permute-start.7
  110.8 1.3 collective-permute-start.4
  112.4 0.9 copy.117
  113.2 0.9 copy.112
  114.7 4.1 collective-permute-done.4
  118.8 1.0 add_add_fusion
  119.8 12.7 %psum.42 = f32[12,384]{0,1:T(8,128)S(1)} all-reduce(f32[12,384]{0,1:T(8,128)S(1)} %add_add_fusion), channel_id=1, replica_groups=mesh['tile'=8,'mp'=4] {'mp'}, use_global_device_ids=true, to_apply=%region_6.7 | all-reduce | flops 4608 | bytes 36864 | tf_op jit(solution)/shard_map/psum | solution.py:202
  133.3 1.4 collective-permute-start.11
  134.7 1.3 collective-permute-start.10
  136.0 4.8 collective-permute-start.9
  140.8 4.7 collective-permute-start.8
  145.6 1.3 fusion
  146.9 0.8 rsqrt.19
  148.0 4.0 while.17
  148.7 1.4 bitcast_dynamic-update-slice_fusion.5
  150.6 1.4 bitcast_dynamic-update-slice_fusion.5
  152.7 0.8 copy.121
  153.5 1.2 fusion.48
  154.7 2.9 fusion.9
  157.6 0.8 fusion.49
  159.2 1.6 fusion.2
  160.8 2.6 convert_element_type.65
  163.5 2.0 copy.124
  165.6 0.8 constant_dynamic-slice_fusion.4
  166.4 2.9 reshape.237
  169.3 1.7 constant_dynamic-slice_fusion.3
  171.1 1.8 reshape.236
  172.9 1.8 constant_dynamic-slice_fusion.5
  174.7 1.3 convolution_bitcast_fusion.1
  176.0 1.8 fusion.10
  177.8 3.1 fusion.34
  180.9 1.9 fusion.17
  182.8 6.7 %reduce-scatter.2.cloned.1.call-done = bf16[64,2,640]{2,0,1:T(8,128)(2,1)} async-done(((bf16[256,2,640]{2,0,1:T(8,128)(2,1)}), bf16[64,2,640]{2,0,1:T(8,128)(2,1)}) %reduce-scatter.2.cloned.1.call-update) | async-done | bytes 163856 | tf_op jit(solution)/shard_map/reduce_scatter | solution.py:235
  189.5 1.2 convert_reduce_fusion.1
  190.7 2.1 convolution_bitcast_fusion.2
  192.8 2.0 fusion.36
  194.9 0.9 copy-done.13
  196.5 119.4 %all-reduce.9.cloned.1.call-done = (f32[16,640]{1,0:T(8,128)}, f32[640,16]{0,1:T(8,128)}) async-done(((f32[16,640]{1,0:T(8,128)}, f32[640,16]{0,1:T(8,128)}), (f32[16,640]{1,0:T(8,128)}, f32[640,16]{0,1:T(8,128)})) %all-reduce.9.cloned.1.call-update) | async-done | bytes 81936 | tf_op jit(solution)/shard_map/psum | solution.py:253
  315.9 181.8 %all-reduce.11.cloned.1.call-done = (f32[640,640]{1,0:T(8,128)}, f32[640,640]{1,0:T(8,128)}, f32[640,640]{1,0:T(8,128)}) async-done(((f32[640,640]{1,0:T(8,128)}, f32[640,640]{1,0:T(8,128)}, f32[640,640]{1,0:T(8,128)}), (f32[640,640]{1,0:T(8,128)}, f32[640,640]{1,0:T(8,128)}, f32[640,640]{1,0:T(8,128)})) %all-reduce.11.cloned.1.call-update) | async-done | bytes 4915216 | tf_op jit(solution)/shard_map/psum | solution.py:254
  497.7 1.4 copy.170
  499.1 2.8 copy.171
  501.9 1.2 copy.172
  503.1 0.9 copy-done.7
  503.9 1.2 copy.173
  (142 shorter events, 17.9 us)
Async XLA Ops:
  7.2 44.9 %copy-start = (bf16[640,640]{1,0:T(8,128)(2,1)S(1)}, bf16[640,640]{1,0:T(8,128)(2,1)}, u32[]{:S(2)}) copy-start(bf16[640,640]{1,0:T(8,128)(2,1)} %param.20) | copy-start | bytes 2457604
  7.2 41.1 %copy-start.26 = (bf16[16,640]{1,0:T(8,128)(2,1)S(1)}, bf16[16,640]{1,0:T(8,128)(2,1)}, u32[]{:S(2)}) copy-start(bf16[16,640]{1,0:T(8,128)(2,1)} %param.17) | copy-start | bytes 61444
  7.2 83.9 %all-reduce.7.cloned.1.call-start = ((), (), s32[]{:S(2)}) async-start(), calls=%async_computation.2 | async-start | bytes 2621440
  7.2 34.2 %collective-permute-start.2 = (bf16[12,384]{1,0:T(8,128)(2,1)}, bf16[12,384]{1,0:T(8,128)(2,1)S(1)}, u32[]{:S(2)}, u32[]{:S(2)}) collective-permute-start(bf16[12,384]{1,0:T(8,128)(2,1)} %param.12), channel_id=1, source_target_pairs={{4,0},{8,4},{12,8},{16,12},{20,16},{24,20},{28,24},{5,1},{9,5},{13... | collective-permute-start | bytes 27656 | tf_op jit(solution)/shard_map/ppermute | solution.py:21
  8.7 32.8 %collective-permute-start.1 = (bf16[12,384]{1,0:T(8,128)(2,1)}, bf16[12,384]{1,0:T(8,128)(2,1)S(1)}, u32[]{:S(2)}, u32[]{:S(2)}) collective-permute-start(bf16[12,384]{1,0:T(8,128)(2,1)} %param.12), channel_id=1, source_target_pairs={{0,4},{4,8},{8,12},{12,16},{16,20},{20,24},{24,28},{1,5},{5,9},{9,... | collective-permute-start | bytes 27656 | tf_op jit(solution)/shard_map/ppermute | solution.py:21
  14.2 27.3 %collective-permute-start = (bf16[12,384]{1,0:T(8,128)(2,1)}, bf16[12,384]{1,0:T(8,128)(2,1)S(1)}, u32[]{:S(2)}, u32[]{:S(2)}) collective-permute-start(bf16[12,384]{1,0:T(8,128)(2,1)} %param.12), channel_id=1, source_target_pairs={{0,8},{4,12},{8,16},{12,20},{16,24},{20,28},{1,9},{5,13},{9,17},{1... | collective-permute-start | bytes 27656 | tf_op jit(solution)/shard_map/ppermute | solution.py:21
  18.2 23.3 %collective-permute-start.3 = (bf16[12,384]{1,0:T(8,128)(2,1)}, bf16[12,384]{1,0:T(8,128)(2,1)S(1)}, u32[]{:S(2)}, u32[]{:S(2)}) collective-permute-start(bf16[12,384]{1,0:T(8,128)(2,1)} %param.12), channel_id=1, source_target_pairs={{8,0},{12,4},{16,8},{20,12},{24,16},{28,20},{9,1},{13,5},{17,9},{2... | collective-permute-start | bytes 27656 | tf_op jit(solution)/shard_map/ppermute | solution.py:21
  42.4 6.6 %copy-start.11 = (bf16[640,640]{1,0:T(8,128)(2,1)S(1)}, bf16[640,640]{1,0:T(8,128)(2,1)}, u32[]{:S(2)}) copy-start(bf16[640,640]{1,0:T(8,128)(2,1)} %param.19) | copy-start | bytes 2457604
  46.4 0.6 copy-start.28
  47.7 0.6 copy-start.16
  48.7 1.2 copy-start.18
  49.0 0.9 copy-start.21
  49.0 1.1 copy-start.1
  50.2 1.9 copy-start.10
  54.7 0.7 copy-start.30
  54.7 2.3 copy-start.14
  54.7 134.7 %reduce-scatter.2.cloned.1.call-start = ((), (), s32[]{:S(2)}) async-start(), calls=%async_computation.1 | async-start | bytes 819200 | tf_op jit(solution)/shard_map/reduce_scatter | solution.py:235
  57.0 0.7 copy-start.9
  92.1 8.4 %copy-start.3 = (f32[64,2,640]{2,1,0:T(2,128)}, f32[64,2,640]{2,1,0:T(2,128)S(1)}, u32[]{:S(2)}) copy-start(f32[64,2,640]{2,1,0:T(2,128)S(1)} %constant_dynamic-slice_fusion.7) | copy-start | bytes 983044
  92.4 19.7 %copy-start.27 = (s32[12,96]{1,0:T(8,128)S(1)}, s32[12,96]{1,0:T(8,128)}, u32[]{:S(2)}) copy-start(s32[12,96]{1,0:T(8,128)} %param.16) | copy-start | bytes 13828
  92.4 19.8 %copy-start.25 = (f32[12,384]{1,0:T(8,128)S(1)}, f32[12,384]{1,0:T(8,128)}, u32[]{:S(2)}) copy-start(f32[12,384]{1,0:T(8,128)} %param.13) | copy-start | bytes 55300
  101.5 12.6 %collective-permute-start.5 = (f32[12,384]{0,1:T(8,128)}, f32[12,384]{0,1:T(8,128)S(1)}, u32[]{:S(2)}, u32[]{:S(2)}) collective-permute-start(f32[12,384]{0,1:T(8,128)} %copy.113), channel_id=1, source_target_pairs={{4,0},{8,4},{12,8},{16,12},{20,16},{24,20},{28,24},{5,1},{9,5},{13... | collective-permute-start | bytes 55304 | tf_op jit(solution)/shard_map/ppermute | solution.py:21
  102.8 11.5 %collective-permute-start.6 = (f32[12,384]{0,1:T(8,128)S(1)}, f32[12,384]{0,1:T(8,128)S(1)}, u32[]{:S(2)}, u32[]{:S(2)}) collective-permute-start(f32[12,384]{0,1:T(8,128)S(1)} %copy.114), channel_id=1, source_target_pairs={{0,4},{4,8},{8,12},{12,16},{16,20},{20,24},{24,28},{1,5},{5,9},{9,... | collective-permute-start | bytes 55304 | tf_op jit(solution)/shard_map/ppermute | solution.py:21
  107.4 7.3 %collective-permute-start.7 = (f32[12,384]{0,1:T(8,128)}, f32[12,384]{0,1:T(8,128)S(1)}, u32[]{:S(2)}, u32[]{:S(2)}) collective-permute-start(f32[12,384]{0,1:T(8,128)} %copy.115), channel_id=1, source_target_pairs={{0,8},{4,12},{8,16},{12,20},{16,24},{20,28},{1,9},{5,13},{9,17},{1... | collective-permute-start | bytes 55304 | tf_op jit(solution)/shard_map/ppermute | solution.py:21
  110.8 8.0 %collective-permute-start.4 = (f32[12,384]{0,1:T(8,128)}, f32[12,384]{0,1:T(8,128)}, u32[]{:S(2)}, u32[]{:S(2)}) collective-permute-start(f32[12,384]{0,1:T(8,128)} %copy.111), channel_id=1, source_target_pairs={{8,0},{12,4},{16,8},{20,12},{24,16},{28,20},{9,1},{13,5},{17,9},{2... | collective-permute-start | bytes 55304 | tf_op jit(solution)/shard_map/ppermute | solution.py:21
  119.8 25.8 %copy-start.19 = (f32[512]{0:T(512)S(1)}, f32[512]{0:T(512)}, u32[]{:S(2)}) copy-start(f32[512]{0:T(512)} %copy-done.18) | copy-start | bytes 6148
  119.8 25.8 %copy-start.22 = (f32[512]{0:T(512)S(1)}, f32[512]{0:T(512)}, u32[]{:S(2)}) copy-start(f32[512]{0:T(512)} %copy-done.21) | copy-start | bytes 6148
  133.3 14.8 %copy-start.29 = (s32[2,2]{1,0:T(2,128)S(1)}, s32[2,2]{1,0:T(2,128)}, u32[]{:S(2)}) copy-start(s32[2,2]{1,0:T(2,128)} %copy-done.28) | copy-start | bytes 52
  133.3 14.4 %collective-permute-start.11 = (bf16[12,384]{0,1:T(8,128)(2,1)S(1)}, bf16[12,384]{0,1:T(8,128)(2,1)S(1)}, u32[]{:S(2)}, u32[]{:S(2)}) collective-permute-start(bf16[12,384]{0,1:T(8,128)(2,1)S(1)} %get-tuple-element.190), channel_id=1, source_target_pairs={{8,0},{12,4},{16,8},{20,12},{24,16},{28,20},{9,1},{13,5},{17,9},{2... | collective-permute-start | bytes 27656 | tf_op jit(solution)/shard_map/ppermute | solution.py:21
  134.7 13.0 %collective-permute-start.10 = (bf16[12,384]{0,1:T(8,128)(2,1)S(1)}, bf16[12,384]{0,1:T(8,128)(2,1)S(1)}, u32[]{:S(2)}, u32[]{:S(2)}) collective-permute-start(bf16[12,384]{0,1:T(8,128)(2,1)S(1)} %get-tuple-element.190), channel_id=1, source_target_pairs={{4,0},{8,4},{12,8},{16,12},{20,16},{24,20},{28,24},{5,1},{9,5},{13... | collective-permute-start | bytes 27656 | tf_op jit(solution)/shard_map/ppermute | solution.py:21
  136.0 11.7 %collective-permute-start.9 = (bf16[12,384]{0,1:T(8,128)(2,1)S(1)}, bf16[12,384]{0,1:T(8,128)(2,1)S(1)}, u32[]{:S(2)}, u32[]{:S(2)}) collective-permute-start(bf16[12,384]{0,1:T(8,128)(2,1)S(1)} %get-tuple-element.190), channel_id=1, source_target_pairs={{0,4},{4,8},{8,12},{12,16},{16,20},{20,24},{24,28},{1,5},{5,9},{9,... | collective-permute-start | bytes 27656 | tf_op jit(solution)/shard_map/ppermute | solution.py:21
  140.8 6.8 %collective-permute-start.8 = (bf16[12,384]{0,1:T(8,128)(2,1)S(1)}, bf16[12,384]{0,1:T(8,128)(2,1)S(1)}, u32[]{:S(2)}, u32[]{:S(2)}) collective-permute-start(bf16[12,384]{0,1:T(8,128)(2,1)S(1)} %get-tuple-element.190), channel_id=1, source_target_pairs={{0,8},{4,12},{8,16},{12,20},{16,24},{20,28},{1,9},{5,13},{9,17},{1... | collective-permute-start | bytes 27656 | tf_op jit(solution)/shard_map/ppermute | solution.py:21
  146.9 6.6 %copy-start.15 = (bf16[640,16]{0,1:T(8,128)(2,1)S(1)}, bf16[640,16]{0,1:T(8,128)(2,1)}, u32[]{:S(2)}) copy-start(bf16[640,16]{0,1:T(8,128)(2,1)} %param.21) | copy-start | bytes 61444
  154.7 2.9 copy-start.2
  157.6 0.8 copy-start.4
  157.6 1.1 copy-start.6
  157.6 1.6 copy-start.12
  165.5 150.4 %all-reduce.9.cloned.1.call-start = ((), (), s32[]{:S(2)}) async-start(), calls=%async_computation.3 | async-start | bytes 163840 | tf_op jit(solution)/shard_map/psum | solution.py:253
  171.1 6.7 %copy-start.20 = (f32[512]{0:T(512)S(1)}, f32[512]{0:T(512)}, u32[]{:S(2)}) copy-start(f32[512]{0:T(512)} %copy-done.18) | copy-start | bytes 6148
  171.1 6.7 %copy-start.23 = (f32[512]{0:T(512)S(1)}, f32[512]{0:T(512)}, u32[]{:S(2)}) copy-start(f32[512]{0:T(512)} %copy-done.21) | copy-start | bytes 6148
  180.9 9.7 %copy-start.17 = (bf16[2,256,16]{1,2,0:T(8,128)(2,1)S(1)}, bf16[2,256,16]{1,2,0:T(8,128)(2,1)}, u32[]{:S(2)}) copy-start(bf16[2,256,16]{1,2,0:T(8,128)(2,1)} %copy-done.16) | copy-start | bytes 49156
  182.8 10.0 %copy-start.5 = (bf16[512,640]{1,0:T(8,128)(2,1)S(1)}, bf16[512,640]{1,0:T(8,128)(2,1)}, u32[]{:S(2)}) copy-start(bf16[512,640]{1,0:T(8,128)(2,1)} %copy-done.4) | copy-start | bytes 1966084
  192.7 304.9 %all-reduce.11.cloned.1.call-start = ((), (), s32[]{:S(2)}) async-start(), calls=%async_computation.4 | async-start | bytes 9830400 | tf_op jit(solution)/shard_map/psum | solution.py:254
  194.8 0.9 copy-start.13
  499.1 2.8 copy-start.8
  501.9 2.0 copy-start.7
  503.9 1.2 copy-start.24
Sparse Core Ops, SparseCore 0:
  54.8 36.2 all-reduce.6
  165.6 23.7 reduce-scatter.1
  195.7 120.1 all-reduce.8
  320.3 177.3 all-reduce.10
where the time goes:
time: 514 us; the launch traced here: 512 us
  waiting for transfers between devices  346 us (67%)
  local copies, waits for them, and re-layouts  51.1 us (10%)
  starting transfers between devices  35.1 us (7%)
  blocking collectives  34.1 us (7%)
  matrix products  22.9 us (4%)
  between operations  15.1 us (3%)
    psum x1, waiting for transfers between devices, per_device(): lax.psum((value_term, gate_term, down_term), 'tile')  182 us
    psum x1, waiting for transfers between devices, per_device(): grad_in, grad_out = lax.psum((in_term, out_term), ('tile', 'mp'))  119 us
    ppermute x12, starting transfers between devices, passed_along(): return lax.ppermute(shard, axis, pairs)  35 us
    unnamed x5, waiting for transfers between devices  33.6 us
    all_gather x1, blocking collectives, per_device(): every_corner = lax.all_gather(offsets, 'tile', axis=0, tiled=True)  21.4 us
    unnamed x76, local copies, waits for them, and re-layouts  15.7 us
    psum x1, blocking collectives, per_device(): blend_total = lax.psum(slab_sum, 'mp')  12.7 us
    dot_general x5, matrix products, contract_rows(): lax.dot_general(left, right, (((0,), (0,)), ((), ())), preferred_element_...  10.9 us
  transfers between devices with their start and end apart: 16, of which 7 were waited for; matrix products, arithmetic and copies ran while one was open for 5% of the time, Pallas kernels for 0%

commit v1 on v0

--- a/solution.py
+++ b/solution.py
@@ -1,8 +1,11 @@
+import functools
 import math
 
 import jax
 import jax.numpy as jnp
 from jax import lax
+from jax.experimental import pallas as pl
+from jax.experimental.pallas import tpu as pltpu
 from jax.sharding import PartitionSpec as P
 
 S = 32
@@ -109,7 +112,7 @@
     return lax.fori_loop(0, pieces.shape[0], add_tile, canvas)
 
 
-def per_device(
+def per_device_sharded(
     latent, reward_grad, curvature, offsets, counts, w_in, w_value, w_gate, w_down, w_out
 ):
     channels = w_in.shape[0] // 4
@@ -255,6 +258,477 @@
     return (blended, grad_in, grad_value, grad_gate, grad_down, grad_out)
 
 
+def dot_lanes(left, right):
+    return lax.dot_general(
+        left, right, (((1,), (1,)), ((), ())), preferred_element_type=jnp.float32
+    )
+
+
+def dot_plain(left, right):
+    return lax.dot_general(
+        left, right, (((1,), (0,)), ((), ())), preferred_element_type=jnp.float32
+    )
+
+
+def split_two(values):
+    high = values.astype(jnp.bfloat16)
+    low = (values - high.astype(jnp.float32)).astype(jnp.bfloat16)
+    return high, low
+
+
+def split_three(values):
+    high = values.astype(jnp.bfloat16)
+    rest = values - high.astype(jnp.float32)
+    middle = rest.astype(jnp.bfloat16)
+    low = (rest - middle.astype(jnp.float32)).astype(jnp.bfloat16)
+    return high, middle, low
+
+
+def fold_matrix(features, half_side):
+    run = features // 2
+    wide = 2 * half_side * run
+    feature = lax.broadcasted_iota(jnp.int32, (features, wide), 0)
+    place = lax.broadcasted_iota(jnp.int32, (features, wide), 1)
+    own = place // (half_side * run) * run + place % run
+    return jnp.where(feature == own, 1.0, 0.0).astype(jnp.bfloat16)
+
+
+def column_mask(features, half_side):
+    run = features // 2
+    wide = 2 * half_side * run
+    token = lax.broadcasted_iota(jnp.int32, (half_side * half_side, wide), 0)
+    place = lax.broadcasted_iota(jnp.int32, (half_side * half_side, wide), 1)
+    return token % half_side == place // run % half_side
+
+
+def spread_tile(canvas_ref, row, col, half_side, features):
+    run = features // 2
+    width = half_side * run
+    panels = canvas_ref.shape[0]
+    cols = panels * width
+    lanes = col * run // 2
+    halves = []
+    for parity in range(2):
+        at = pl.ds(row + parity, half_side, stride=2)
+        rows = jnp.concatenate([canvas_ref[panel, at, :] for panel in range(panels)], axis=1)
+        rolled = pltpu.roll(rows, lax.rem(cols - lanes, cols), 1)
+        halves.append(rolled[:, :width])
+    pair = jnp.concatenate(halves, axis=1).astype(jnp.bfloat16)
+    token = lax.broadcasted_iota(jnp.int32, (half_side * half_side, half_side), 0)
+    patch_row = lax.broadcasted_iota(jnp.int32, (half_side * half_side, half_side), 1)
+    repeat = jnp.where(token // half_side == patch_row, 1.0, 0.0).astype(jnp.bfloat16)
+    repeated = dot_plain(repeat, pair)
+    return jnp.where(column_mask(features, half_side), repeated, 0.0).astype(jnp.bfloat16)
+
+
+def forward_kernel(
+    half_side,
+    corner_ref,
+    latent_ref,
+    w_in_ref,
+    w_value_ref,
+    w_gate_ref,
+    w_down_ref,
+    w_out_ref,
+    canvas_ref,
+    cover_ref,
+    value_ref,
+    gate_ref,
+    normal_ref,
+    unit_ref,
+    active_ref,
+    hidden_ref,
+    patch_ref,
+    scale_ref,
+    latent_wide,
+    w_in_spread,
+    w_both,
+    w_noise,
+):
+    tile = pl.program_id(0)
+    features, model_width = w_in_ref.shape
+    units = w_value_ref.shape[1]
+    slabs, slab_rows, cols = latent_ref.shape
+    panels, rows, width = canvas_ref.shape
+    own_rows = rows // slabs
+
+    @pl.when(tile == 0)
+    def _prepare():
+        for slab in range(slabs):
+            own = latent_ref[slab].astype(jnp.float32)[:own_rows]
+            for panel in range(panels):
+                latent_wide[panel, slab * own_rows : (slab + 1) * own_rows, :] = own[
+                    :, panel * width : (panel + 1) * width
+                ]
+        fold = fold_matrix(features, half_side)
+        w_in_spread[...] = lax.dot_general(
+            w_in_ref[...], fold, (((0,), (0,)), ((), ())), preferred_element_type=jnp.float32
+        ).astype(jnp.bfloat16)
+        w_both[:units, :] = w_value_ref[...].T
+        w_both[units:, :] = w_gate_ref[...].T
+        both = lax.dot_general(
+            w_out_ref[...],
+            w_down_ref[...],
+            (((0,), (1,)), ((), ())),
+            preferred_element_type=jnp.float32,
+        )
+        high, low = split_two(both)
+        w_noise[:features, :] = high
+        w_noise[features:, :] = low
+        canvas_ref[...] = jnp.zeros_like(canvas_ref)
+        cover_ref[...] = jnp.zeros_like(cover_ref)
+
+    row = corner_ref[tile, 0]
+    col = corner_ref[tile, 1]
+    spread = spread_tile(latent_wide, row, col, half_side, features)
+    fold = fold_matrix(features, half_side)
+    patch_ref[0] = dot_lanes(fold, spread).astype(jnp.bfloat16)
+    hidden_b = dot_lanes(w_in_spread[...], spread).astype(jnp.bfloat16)
+    hidden_ref[0] = hidden_b
+    hidden = hidden_b.astype(jnp.float32)
+    center = hidden - jnp.mean(hidden, axis=0, keepdims=True)
+    variance = jnp.mean(center * center, axis=0, keepdims=True)
+    inv_scale = lax.rsqrt(variance + layer_eps)
+    scale_ref[0] = inv_scale
+    unit = (center * inv_scale).astype(jnp.bfloat16)
+    unit_ref[0] = unit
+    both = dot_plain(w_both[...], unit)
+    value = both[:units]
+    gate = both[units:]
+    value_ref[0] = value
+    gate_ref[0] = gate
+    normal = 0.5 * (1.0 + lax.erf(gate * root_half))
+    normal_ref[0] = normal
+    active = (value * (gate * normal)).astype(jnp.bfloat16)
+    active_ref[0] = active
+    parts = dot_plain(w_noise[...], active)
+    noise = parts[:features] + parts[features:]
+    add_noise(canvas_ref, noise, row, col, half_side, features)
+
+    @pl.when(lax.rem(tile, lax.axis_size("mp")) == lax.axis_index("mp"))
+    def _direct():
+        direct = lax.dot_general(
+            w_out_ref[...], hidden_b, (((0,), (0,)), ((), ())), preferred_element_type=jnp.float32
+        )
+        add_noise(canvas_ref, direct, row, col, half_side, features)
+
+    shape = cover_ref.shape
+    row_at = lax.broadcasted_iota(jnp.int32, shape, 1) - row
+    col_at = (
+        lax.broadcasted_iota(jnp.int32, shape, 0) * width
+        + lax.broadcasted_iota(jnp.int32, shape, 2)
+        - col * (features // 4)
+    )
+    inside = (
+        (row_at >= 0)
+        & (row_at < 2 * half_side)
+        & (col_at >= 0)
+        & (col_at < half_side * features // 2)
+    )
+    cover_ref[...] += jnp.where(inside, 1.0, 0.0)
+
+
+def add_noise(canvas_ref, noise, row, col, half_side, features):
+    run = features // 2
+    width = half_side * run
+    panels = canvas_ref.shape[0]
+    fold = fold_matrix(features, half_side)
+    tall = lax.dot_general(
+        jnp.concatenate(split_three(noise), axis=0),
+        jnp.concatenate([fold, fold, fold], axis=0),
+        (((0,), (0,)), ((), ())),
+        preferred_element_type=jnp.float32,
+    )
+    kept = jnp.where(column_mask(features, half_side), tall, 0.0)
+    pair = jnp.sum(kept.reshape(half_side, half_side, 2 * width), axis=1)
+    blank = jnp.zeros((half_side, (panels - 1) * width), jnp.float32)
+    for parity in range(2):
+        placed = jnp.concatenate([pair[:, parity * width : (parity + 1) * width], blank], axis=1)
+        placed = pltpu.roll(placed, col * run // 2, 1)
+        at = pl.ds(row + parity, half_side, stride=2)
+        for panel in range(panels):
+            own = placed[:, panel * width : (panel + 1) * width]
+            canvas_ref[panel, at, :] = canvas_ref[panel, at, :] + own
+
+
+def backward_kernel(
+    half_side,
+    scale_factor,
+    corner_ref,
+    sum_ref,
+    other_ref,
+    reward_ref,
+    cover_ref,
+    w_value_ref,
+    w_gate_ref,
+    w_down_ref,
+    w_out_ref,
+    value_ref,
+    gate_ref,
+    normal_ref,
+    unit_ref,
+    active_ref,
+    hidden_ref,
+    patch_ref,
+    scale_ref,
+    blended_ref,
+    grad_value_ref,
+    grad_gate_ref,
+    grad_down_ref,
+    small_ref,
+    cot_wide,
+    w_out_spread,
+    scaled_sum,
+    mean_sum,
+    active_sum,
+    hidden_sum,
+    patch_sum,
+):
+    tile = pl.program_id(0)
+    model_width, features = w_out_ref.shape
+    units = w_down_ref.shape[0]
+    slabs, two_slabs, cols = reward_ref.shape
+    slab_rows = two_slabs // 2
+    panels, rows, width = sum_ref.shape
+
+    @pl.when(tile == 0)
+    def _prepare():
+        for panel in range(panels):
+            lanes = slice(panel * width, (panel + 1) * width)
+            cover = cover_ref[panel]
+            blended = (sum_ref[panel] + other_ref[panel]) / cover
+            blended_ref[:, lanes] = blended
+            reward = jnp.concatenate(
+                [reward_ref[slab, :slab_rows, lanes] for slab in range(slabs)], axis=0
+            )
+            curvature = jnp.concatenate(
+                [reward_ref[slab, slab_rows:, lanes] for slab in range(slabs)], axis=0
+            )
+            cot_wide[panel] = (
+                ((reward - curvature * blended) / cover * scale_factor)
+                .astype(jnp.bfloat16)
+                .astype(jnp.float32)
+            )
+        w_out_spread[...] = dot_plain(w_out_ref[...], fold_matrix(features, half_side)).astype(
+            jnp.bfloat16
+        )
+        for ref in (
+            grad_value_ref,
+            grad_gate_ref,
+            scaled_sum,
+            mean_sum,
+            active_sum,
+            hidden_sum,
+            patch_sum,
+        ):
+            ref[...] = jnp.zeros_like(ref)
+
+    spread = spread_tile(cot_wide, corner_ref[tile, 0], corner_ref[tile, 1], half_side, features)
+    cot = dot_lanes(fold_matrix(features, half_side), spread).astype(jnp.bfloat16)
+    d_feat_b = dot_lanes(w_out_spread[...], spread).astype(jnp.bfloat16)
+    d_active = dot_plain(w_down_ref[...], d_feat_b)
+    value = value_ref[0]
+    gate = gate_ref[0]
+    normal = normal_ref[0]
+    unit = unit_ref[0]
+    slope = normal + gate * jnp.exp(-0.5 * gate * gate) * inv_root_two_pi
+    d_value = (d_active * (gate * normal)).astype(jnp.bfloat16)
+    d_gate = (d_active * value * slope).astype(jnp.bfloat16)
+    along = jnp.sum(
+        d_value.astype(jnp.float32) * value + d_gate.astype(jnp.float32) * gate,
+        axis=0,
+        keepdims=True,
+    ) * (1.0 / model_width)
+    scaled = patch_ref[0].astype(jnp.float32) * scale_ref[0]
+    left = jnp.concatenate([unit, *split_two(scaled)], axis=0)
+    grads = dot_lanes(left, jnp.concatenate([d_value, d_gate], axis=0))
+    grad_value_ref[...] += grads[:model_width, :units]
+    grad_gate_ref[...] += grads[:model_width, units:]
+    scaled_sum[...] += grads[model_width:]
+    mean_sum[...] += dot_lanes(jnp.concatenate(split_two(scaled * along), axis=0), unit)
+    active_sum[...] += dot_lanes(cot, active_ref[0])
+
+    @pl.when(lax.rem(tile, lax.axis_size("mp")) == lax.axis_index("mp"))
+    def _direct():
+        hidden_sum[...] += dot_lanes(cot, hidden_ref[0])
+        patch_sum[...] += dot_lanes(patch_ref[0], cot)
+
+    @pl.when(tile == pl.num_programs(0) - 1)
+    def _finish():
+        active_two = jnp.concatenate(split_two(active_sum[...]), axis=0)
+        w_out_two = jnp.concatenate([w_out_ref[...], w_out_ref[...]], axis=1)
+        grad_down_ref[...] = lax.dot_general(
+            active_two, w_out_two, (((0,), (1,)), ((), ())), preferred_element_type=jnp.float32
+        )
+        through = dot_plain(active_two, w_down_ref[...])
+        small_ref[features:] = hidden_sum[...] + through[:features] + through[features:]
+        scaled_both = scaled_sum[:features] + scaled_sum[features:]
+        scaled_two = jnp.concatenate(split_two(scaled_both), axis=0)
+        moved = dot_lanes(scaled_two[:, :units], w_value_ref[...]) + dot_lanes(
+            scaled_two[:, units:], w_gate_ref[...]
+        )
+        moved = moved[:features] + moved[features:]
+        patch_two = jnp.concatenate(split_two(patch_sum[...]), axis=0)
+        direct = dot_lanes(patch_two, w_out_ref[...])
+        small_ref[:features] = (
+            direct[:features]
+            + direct[features:]
+            + moved
+            - jnp.mean(moved, axis=1, keepdims=True)
+            - mean_sum[:features]
+            - mean_sum[features:]
+        )
+
+
+def whole(shape):
+    return pl.BlockSpec(shape, lambda *_: (0,) * len(shape))
+
+
+def one_tile(shape):
+    return pl.BlockSpec((1,) + shape, lambda tile, *_: (tile,) + (0,) * len(shape))
+
+
+def over_mp(values):
+    peers = lax.axis_size("mp")
+    by = 1
+    total = values
+    other = None
+    while by < peers:
+        if other is not None:
+            total = total + other
+        other = lax.ppermute(total, "mp", [(i, i ^ by) for i in range(peers)])
+        by *= 2
+    return total, other
+
+
+def per_device_replicated(
+    latent, reward_grad, curvature, offsets, counts, w_in, w_value, w_gate, w_down, w_out
+):
+    features, model_width = w_in.shape
+    units = w_value.shape[1]
+    half_side = S // 2
+    token_count = half_side * half_side
+    slab_rows, cols = latent.shape
+    tiles_here = offsets.shape[0]
+    slabs = lax.axis_size("tile")
+    tiles = tiles_here * slabs
+    rows = slab_rows * slabs
+    digits = jnp.stack([offsets // 256, offsets % 256]).reshape(1, -1).astype(latent.dtype)
+    digit_row = jnp.pad(digits, ((0, 0), (0, cols - digits.shape[1])))
+    spare = -(slab_rows + 1) % 16
+    packed = jnp.pad(jnp.concatenate([latent, digit_row], axis=0), ((0, spare), (0, 0)))
+
+    def to_all(values):
+        return lax.all_to_all(
+            jnp.broadcast_to(values[None], (slabs,) + values.shape), "tile", 0, 0
+        )
+
+    latents = to_all(packed)
+    rewards = to_all(jnp.concatenate([reward_grad, curvature], axis=0))
+    digits = latents[:, slab_rows, : 4 * tiles_here].astype(jnp.int32)
+    digits = digits.reshape(slabs, 2, tiles_here, 2)
+    corners = (digits[:, 0] * 256 + digits[:, 1]).reshape(tiles, 2)
+
+    wide = 2 * half_side * features // 2
+    f32 = jnp.float32
+    b16 = jnp.bfloat16
+
+    def saved(kind, height):
+        return jax.ShapeDtypeStruct((tiles, height, token_count), kind)
+
+    kept = [
+        saved(f32, units),
+        saved(f32, units),
+        saved(f32, units),
+        saved(b16, model_width),
+        saved(b16, units),
+        saved(b16, model_width),
+        saved(b16, features),
+        saved(f32, 1),
+    ]
+    width = half_side * features // 2
+    panels = cols // width
+    canvas = jax.ShapeDtypeStruct((panels, rows, width), f32)
+    params = pltpu.CompilerParams(
+        dimension_semantics=("arbitrary",), vmem_limit_bytes=52 * 2**20
+    )
+    weights = [w_in, w_value, w_gate, w_down, w_out]
+    sums, cover, *stored = pl.pallas_call(
+        functools.partial(forward_kernel, half_side),
+        out_shape=[canvas, canvas, *kept],
+        grid_spec=pltpu.PrefetchScalarGridSpec(
+            num_scalar_prefetch=1,
+            grid=(tiles,),
+            in_specs=[whole(latents.shape)] + [whole(w.shape) for w in weights],
+            out_specs=[whole(canvas.shape)] * 2 + [one_tile(k.shape[1:]) for k in kept],
+            scratch_shapes=[
+                pltpu.VMEM(canvas.shape, f32),
+                pltpu.VMEM((model_width, wide), b16),
+                pltpu.VMEM((2 * units, model_width), b16),
+                pltpu.VMEM((2 * features, units), b16),
+            ],
+        ),
+        compiler_params=params,
+        name="forward",
+    )(corners, latents, *weights)
+    total, other = over_mp(sums)
+    scale_factor = 16.0 / math.sqrt(tiles * token_count)
+    weights = [w_value, w_gate, w_down, w_out]
+    blended, grad_value, grad_gate, grad_down, small = pl.pallas_call(
+        functools.partial(backward_kernel, half_side, scale_factor),
+        out_shape=[
+            jax.ShapeDtypeStruct((rows, cols), f32),
+            jax.ShapeDtypeStruct((model_width, units), f32),
+            jax.ShapeDtypeStruct((model_width, units), f32),
+            jax.ShapeDtypeStruct((units, model_width), f32),
+            jax.ShapeDtypeStruct((2 * features, model_width), f32),
+        ],
+        grid_spec=pltpu.PrefetchScalarGridSpec(
+            num_scalar_prefetch=1,
+            grid=(tiles,),
+            in_specs=[whole(canvas.shape)] * 2
+            + [whole(rewards.shape), whole(canvas.shape)]
+            + [whole(w.shape) for w in weights]
+            + [one_tile(k.shape[1:]) for k in kept],
+            out_specs=[
+                whole((rows, cols)),
+                whole((model_width, units)),
+                whole((model_width, units)),
+                whole((units, model_width)),
+                whole((2 * features, model_width)),
+            ],
+            scratch_shapes=[
+                pltpu.VMEM(canvas.shape, f32),
+                pltpu.VMEM((model_width, wide), b16),
+                pltpu.VMEM((2 * features, 2 * units), f32),
+                pltpu.VMEM((2 * features, model_width), f32),
+                pltpu.VMEM((features, units), f32),
+                pltpu.VMEM((features, model_width), f32),
+                pltpu.VMEM((features, features), f32),
+            ],
+        ),
+        compiler_params=params,
+        name="backward",
+    )(corners, total, other, rewards, cover, *weights, *stored)
+    own = lax.dynamic_slice_in_dim(blended, lax.axis_index("tile") * slab_rows, slab_rows, 0)
+    mine, theirs = over_mp(small)
+    small = mine + theirs
+    return (own, small[:features], grad_value, grad_gate, grad_down, small[features:].T)
+
+
+def per_device(
+    latent, reward_grad, curvature, offsets, counts, w_in, w_value, w_gate, w_down, w_out
+):
+    tiles = offsets.shape[0] * lax.axis_size("tile")
+    stored_bytes = tiles * (S // 2) ** 2 * (14 * w_value.shape[1] + 4 * w_in.shape[1])
+    peers = lax.axis_size("mp")
+    replicate = stored_bytes <= 48 * 2**20 and peers > 1 and peers & (peers - 1) == 0
+    plan = per_device_replicated if replicate else per_device_sharded
+    return plan(
+        latent, reward_grad, curvature, offsets, counts, w_in, w_value, w_gate, w_down, w_out
+    )
+
+
 def solution(mesh):
     return jax.shard_map(
         per_device,

time: 514 us -> 117 us (0.23)
  waiting for transfers between devices: 346 us -> 14.9 us
  Pallas kernels: 0 us -> 78.8 us
  local copies, waits for them, and re-layouts: 51.1 us -> 5.66 us
  blocking collectives: 34.1 us -> 0 us
  matrix products: 22.9 us -> 0 us
  starting transfers between devices: 35.1 us -> 13.8 us
  between operations: 15.1 us -> 0.68 us
    psum x2 -> x0, waiting for transfers between devices: 301 us -> none  [the longest x1 182 us: per_device(): lax.psum((value_term, gate_term, down_term), 'tile')]
    pallas_call x0 -> x2, Pallas kernels: none -> 78.8 us  [the longest x1 39.5 us: per_device_replicated(): pl.pallas_call(functools.partial(backward_kernel, half_side, scale_factor...]
    unnamed x5 -> x0, waiting for transfers between devices: 33.6 us -> none
    ppermute x12 -> x4, starting transfers between devices: 35 us -> 3.17 us  [over_mp(): other = lax.ppermute(total, 'mp', [(i, i ^ by) for i in range(peers)])]
    dot_general x16 -> x0, matrix products: 22.9 us -> none  [the longest x5 10.9 us: contract_rows(): lax.dot_general(left, right, (((0,), (0,)), ((), ())), preferred_element_...]
    all_gather x1 -> x0, blocking collectives: 21.4 us -> none  [per_device(): every_corner = lax.all_gather(offsets, 'tile', axis=0, tiled=True)]
    unnamed x76 -> x5, local copies, waits for them, and re-layouts: 15.7 us -> 2.76 us
    psum x1 -> x0, blocking collectives: 12.7 us -> none  [per_device(): blend_total = lax.psum(slab_sum, 'mp')]
  transfers between devices with their start and end apart: 16 -> 6, of which waited for: 7 -> 5; matrix products, arithmetic and copies ran while one was open for 5% -> 2% of each run, Pallas kernels for 0% -> 34%
where the time goes in v1:
time: 117 us; the launch traced here: 116 us
  Pallas kernels  78.8 us (67%)
  waiting for transfers between devices  14.9 us (13%)
  starting transfers between devices  13.8 us (12%)
  local copies, waits for them, and re-layouts  5.66 us (5%)
  other arithmetic  2.26 us (2%)
    pallas_call x1, Pallas kernels, per_device_replicated(): pl.pallas_call(functools.partial(backward_kernel, half_side, scale_factor...  39.5 us
    pallas_call x1, Pallas kernels, per_device_replicated(): pl.pallas_call(functools.partial(forward_kernel, half_side), out_shape=[c...  39.3 us
    all_to_all x2, starting transfers between devices, to_all(): lax.all_to_all(jnp.broadcast_to(values[None], (slabs,) + values.shape), '...  10.7 us
    ppermute x4, waiting for transfers between devices, over_mp(): other = lax.ppermute(total, 'mp', [(i, i ^ by) for i in range(peers)])  9.38 us
    all_to_all x2, waiting for transfers between devices, to_all(): lax.all_to_all(jnp.broadcast_to(values[None], (slabs,) + values.shape), '...  5.47 us
    ppermute x4, starting transfers between devices, over_mp(): other = lax.ppermute(total, 'mp', [(i, i ^ by) for i in range(peers)])  3.17 us
    unnamed x5, local copies, waits for them, and re-layouts  2.76 us
  transfers between devices with their start and end apart: 6, of which 5 were waited for; matrix products, arithmetic and copies ran while one was open for 2% of the time, Pallas kernels for 34%

profile of v1, /device:TPU:0, one launch (start us, length us, event | category | flops | bytes accessed | tf_op | source)
XLA Modules:
  0.0 116.1 jit_solution(3815756722259509150)
XLA Ops:
  0.6 0.7 fusion.5
  1.3 0.1 convert_element_type.23
  1.4 0.7 fusion.1
  2.1 0.7 broadcast_in_dim.4
  2.8 7.3 %all-to-all-start = ((bf16[8,16,384]{2,1,0:T(8,128)(2,1)}), bf16[8,16,384]{2,1,0:T(8,128)(2,1)S(1)}, u32[]{:S(2)}, u32[]{:S(2)}) async-start(bf16[8,16,384]{2,1,0:T(8,128)(2,1)} %broadcast_in_dim.4), calls=%async_computation | async-start | bytes 196608 | tf_op jit(solution)/shard_map/all_to_all | solution.py:622
  10.1 0.9 copy.30.w_out_ref
  10.9 0.8 pad_maximum_fusion
  11.7 5.5 %all-to-all-done.latent_ref = bf16[8,16,384]{2,1,0:T(8,128)(2,1)S(1)} async-done(((bf16[8,16,384]{2,1,0:T(8,128)(2,1)}), bf16[8,16,384]{2,1,0:T(8,128)(2,1)S(1)}, u32[]{:S(2)}, u32[]{:S(2)}) %all-to-all-start) | async-done | bytes 98336 | tf_op jit(solution)/shard_map/all_to_all | solution.py:622
  17.2 0.7 broadcast_in_dim.5
  17.9 3.4 %all-to-all-start.1 = ((f32[8,24,384]{2,1,0:T(8,128)}), f32[8,24,384]{2,1,0:T(8,128)S(1)}, u32[]{:S(2)}, u32[]{:S(2)}) async-start(f32[8,24,384]{2,1,0:T(8,128)} %broadcast_in_dim.5), calls=%async_computation.1 | async-start | bytes 589824 | tf_op jit(solution)/shard_map/all_to_all | solution.py:622
  21.4 0.1 copy.27
  21.4 0.1 copy.33
  21.5 0.0 copy-start
  21.5 1.1 copy-done
  22.7 0.0 copy-start.1
  22.7 0.7 copy-done.1
  23.4 39.3 %forward.1 = (f32[3,96,128]{2,1,0:T(8,128)S(1)}, f32[3,96,128]{2,1,0:T(8,128)S(1)}, f32[16,640,256]{2,1,0:T(8,128)}, f32[16,640,256]{2,1,0:T(8,128)}, f32[16,640...) custom-call(s32[16,2]{1,0:T(8,128)S(1)} %bitcast.8, ...), custom_call_target="tpu_custom_call" | custom-call | tf_op jit(solution)/shard_map/forward/pallas_call | solution.py:656
  62.7 0.0 collective-permute-start
  62.7 1.4 %collective-permute-done = f32[3,96,128]{2,1,0:T(8,128)S(1)} collective-permute-done((f32[3,96,128]{2,1,0:T(8,128)S(1)}, f32[3,96,128]{2,1,0:T(8,128)S(1)}, u32[]{:S(2)}, u32[]{:S(2)}) %collective-permute-start) | collective-permute-done | bytes 147488 | tf_op jit(solution)/shard_map/ppermute | solution.py:599
  64.1 1.6 %collective-permute-start.1 = (f32[3,96,128]{2,1,0:T(8,128)S(1)}, f32[3,96,128]{2,1,0:T(8,128)S(1)}, u32[]{:S(2)}, u32[]{:S(2)}) collective-permute-start(f32[3,96,128]{2,1,0:T(8,128)S(1)} %add.33.sum_ref), channel_id=1, source_target_pairs={{0,2},{1,3},{2,0},{3,1},{4,6},{5,7},{6,4},{7,5},{8,10},{9,11},{10,... | collective-permute-start | bytes 442376 | tf_op jit(solution)/shard_map/ppermute | solution.py:599
  65.7 4.4 %collective-permute-done.1.other_ref = f32[3,96,128]{2,1,0:T(8,128)S(1)} collective-permute-done((f32[3,96,128]{2,1,0:T(8,128)S(1)}, f32[3,96,128]{2,1,0:T(8,128)S(1)}, u32[]{:S(2)}, u32[]{:S(2)}) %collective-permute-start.1) | collective-permute-done | bytes 147488 | tf_op jit(solution)/shard_map/ppermute | solution.py:599
  70.1 0.0 all-to-all-done.1.reward_ref
  70.1 39.5 %backward.1 = (f32[96,384]{1,0:T(8,128)S(1)}, f32[640,640]{1,0:T(8,128)}, f32[640,640]{1,0:T(8,128)}, f32[640,640]{1,0:T(8,128)}, f32[32,640]{1,0:T(8,128)S(1)}) custom-call(s32[16,2]{1,0:T(8,128)S(1)} %bitcast.9, f32[3,96,128]{2,1,0:T(8,128)S(1)} %add.33.sum_ref, f32[3,96,128]{2,1,0:T(8,128)S(1)} %collective-permute-done.1.other_ref, ...), custom_call_target="tpu_custom_call" | custom-call | tf_op jit(solution)/shard_map/backward/pallas_call | solution.py:677
  109.6 0.0 collective-permute-start.2
  109.6 1.3 %collective-permute-done.2 = f32[32,640]{1,0:T(8,128)S(1)} collective-permute-done((f32[32,640]{1,0:T(8,128)S(1)}, f32[32,640]{1,0:T(8,128)S(1)}, u32[]{:S(2)}, u32[]{:S(2)}) %collective-permute-start.2) | collective-permute-done | bytes 81952 | tf_op jit(solution)/shard_map/ppermute | solution.py:599
  110.9 1.6 %collective-permute-start.3 = (f32[32,640]{1,0:T(8,128)S(1)}, f32[32,640]{1,0:T(8,128)S(1)}, u32[]{:S(2)}, u32[]{:S(2)}) collective-permute-start(f32[32,640]{1,0:T(8,128)S(1)} %add.35), channel_id=1, source_target_pairs={{0,2},{1,3},{2,0},{3,1},{4,6},{5,7},{6,4},{7,5},{8,10},{9,11},{10,... | collective-permute-start | bytes 245768 | tf_op jit(solution)/shard_map/ppermute | solution.py:599
  112.5 0.6 constant_dynamic-slice_fusion
  113.1 2.4 %collective-permute-done.3 = f32[32,640]{1,0:T(8,128)S(1)} collective-permute-done((f32[32,640]{1,0:T(8,128)S(1)}, f32[32,640]{1,0:T(8,128)S(1)}, u32[]{:S(2)}, u32[]{:S(2)}) %collective-permute-start.3) | collective-permute-done | bytes 81952 | tf_op jit(solution)/shard_map/ppermute | solution.py:599
  115.5 0.6 slice_bitcast_fusion
  (7 shorter events, 0.1 us)
Async XLA Ops:
  2.8 14.4 %all-to-all-start = ((bf16[8,16,384]{2,1,0:T(8,128)(2,1)}), bf16[8,16,384]{2,1,0:T(8,128)(2,1)S(1)}, u32[]{:S(2)}, u32[]{:S(2)}) async-start(bf16[8,16,384]{2,1,0:T(8,128)(2,1)} %broadcast_in_dim.4), calls=%async_computation | async-start | bytes 196608 | tf_op jit(solution)/shard_map/all_to_all | solution.py:622
  17.9 52.2 %all-to-all-start.1 = ((f32[8,24,384]{2,1,0:T(8,128)}), f32[8,24,384]{2,1,0:T(8,128)S(1)}, u32[]{:S(2)}, u32[]{:S(2)}) async-start(f32[8,24,384]{2,1,0:T(8,128)} %broadcast_in_dim.5), calls=%async_computation.1 | async-start | bytes 589824 | tf_op jit(solution)/shard_map/all_to_all | solution.py:622
  21.5 1.1 copy-start
  22.7 0.7 copy-start.1
  62.7 1.4 %collective-permute-start = (f32[3,96,128]{2,1,0:T(8,128)S(1)}, f32[3,96,128]{2,1,0:T(8,128)S(1)}, u32[]{:S(2)}, u32[]{:S(2)}) collective-permute-start(f32[3,96,128]{2,1,0:T(8,128)S(1)} %get-tuple-element.21), channel_id=1, source_target_pairs={{0,1},{1,0},{2,3},{3,2},{4,5},{5,4},{6,7},{7,6},{8,9},{9,8},{10,11... | collective-permute-start | bytes 442376 | tf_op jit(solution)/shard_map/ppermute | solution.py:599
  64.1 6.0 %collective-permute-start.1 = (f32[3,96,128]{2,1,0:T(8,128)S(1)}, f32[3,96,128]{2,1,0:T(8,128)S(1)}, u32[]{:S(2)}, u32[]{:S(2)}) collective-permute-start(f32[3,96,128]{2,1,0:T(8,128)S(1)} %add.33.sum_ref), channel_id=1, source_target_pairs={{0,2},{1,3},{2,0},{3,1},{4,6},{5,7},{6,4},{7,5},{8,10},{9,11},{10,... | collective-permute-start | bytes 442376 | tf_op jit(solution)/shard_map/ppermute | solution.py:599
  109.6 1.3 %collective-permute-start.2 = (f32[32,640]{1,0:T(8,128)S(1)}, f32[32,640]{1,0:T(8,128)S(1)}, u32[]{:S(2)}, u32[]{:S(2)}) collective-permute-start(f32[32,640]{1,0:T(8,128)S(1)} %get-tuple-element.32), channel_id=1, source_target_pairs={{0,1},{1,0},{2,3},{3,2},{4,5},{5,4},{6,7},{7,6},{8,9},{9,8},{10,11... | collective-permute-start | bytes 245768 | tf_op jit(solution)/shard_map/ppermute | solution.py:599
  110.9 4.6 %collective-permute-start.3 = (f32[32,640]{1,0:T(8,128)S(1)}, f32[32,640]{1,0:T(8,128)S(1)}, u32[]{:S(2)}, u32[]{:S(2)}) collective-permute-start(f32[32,640]{1,0:T(8,128)S(1)} %add.35), channel_id=1, source_target_pairs={{0,2},{1,3},{2,0},{3,1},{4,6},{5,7},{6,4},{7,5},{8,10},{9,11},{10,... | collective-permute-start | bytes 245768 | tf_op jit(solution)/shard_map/ppermute | solution.py:599

commit v2 on v1

--- a/solution.py
+++ b/solution.py
@@ -321,6 +321,10 @@
     return jnp.where(column_mask(features, half_side), repeated, 0.0).astype(jnp.bfloat16)
 
 
+def token_at(tile, tokens):
+    return pl.ds(pl.multiple_of(tile * tokens, tokens), tokens)
+
+
 def forward_kernel(
     half_side,
     corner_ref,
@@ -334,25 +338,27 @@
     cover_ref,
     value_ref,
     gate_ref,
-    normal_ref,
-    unit_ref,
-    active_ref,
+    left_ref,
+    patch_ref,
     hidden_ref,
-    patch_ref,
-    scale_ref,
     latent_wide,
     w_in_spread,
     w_both,
     w_noise,
+    hidden_all,
+    active,
+    noise,
 ):
-    tile = pl.program_id(0)
+    step = pl.program_id(0)
     features, model_width = w_in_ref.shape
     units = w_value_ref.shape[1]
     slabs, slab_rows, cols = latent_ref.shape
     panels, rows, width = canvas_ref.shape
     own_rows = rows // slabs
-
-    @pl.when(tile == 0)
+    tokens = half_side * half_side
+    tiles_here = active.shape[1] // tokens
+
+    @pl.when(step == 0)
     def _prepare():
         for slab in range(slabs):
             own = latent_ref[slab].astype(jnp.float32)[:own_rows]
@@ -377,58 +383,83 @@
         w_noise[features:, :] = low
         canvas_ref[...] = jnp.zeros_like(canvas_ref)
         cover_ref[...] = jnp.zeros_like(cover_ref)
-
-    row = corner_ref[tile, 0]
-    col = corner_ref[tile, 1]
-    spread = spread_tile(latent_wide, row, col, half_side, features)
+        noise[...] = jnp.zeros_like(noise)
+
+    def corners_of(group):
+        return [
+            (corner_ref[group * tiles_here + tile, 0], corner_ref[group * tiles_here + tile, 1])
+            for tile in range(tiles_here)
+        ]
+
+    corners = corners_of(step)
+    add_noise(canvas_ref, noise[...], corners_of(jnp.maximum(step - 1, 0)), half_side, features)
     fold = fold_matrix(features, half_side)
-    patch_ref[0] = dot_lanes(fold, spread).astype(jnp.bfloat16)
-    hidden_b = dot_lanes(w_in_spread[...], spread).astype(jnp.bfloat16)
-    hidden_ref[0] = hidden_b
-    hidden = hidden_b.astype(jnp.float32)
-    center = hidden - jnp.mean(hidden, axis=0, keepdims=True)
-    variance = jnp.mean(center * center, axis=0, keepdims=True)
-    inv_scale = lax.rsqrt(variance + layer_eps)
-    scale_ref[0] = inv_scale
-    unit = (center * inv_scale).astype(jnp.bfloat16)
-    unit_ref[0] = unit
-    both = dot_plain(w_both[...], unit)
-    value = both[:units]
-    gate = both[units:]
-    value_ref[0] = value
-    gate_ref[0] = gate
-    normal = 0.5 * (1.0 + lax.erf(gate * root_half))
-    normal_ref[0] = normal
-    active = (value * (gate * normal)).astype(jnp.bfloat16)
-    active_ref[0] = active
-    parts = dot_plain(w_noise[...], active)
-    noise = parts[:features] + parts[features:]
-    add_noise(canvas_ref, noise, row, col, half_side, features)
-
-    @pl.when(lax.rem(tile, lax.axis_size("mp")) == lax.axis_index("mp"))
-    def _direct():
-        direct = lax.dot_general(
-            w_out_ref[...], hidden_b, (((0,), (0,)), ((), ())), preferred_element_type=jnp.float32
-        )
-        add_noise(canvas_ref, direct, row, col, half_side, features)
+    for tile, (row, col) in enumerate(corners):
+        here = slice(tile * tokens, (tile + 1) * tokens)
+        spread = spread_tile(latent_wide, row, col, half_side, features)
+        patch = dot_lanes(fold, spread)
+        patch_ref[:, here] = patch.astype(jnp.bfloat16)
+        hidden_all[:, here] = dot_lanes(w_in_spread[...], spread).astype(jnp.bfloat16)
+        total = jnp.zeros((chunk_rows, tokens), jnp.float32)
+        for at in range(0, model_width, chunk_rows):
+            total = total + hidden_all[at : at + chunk_rows, here].astype(jnp.float32)
+        mean = jnp.sum(total, axis=0, keepdims=True) * (1.0 / model_width)
+        total = jnp.zeros((chunk_rows, tokens), jnp.float32)
+        for at in range(0, model_width, chunk_rows):
+            center = hidden_all[at : at + chunk_rows, here].astype(jnp.float32) - mean
+            total = total + center * center
+        variance = jnp.sum(total, axis=0, keepdims=True) * (1.0 / model_width)
+        inv_scale = lax.rsqrt(variance + layer_eps)
+        for at in range(0, model_width, chunk_rows):
+            center = hidden_all[at : at + chunk_rows, here].astype(jnp.float32) - mean
+            left_ref[at : at + chunk_rows, here] = (center * inv_scale).astype(jnp.bfloat16)
+        high, low = split_two(patch * inv_scale)
+        left_ref[model_width : model_width + features, here] = high
+        left_ref[model_width + features :, here] = low
+    for tile in range(tiles_here):
+        here = slice(tile * tokens, (tile + 1) * tokens)
+        unit = left_ref[:model_width, here]
+        value_ref[:, here] = dot_plain(w_both[:units, :], unit)
+        gate_ref[:, here] = dot_plain(w_both[units:, :], unit)
+        for at in range(0, units, chunk_rows):
+            value = value_ref[at : at + chunk_rows, here]
+            gate = gate_ref[at : at + chunk_rows, here]
+            normal = 0.5 * (1.0 + lax.erf(gate * root_half))
+            active[at : at + chunk_rows, here] = (value * (gate * normal)).astype(jnp.bfloat16)
+    parts = dot_plain(w_noise[...], active[...])
+    noise[...] = parts[:features] + parts[features:]
+    peers = lax.axis_size("mp")
+    for group in range(tiles_here // peers):
+        own = token_at(group * peers + lax.axis_index("mp"), tokens)
+        hidden = hidden_all[:, own]
+        hidden_ref[:, group * tokens : (group + 1) * tokens] = hidden
+        noise[:, own] = noise[:, own] + lax.dot_general(
+            w_out_ref[...], hidden, (((0,), (0,)), ((), ())), preferred_element_type=jnp.float32
+        )
+
+    @pl.when(step == pl.num_programs(0) - 1)
+    def _last():
+        add_noise(canvas_ref, noise[...], corners, half_side, features)
 
     shape = cover_ref.shape
-    row_at = lax.broadcasted_iota(jnp.int32, shape, 1) - row
-    col_at = (
-        lax.broadcasted_iota(jnp.int32, shape, 0) * width
-        + lax.broadcasted_iota(jnp.int32, shape, 2)
-        - col * (features // 4)
-    )
-    inside = (
-        (row_at >= 0)
-        & (row_at < 2 * half_side)
-        & (col_at >= 0)
-        & (col_at < half_side * features // 2)
-    )
-    cover_ref[...] += jnp.where(inside, 1.0, 0.0)
-
-
-def add_noise(canvas_ref, noise, row, col, half_side, features):
+    row_at = lax.broadcasted_iota(jnp.int32, shape, 1)
+    col_at = lax.broadcasted_iota(jnp.int32, shape, 0) * width + lax.broadcasted_iota(
+        jnp.int32, shape, 2
+    )
+    cover = cover_ref[...]
+    for row, col in corners:
+        left = col * (features // 4)
+        inside = (
+            (row_at >= row)
+            & (row_at < row + 2 * half_side)
+            & (col_at >= left)
+            & (col_at < left + half_side * features // 2)
+        )
+        cover = cover + jnp.where(inside, 1.0, 0.0)
+    cover_ref[...] = cover
+
+
+def add_noise(canvas_ref, noise, corners, half_side, features):
     run = features // 2
     width = half_side * run
     panels = canvas_ref.shape[0]
@@ -439,16 +470,18 @@
         (((0,), (0,)), ((), ())),
         preferred_element_type=jnp.float32,
     )
-    kept = jnp.where(column_mask(features, half_side), tall, 0.0)
-    pair = jnp.sum(kept.reshape(half_side, half_side, 2 * width), axis=1)
+    tall = tall.reshape(len(corners), half_side * half_side, 2 * width)
+    kept = jnp.where(column_mask(features, half_side)[None], tall, 0.0)
+    pairs = jnp.sum(kept.reshape(len(corners), half_side, half_side, 2 * width), axis=2)
     blank = jnp.zeros((half_side, (panels - 1) * width), jnp.float32)
-    for parity in range(2):
-        placed = jnp.concatenate([pair[:, parity * width : (parity + 1) * width], blank], axis=1)
-        placed = pltpu.roll(placed, col * run // 2, 1)
-        at = pl.ds(row + parity, half_side, stride=2)
-        for panel in range(panels):
-            own = placed[:, panel * width : (panel + 1) * width]
-            canvas_ref[panel, at, :] = canvas_ref[panel, at, :] + own
+    for tile, (row, col) in enumerate(corners):
+        for parity in range(2):
+            own = pairs[tile, :, parity * width : (parity + 1) * width]
+            placed = pltpu.roll(jnp.concatenate([own, blank], axis=1), col * run // 2, 1)
+            at = pl.ds(row + parity, half_side, stride=2)
+            for panel in range(panels):
+                here = placed[:, panel * width : (panel + 1) * width]
+                canvas_ref[panel, at, :] = canvas_ref[panel, at, :] + here
 
 
 def backward_kernel(
@@ -465,33 +498,37 @@
     w_out_ref,
     value_ref,
     gate_ref,
-    normal_ref,
-    unit_ref,
-    active_ref,
+    left_ref,
+    patch_ref,
     hidden_ref,
-    patch_ref,
-    scale_ref,
     blended_ref,
     grad_value_ref,
     grad_gate_ref,
     grad_down_ref,
     small_ref,
     cot_wide,
-    w_out_spread,
+    w_through,
     scaled_sum,
     mean_sum,
     active_sum,
     hidden_sum,
     patch_sum,
+    cot,
+    d_active,
+    d_both,
+    active,
+    along_scaled,
 ):
-    tile = pl.program_id(0)
+    step = pl.program_id(0)
     model_width, features = w_out_ref.shape
     units = w_down_ref.shape[0]
     slabs, two_slabs, cols = reward_ref.shape
     slab_rows = two_slabs // 2
     panels, rows, width = sum_ref.shape
-
-    @pl.when(tile == 0)
+    tokens = half_side * half_side
+    tiles_here = active.shape[1] // tokens
+
+    @pl.when(step == 0)
     def _prepare():
         for panel in range(panels):
             lanes = slice(panel * width, (panel + 1) * width)
@@ -509,8 +546,8 @@
                 .astype(jnp.bfloat16)
                 .astype(jnp.float32)
             )
-        w_out_spread[...] = dot_plain(w_out_ref[...], fold_matrix(features, half_side)).astype(
-            jnp.bfloat16
+        w_through[...] = jnp.concatenate(
+            split_two(dot_plain(w_down_ref[...], w_out_ref[...])), axis=1
         )
         for ref in (
             grad_value_ref,
@@ -523,39 +560,59 @@
         ):
             ref[...] = jnp.zeros_like(ref)
 
-    spread = spread_tile(cot_wide, corner_ref[tile, 0], corner_ref[tile, 1], half_side, features)
-    cot = dot_lanes(fold_matrix(features, half_side), spread).astype(jnp.bfloat16)
-    d_feat_b = dot_lanes(w_out_spread[...], spread).astype(jnp.bfloat16)
-    d_active = dot_plain(w_down_ref[...], d_feat_b)
-    value = value_ref[0]
-    gate = gate_ref[0]
-    normal = normal_ref[0]
-    unit = unit_ref[0]
-    slope = normal + gate * jnp.exp(-0.5 * gate * gate) * inv_root_two_pi
-    d_value = (d_active * (gate * normal)).astype(jnp.bfloat16)
-    d_gate = (d_active * value * slope).astype(jnp.bfloat16)
-    along = jnp.sum(
-        d_value.astype(jnp.float32) * value + d_gate.astype(jnp.float32) * gate,
-        axis=0,
-        keepdims=True,
-    ) * (1.0 / model_width)
-    scaled = patch_ref[0].astype(jnp.float32) * scale_ref[0]
-    left = jnp.concatenate([unit, *split_two(scaled)], axis=0)
-    grads = dot_lanes(left, jnp.concatenate([d_value, d_gate], axis=0))
+    for tile in range(tiles_here):
+        here = slice(tile * tokens, (tile + 1) * tokens)
+        spread = spread_tile(
+            cot_wide,
+            corner_ref[step * tiles_here + tile, 0],
+            corner_ref[step * tiles_here + tile, 1],
+            half_side,
+            features,
+        )
+        cots = dot_lanes(fold_matrix(features, half_side), spread).astype(jnp.bfloat16)
+        cot[:, here] = cots
+        d_active[:, here] = dot_plain(w_through[...], jnp.concatenate([cots, cots], axis=0))
+    for tile in range(tiles_here):
+        here = slice(tile * tokens, (tile + 1) * tokens)
+        total = jnp.zeros((chunk_rows, tokens), jnp.float32)
+        for at in range(0, units, chunk_rows):
+            chunk = slice(at, at + chunk_rows)
+            value = value_ref[chunk, here]
+            gate = gate_ref[chunk, here]
+            passed = d_active[chunk, here]
+            normal = 0.5 * (1.0 + lax.erf(gate * root_half))
+            slope = normal + gate * jnp.exp(-0.5 * gate * gate) * inv_root_two_pi
+            active[chunk, here] = (value * (gate * normal)).astype(jnp.bfloat16)
+            d_value = (passed * (gate * normal)).astype(jnp.bfloat16)
+            d_gate = (passed * value * slope).astype(jnp.bfloat16)
+            d_both[chunk, here] = d_value
+            d_both[units + at : units + at + chunk_rows, here] = d_gate
+            total = total + d_value.astype(jnp.float32) * value
+            total = total + d_gate.astype(jnp.float32) * gate
+        along = jnp.sum(total, axis=0, keepdims=True) * (1.0 / model_width)
+        scaled = left_ref[model_width:, here].astype(jnp.float32)
+        high, low = split_two((scaled[:features] + scaled[features:]) * along)
+        along_scaled[:features, here] = high
+        along_scaled[features:, here] = low
+    grads = dot_lanes(left_ref[...], d_both[...])
     grad_value_ref[...] += grads[:model_width, :units]
     grad_gate_ref[...] += grads[:model_width, units:]
     scaled_sum[...] += grads[model_width:]
-    mean_sum[...] += dot_lanes(jnp.concatenate(split_two(scaled * along), axis=0), unit)
-    active_sum[...] += dot_lanes(cot, active_ref[0])
-
-    @pl.when(lax.rem(tile, lax.axis_size("mp")) == lax.axis_index("mp"))
-    def _direct():
-        hidden_sum[...] += dot_lanes(cot, hidden_ref[0])
-        patch_sum[...] += dot_lanes(patch_ref[0], cot)
-
-    @pl.when(tile == pl.num_programs(0) - 1)
+    mean_sum[...] += dot_lanes(left_ref[:model_width, :], along_scaled[...])
+    active_sum[...] += dot_lanes(active[...], cot[...])
+    peers = lax.axis_size("mp")
+    for group in range(tiles_here // peers):
+        own = token_at(group * peers + lax.axis_index("mp"), tokens)
+        own_cot = cot[:, own]
+        hidden_sum[...] += dot_lanes(
+            own_cot, hidden_ref[:, group * tokens : (group + 1) * tokens]
+        )
+        patch_sum[...] += dot_lanes(patch_ref[:, own], own_cot)
+
+    @pl.when(step == pl.num_programs(0) - 1)
     def _finish():
-        active_two = jnp.concatenate(split_two(active_sum[...]), axis=0)
+        active_two = jnp.concatenate(split_two(active_sum[...].T), axis=0)
+        mean_both = mean_sum[...].T
         w_out_two = jnp.concatenate([w_out_ref[...], w_out_ref[...]], axis=1)
         grad_down_ref[...] = lax.dot_general(
             active_two, w_out_two, (((0,), (1,)), ((), ())), preferred_element_type=jnp.float32
@@ -575,17 +632,13 @@
             + direct[features:]
             + moved
             - jnp.mean(moved, axis=1, keepdims=True)
-            - mean_sum[:features]
-            - mean_sum[features:]
+            - mean_both[:features]
+            - mean_both[features:]
         )
 
 
 def whole(shape):
     return pl.BlockSpec(shape, lambda *_: (0,) * len(shape))
-
-
-def one_tile(shape):
-    return pl.BlockSpec((1,) + shape, lambda tile, *_: (tile,) + (0,) * len(shape))
 
 
 def over_mp(values):
@@ -599,6 +652,123 @@
         other = lax.ppermute(total, "mp", [(i, i ^ by) for i in range(peers)])
         by *= 2
     return total, other
+
+
+chunk_rows = 32
+
+
+def some_tokens(height, tokens):
+    return pl.BlockSpec((height, tokens), lambda step, *_: (0, step))
+
+
+def step_tiles(tiles):
+    peers = lax.axis_size("mp")
+    return max(peers * count for count in (1,) if tiles % (peers * count) == 0)
+
+
+def saved_arrays(tiles, token_count, features, model_width, units):
+    every = tiles * token_count
+    shapes = [
+        ((units, every), jnp.float32),
+        ((units, every), jnp.float32),
+        ((model_width + 2 * features, every), jnp.bfloat16),
+        ((features, every), jnp.bfloat16),
+        ((model_width, every // lax.axis_size("mp")), jnp.bfloat16),
+    ]
+    return [jax.ShapeDtypeStruct(shape, kind) for shape, kind in shapes]
+
+
+kernel_params = pltpu.CompilerParams(
+    dimension_semantics=("arbitrary",), vmem_limit_bytes=52 * 2**20
+)
+
+
+def run_forward(corners, latents, weights, half_side, rows):
+    features, model_width = weights[0].shape
+    units = weights[1].shape[1]
+    tiles = corners.shape[0]
+    cols = latents.shape[2]
+    steps = tiles // step_tiles(tiles)
+    tokens = step_tiles(tiles) * half_side * half_side
+    width = half_side * features // 2
+    f32 = jnp.float32
+    b16 = jnp.bfloat16
+    canvas = jax.ShapeDtypeStruct((cols // width, rows, width), f32)
+    kept = saved_arrays(tiles, half_side * half_side, features, model_width, units)
+    return pl.pallas_call(
+        functools.partial(forward_kernel, half_side),
+        out_shape=[canvas, canvas, *kept],
+        grid_spec=pltpu.PrefetchScalarGridSpec(
+            num_scalar_prefetch=1,
+            grid=(steps,),
+            in_specs=[whole(latents.shape)] + [whole(w.shape) for w in weights],
+            out_specs=[whole(canvas.shape)] * 2 + [some_tokens(k.shape[0], k.shape[1] // steps) for k in kept],
+            scratch_shapes=[
+                pltpu.VMEM(canvas.shape, f32),
+                pltpu.VMEM((model_width, 2 * width), b16),
+                pltpu.VMEM((2 * units, model_width), b16),
+                pltpu.VMEM((2 * features, units), b16),
+                pltpu.VMEM((model_width, tokens), b16),
+                pltpu.VMEM((units, tokens), b16),
+                pltpu.VMEM((features, tokens), f32),
+            ],
+        ),
+        compiler_params=kernel_params,
+        name="forward",
+    )(corners, latents, *weights)
+
+
+def run_backward(corners, total, other, rewards, cover, weights, stored, half_side):
+    features, model_width = weights[0].shape
+    units = weights[1].shape[1]
+    tiles = corners.shape[0]
+    token_count = half_side * half_side
+    steps = tiles // step_tiles(tiles)
+    tokens = step_tiles(tiles) * token_count
+    panels, rows, width = total.shape
+    f32 = jnp.float32
+    scale_factor = 16.0 / math.sqrt(tiles * token_count)
+    return pl.pallas_call(
+        functools.partial(backward_kernel, half_side, scale_factor),
+        out_shape=[
+            jax.ShapeDtypeStruct((rows, panels * width), f32),
+            jax.ShapeDtypeStruct((model_width, units), f32),
+            jax.ShapeDtypeStruct((model_width, units), f32),
+            jax.ShapeDtypeStruct((units, model_width), f32),
+            jax.ShapeDtypeStruct((2 * features, model_width), f32),
+        ],
+        grid_spec=pltpu.PrefetchScalarGridSpec(
+            num_scalar_prefetch=1,
+            grid=(steps,),
+            in_specs=[whole(total.shape)] * 2
+            + [whole(rewards.shape), whole(cover.shape)]
+            + [whole(w.shape) for w in weights[1:]]
+            + [some_tokens(k.shape[0], k.shape[1] // steps) for k in stored],
+            out_specs=[
+                whole((rows, panels * width)),
+                whole((model_width, units)),
+                whole((model_width, units)),
+                whole((units, model_width)),
+                whole((2 * features, model_width)),
+            ],
+            scratch_shapes=[
+                pltpu.VMEM(total.shape, f32),
+                pltpu.VMEM((units, 2 * features), jnp.bfloat16),
+                pltpu.VMEM((2 * features, 2 * units), f32),
+                pltpu.VMEM((model_width, 2 * features), f32),
+                pltpu.VMEM((units, features), f32),
+                pltpu.VMEM((features, model_width), f32),
+                pltpu.VMEM((features, features), f32),
+                pltpu.VMEM((features, tokens), jnp.bfloat16),
+                pltpu.VMEM((units, tokens), f32),
+                pltpu.VMEM((2 * units, tokens), jnp.bfloat16),
+                pltpu.VMEM((units, tokens), jnp.bfloat16),
+                pltpu.VMEM((2 * features, tokens), jnp.bfloat16),
+            ],
+        ),
+        compiler_params=kernel_params,
+        name="backward",
+    )(corners, total, other, rewards, cover, *weights[1:], *stored)
 
 
 def per_device_replicated(
@@ -629,87 +799,12 @@
     digits = digits.reshape(slabs, 2, tiles_here, 2)
     corners = (digits[:, 0] * 256 + digits[:, 1]).reshape(tiles, 2)
 
-    wide = 2 * half_side * features // 2
-    f32 = jnp.float32
-    b16 = jnp.bfloat16
-
-    def saved(kind, height):
-        return jax.ShapeDtypeStruct((tiles, height, token_count), kind)
-
-    kept = [
-        saved(f32, units),
-        saved(f32, units),
-        saved(f32, units),
-        saved(b16, model_width),
-        saved(b16, units),
-        saved(b16, model_width),
-        saved(b16, features),
-        saved(f32, 1),
-    ]
-    width = half_side * features // 2
-    panels = cols // width
-    canvas = jax.ShapeDtypeStruct((panels, rows, width), f32)
-    params = pltpu.CompilerParams(
-        dimension_semantics=("arbitrary",), vmem_limit_bytes=52 * 2**20
-    )
-    weights = [w_in, w_value, w_gate, w_down, w_out]
-    sums, cover, *stored = pl.pallas_call(
-        functools.partial(forward_kernel, half_side),
-        out_shape=[canvas, canvas, *kept],
-        grid_spec=pltpu.PrefetchScalarGridSpec(
-            num_scalar_prefetch=1,
-            grid=(tiles,),
-            in_specs=[whole(latents.shape)] + [whole(w.shape) for w in weights],
-            out_specs=[whole(canvas.shape)] * 2 + [one_tile(k.shape[1:]) for k in kept],
-            scratch_shapes=[
-                pltpu.VMEM(canvas.shape, f32),
-                pltpu.VMEM((model_width, wide), b16),
-                pltpu.VMEM((2 * units, model_width), b16),
-                pltpu.VMEM((2 * features, units), b16),
-            ],
-        ),
-        compiler_params=params,
-        name="forward",
-    )(corners, latents, *weights)
+    weights = (w_in, w_value, w_gate, w_down, w_out)
+    sums, cover, *stored = run_forward(corners, latents, weights, half_side, rows)
     total, other = over_mp(sums)
-    scale_factor = 16.0 / math.sqrt(tiles * token_count)
-    weights = [w_value, w_gate, w_down, w_out]
-    blended, grad_value, grad_gate, grad_down, small = pl.pallas_call(
-        functools.partial(backward_kernel, half_side, scale_factor),
-        out_shape=[
-            jax.ShapeDtypeStruct((rows, cols), f32),
-            jax.ShapeDtypeStruct((model_width, units), f32),
-            jax.ShapeDtypeStruct((model_width, units), f32),
-            jax.ShapeDtypeStruct((units, model_width), f32),
-            jax.ShapeDtypeStruct((2 * features, model_width), f32),
-        ],
-        grid_spec=pltpu.PrefetchScalarGridSpec(
-            num_scalar_prefetch=1,
-            grid=(tiles,),
-            in_specs=[whole(canvas.shape)] * 2
-            + [whole(rewards.shape), whole(canvas.shape)]
-            + [whole(w.shape) for w in weights]
-            + [one_tile(k.shape[1:]) for k in kept],
-            out_specs=[
-                whole((rows, cols)),
-                whole((model_width, units)),
-                whole((model_width, units)),
-                whole((units, model_width)),
-                whole((2 * features, model_width)),
-            ],
-            scratch_shapes=[
-                pltpu.VMEM(canvas.shape, f32),
-                pltpu.VMEM((model_width, wide), b16),
-                pltpu.VMEM((2 * features, 2 * units), f32),
-                pltpu.VMEM((2 * features, model_width), f32),
-                pltpu.VMEM((features, units), f32),
-                pltpu.VMEM((features, model_width), f32),
-                pltpu.VMEM((features, features), f32),
-            ],
-        ),
-        compiler_params=params,
-        name="backward",
-    )(corners, total, other, rewards, cover, *weights, *stored)
+    blended, grad_value, grad_gate, grad_down, small = run_backward(
+        corners, total, other, rewards, cover, weights, stored, half_side
+    )
     own = lax.dynamic_slice_in_dim(blended, lax.axis_index("tile") * slab_rows, slab_rows, 0)
     mine, theirs = over_mp(small)
     small = mine + theirs
@@ -720,9 +815,10 @@
     latent, reward_grad, curvature, offsets, counts, w_in, w_value, w_gate, w_down, w_out
 ):
     tiles = offsets.shape[0] * lax.axis_size("tile")
-    stored_bytes = tiles * (S // 2) ** 2 * (14 * w_value.shape[1] + 4 * w_in.shape[1])
+    stored_bytes = tiles * (S // 2) ** 2 * (8 * w_value.shape[1] + 3 * w_in.shape[1])
     peers = lax.axis_size("mp")
-    replicate = stored_bytes <= 48 * 2**20 and peers > 1 and peers & (peers - 1) == 0
+    pairs = peers > 1 and peers & (peers - 1) == 0 and tiles % peers == 0
+    replicate = pairs and stored_bytes <= 40 * 2**20
     plan = per_device_replicated if replicate else per_device_sharded
     return plan(
         latent, reward_grad, curvature, offsets, counts, w_in, w_value, w_gate, w_down, w_out

time: 117 us -> 84.2 us (0.72)
  Pallas kernels: 78.8 us -> 47.5 us
    pallas_call x2, Pallas kernels: 78.8 us -> 47.5 us  [the longest x1 25.2 us: run_backward(): pl.pallas_call(functools.partial(backward_kernel, half_side, scale_factor...]
  transfers between devices with their start and end apart: 6 -> 6, of which waited for: 5 -> 5; matrix products, arithmetic and copies ran while one was open for 2% -> 3% of each run, Pallas kernels for 34% -> 27%
where the time goes in v2:
time: 84.2 us; the launch traced here: 83.7 us
  Pallas kernels  47.5 us (56%)
  waiting for transfers between devices  14.9 us (18%)
  starting transfers between devices  13.8 us (16%)
  local copies, waits for them, and re-layouts  4.52 us (5%)
  other arithmetic  2.33 us (3%)
    pallas_call x1, Pallas kernels, run_backward(): pl.pallas_call(functools.partial(backward_kernel, half_side, scale_factor...  25.2 us
    pallas_call x1, Pallas kernels, run_forward(): pl.pallas_call(functools.partial(forward_kernel, half_side), out_shape=[c...  22.2 us
    all_to_all x2, starting transfers between devices, to_all(): lax.all_to_all(jnp.broadcast_to(values[None], (slabs,) + values.shape), '...  10.7 us
    ppermute x4, waiting for transfers between devices, over_mp(): other = lax.ppermute(total, 'mp', [(i, i ^ by) for i in range(peers)])  9.41 us
    all_to_all x2, waiting for transfers between devices, to_all(): lax.all_to_all(jnp.broadcast_to(values[None], (slabs,) + values.shape), '...  5.47 us
    ppermute x4, starting transfers between devices, over_mp(): other = lax.ppermute(total, 'mp', [(i, i ^ by) for i in range(peers)])  3.16 us
  transfers between devices with their start and end apart: 6, of which 5 were waited for; matrix products, arithmetic and copies ran while one was open for 3% of the time, Pallas kernels for 27%

profile of v2, /device:TPU:0, one launch (start us, length us, event | category | flops | bytes accessed | tf_op | source)
XLA Modules:
  0.0 83.7 jit_solution(17131533976834469588)
XLA Ops:
  0.6 0.0 copy-start
  0.6 0.8 fusion.5
  1.4 0.1 convert_element_type.23
  1.5 0.7 fusion.1
  2.2 0.7 broadcast_in_dim.4
  2.9 7.3 %all-to-all-start = ((bf16[8,16,384]{2,1,0:T(8,128)(2,1)}), bf16[8,16,384]{2,1,0:T(8,128)(2,1)S(1)}, u32[]{:S(2)}, u32[]{:S(2)}) async-start(bf16[8,16,384]{2,1,0:T(8,128)(2,1)} %broadcast_in_dim.4), calls=%async_computation | async-start | bytes 196608 | tf_op jit(solution)/shard_map/all_to_all | solution.py:792
  10.1 0.9 %copy.30.w_out_ref = bf16[640,16]{1,0:T(8,128)(2,1)S(1)} copy(bf16[640,16]{0,1:T(8,128)(2,1)} %param.18) | data formatting | bytes 40960 | tf_op args[9]
  11.0 0.8 pad_maximum_fusion
  11.8 5.5 %all-to-all-done.latent_ref = bf16[8,16,384]{2,1,0:T(8,128)(2,1)S(1)} async-done(((bf16[8,16,384]{2,1,0:T(8,128)(2,1)}), bf16[8,16,384]{2,1,0:T(8,128)(2,1)S(1)}, u32[]{:S(2)}, u32[]{:S(2)}) %all-to-all-start) | async-done | bytes 98336 | tf_op jit(solution)/shard_map/all_to_all | solution.py:792
  17.3 0.7 broadcast_in_dim.5
  18.0 3.4 %all-to-all-start.1 = ((f32[8,24,384]{2,1,0:T(8,128)}), f32[8,24,384]{2,1,0:T(8,128)S(1)}, u32[]{:S(2)}, u32[]{:S(2)}) async-start(f32[8,24,384]{2,1,0:T(8,128)} %broadcast_in_dim.5), calls=%async_computation.1 | async-start | bytes 589824 | tf_op jit(solution)/shard_map/all_to_all | solution.py:792
  21.4 0.1 copy.27
  21.5 0.1 copy.33
  21.6 0.0 copy-done
  21.6 0.0 copy-start.1
  21.6 0.7 copy-done.1
  22.4 22.2 %forward.1 = (f32[3,96,128]{2,1,0:T(8,128)S(1)}, f32[3,96,128]{2,1,0:T(8,128)S(1)}, f32[640,4096]{1,0:T(8,128)}, f32[640,4096]{1,0:T(8,128)}, bf16[672,4096]{1,0...) custom-call(s32[16,2]{1,0:T(8,128)S(1)} %bitcast.8, ...), custom_call_target="tpu_custom_call" | custom-call | tf_op jit(solution)/shard_map/forward/pallas_call | solution.py:698
  44.6 0.0 collective-permute-start
  44.6 1.4 %collective-permute-done = f32[3,96,128]{2,1,0:T(8,128)S(1)} collective-permute-done((f32[3,96,128]{2,1,0:T(8,128)S(1)}, f32[3,96,128]{2,1,0:T(8,128)S(1)}, u32[]{:S(2)}, u32[]{:S(2)}) %collective-permute-start) | collective-permute-done | bytes 147488 | tf_op jit(solution)/shard_map/ppermute | solution.py:652
  46.0 1.6 %collective-permute-start.1 = (f32[3,96,128]{2,1,0:T(8,128)S(1)}, f32[3,96,128]{2,1,0:T(8,128)S(1)}, u32[]{:S(2)}, u32[]{:S(2)}) collective-permute-start(f32[3,96,128]{2,1,0:T(8,128)S(1)} %add.33.sum_ref), channel_id=1, source_target_pairs={{0,2},{1,3},{2,0},{3,1},{4,6},{5,7},{6,4},{7,5},{8,10},{9,11},{10,... | collective-permute-start | bytes 442376 | tf_op jit(solution)/shard_map/ppermute | solution.py:652
  47.6 4.4 %collective-permute-done.1.other_ref = f32[3,96,128]{2,1,0:T(8,128)S(1)} collective-permute-done((f32[3,96,128]{2,1,0:T(8,128)S(1)}, f32[3,96,128]{2,1,0:T(8,128)S(1)}, u32[]{:S(2)}, u32[]{:S(2)}) %collective-permute-start.1) | collective-permute-done | bytes 147488 | tf_op jit(solution)/shard_map/ppermute | solution.py:652
  51.9 0.0 all-to-all-done.1.reward_ref
  51.9 25.2 %backward.1 = (f32[96,384]{1,0:T(8,128)S(1)}, f32[640,640]{1,0:T(8,128)}, f32[640,640]{1,0:T(8,128)}, f32[640,640]{1,0:T(8,128)}, f32[32,640]{1,0:T(8,128)S(1)}) custom-call(s32[16,2]{1,0:T(8,128)S(1)} %bitcast.9, f32[3,96,128]{2,1,0:T(8,128)S(1)} %add.33.sum_ref, f32[3,96,128]{2,1,0:T(8,128)S(1)} %collective-permute-done.1.other_ref, ...), custom_call_target="tpu_custom_call" | custom-call | tf_op jit(solution)/shard_map/backward/pallas_call | solution.py:731
  77.2 0.0 collective-permute-start.2
  77.2 1.3 %collective-permute-done.2 = f32[32,640]{1,0:T(8,128)S(1)} collective-permute-done((f32[32,640]{1,0:T(8,128)S(1)}, f32[32,640]{1,0:T(8,128)S(1)}, u32[]{:S(2)}, u32[]{:S(2)}) %collective-permute-start.2) | collective-permute-done | bytes 81952 | tf_op jit(solution)/shard_map/ppermute | solution.py:652
  78.5 1.6 %collective-permute-start.3 = (f32[32,640]{1,0:T(8,128)S(1)}, f32[32,640]{1,0:T(8,128)S(1)}, u32[]{:S(2)}, u32[]{:S(2)}) collective-permute-start(f32[32,640]{1,0:T(8,128)S(1)} %add.35), channel_id=1, source_target_pairs={{0,2},{1,3},{2,0},{3,1},{4,6},{5,7},{6,4},{7,5},{8,10},{9,11},{10,... | collective-permute-start | bytes 245768 | tf_op jit(solution)/shard_map/ppermute | solution.py:652
  80.0 0.6 constant_dynamic-slice_fusion
  80.7 2.4 %collective-permute-done.3 = f32[32,640]{1,0:T(8,128)S(1)} collective-permute-done((f32[32,640]{1,0:T(8,128)S(1)}, f32[32,640]{1,0:T(8,128)S(1)}, u32[]{:S(2)}, u32[]{:S(2)}) %collective-permute-start.3) | collective-permute-done | bytes 81952 | tf_op jit(solution)/shard_map/ppermute | solution.py:652
  83.1 0.6 slice_bitcast_fusion
  (7 shorter events, 0.1 us)
Async XLA Ops:
  0.6 21.0 %copy-start = (bf16[640,640]{1,0:T(8,128)(2,1)S(1)}, bf16[640,640]{1,0:T(8,128)(2,1)}, u32[]{:S(2)}) copy-start(bf16[640,640]{1,0:T(8,128)(2,1)} %w_value_ref.3) | copy-start | bytes 2457604
  2.9 14.4 %all-to-all-start = ((bf16[8,16,384]{2,1,0:T(8,128)(2,1)}), bf16[8,16,384]{2,1,0:T(8,128)(2,1)S(1)}, u32[]{:S(2)}, u32[]{:S(2)}) async-start(bf16[8,16,384]{2,1,0:T(8,128)(2,1)} %broadcast_in_dim.4), calls=%async_computation | async-start | bytes 196608 | tf_op jit(solution)/shard_map/all_to_all | solution.py:792
  18.0 33.9 %all-to-all-start.1 = ((f32[8,24,384]{2,1,0:T(8,128)}), f32[8,24,384]{2,1,0:T(8,128)S(1)}, u32[]{:S(2)}, u32[]{:S(2)}) async-start(f32[8,24,384]{2,1,0:T(8,128)} %broadcast_in_dim.5), calls=%async_computation.1 | async-start | bytes 589824 | tf_op jit(solution)/shard_map/all_to_all | solution.py:792
  21.6 0.7 copy-start.1
  44.6 1.4 %collective-permute-start = (f32[3,96,128]{2,1,0:T(8,128)S(1)}, f32[3,96,128]{2,1,0:T(8,128)S(1)}, u32[]{:S(2)}, u32[]{:S(2)}) collective-permute-start(f32[3,96,128]{2,1,0:T(8,128)S(1)} %get-tuple-element.18), channel_id=1, source_target_pairs={{0,1},{1,0},{2,3},{3,2},{4,5},{5,4},{6,7},{7,6},{8,9},{9,8},{10,11... | collective-permute-start | bytes 442376 | tf_op jit(solution)/shard_map/ppermute | solution.py:652
  46.0 6.0 %collective-permute-start.1 = (f32[3,96,128]{2,1,0:T(8,128)S(1)}, f32[3,96,128]{2,1,0:T(8,128)S(1)}, u32[]{:S(2)}, u32[]{:S(2)}) collective-permute-start(f32[3,96,128]{2,1,0:T(8,128)S(1)} %add.33.sum_ref), channel_id=1, source_target_pairs={{0,2},{1,3},{2,0},{3,1},{4,6},{5,7},{6,4},{7,5},{8,10},{9,11},{10,... | collective-permute-start | bytes 442376 | tf_op jit(solution)/shard_map/ppermute | solution.py:652
  77.2 1.3 %collective-permute-start.2 = (f32[32,640]{1,0:T(8,128)S(1)}, f32[32,640]{1,0:T(8,128)S(1)}, u32[]{:S(2)}, u32[]{:S(2)}) collective-permute-start(f32[32,640]{1,0:T(8,128)S(1)} %get-tuple-element.26), channel_id=1, source_target_pairs={{0,1},{1,0},{2,3},{3,2},{4,5},{5,4},{6,7},{7,6},{8,9},{9,8},{10,11... | collective-permute-start | bytes 245768 | tf_op jit(solution)/shard_map/ppermute | solution.py:652
  78.5 4.6 %collective-permute-start.3 = (f32[32,640]{1,0:T(8,128)S(1)}, f32[32,640]{1,0:T(8,128)S(1)}, u32[]{:S(2)}, u32[]{:S(2)}) collective-permute-start(f32[32,640]{1,0:T(8,128)S(1)} %add.35), channel_id=1, source_target_pairs={{0,2},{1,3},{2,0},{3,1},{4,6},{5,7},{6,4},{7,5},{8,10},{9,11},{10,... | collective-permute-start | bytes 245768 | tf_op jit(solution)/shard_map/ppermute | solution.py:652

commit v3 on v2

--- a/solution.py
+++ b/solution.py
@@ -325,14 +325,53 @@
     return pl.ds(pl.multiple_of(tile * tokens, tokens), tokens)
 
 
+def weight_kernel(
+    half_side,
+    w_in_ref,
+    w_value_ref,
+    w_gate_ref,
+    w_down_ref,
+    w_out_ref,
+    packed,
+    w_through,
+):
+    features, model_width = w_in_ref.shape
+    units = w_value_ref.shape[1]
+    fold = fold_matrix(features, half_side)
+    packed[...] = jnp.zeros_like(packed)
+    packed[:model_width, model_width:] = lax.dot_general(
+        w_in_ref[...], fold, (((0,), (0,)), ((), ())), preferred_element_type=jnp.float32
+    ).astype(jnp.bfloat16)
+    packed[:units, :model_width] = w_value_ref[...].T
+    packed[units : 2 * units, :model_width] = w_gate_ref[...].T
+    both = dot_plain(w_down_ref[...], w_out_ref[...])
+    w_through[...] = jnp.concatenate(split_two(both), axis=1)
+    packed[2 * units :, :units] = jnp.concatenate(split_two(both.T), axis=0)
+
+
+def run_weights(weights, half_side):
+    features, model_width = weights[0].shape
+    units = weights[1].shape[1]
+    width = half_side * features // 2
+    vmem = pl.BlockSpec(memory_space=pltpu.VMEM)
+    shapes = [
+        (2 * units + 2 * features, max(model_width + 2 * width, units)),
+        (units, 2 * features),
+    ]
+    return pl.pallas_call(
+        functools.partial(weight_kernel, half_side),
+        out_shape=[jax.ShapeDtypeStruct(shape, jnp.bfloat16) for shape in shapes],
+        in_specs=[vmem] * len(weights),
+        out_specs=[vmem] * len(shapes),
+        name="weights",
+    )(*weights)
+
+
 def forward_kernel(
     half_side,
     corner_ref,
     latent_ref,
-    w_in_ref,
-    w_value_ref,
-    w_gate_ref,
-    w_down_ref,
+    weights_ref,
     w_out_ref,
     canvas_ref,
     cover_ref,
@@ -342,16 +381,14 @@
     patch_ref,
     hidden_ref,
     latent_wide,
-    w_in_spread,
-    w_both,
-    w_noise,
+    spread,
     hidden_all,
     active,
     noise,
 ):
     step = pl.program_id(0)
-    features, model_width = w_in_ref.shape
-    units = w_value_ref.shape[1]
+    model_width, features = w_out_ref.shape
+    units = weights_ref.shape[0] // 2 - features
     slabs, slab_rows, cols = latent_ref.shape
     panels, rows, width = canvas_ref.shape
     own_rows = rows // slabs
@@ -366,21 +403,6 @@
                 latent_wide[panel, slab * own_rows : (slab + 1) * own_rows, :] = own[
                     :, panel * width : (panel + 1) * width
                 ]
-        fold = fold_matrix(features, half_side)
-        w_in_spread[...] = lax.dot_general(
-            w_in_ref[...], fold, (((0,), (0,)), ((), ())), preferred_element_type=jnp.float32
-        ).astype(jnp.bfloat16)
-        w_both[:units, :] = w_value_ref[...].T
-        w_both[units:, :] = w_gate_ref[...].T
-        both = lax.dot_general(
-            w_out_ref[...],
-            w_down_ref[...],
-            (((0,), (1,)), ((), ())),
-            preferred_element_type=jnp.float32,
-        )
-        high, low = split_two(both)
-        w_noise[:features, :] = high
-        w_noise[features:, :] = low
         canvas_ref[...] = jnp.zeros_like(canvas_ref)
         cover_ref[...] = jnp.zeros_like(cover_ref)
         noise[...] = jnp.zeros_like(noise)
@@ -396,37 +418,39 @@
     fold = fold_matrix(features, half_side)
     for tile, (row, col) in enumerate(corners):
         here = slice(tile * tokens, (tile + 1) * tokens)
-        spread = spread_tile(latent_wide, row, col, half_side, features)
-        patch = dot_lanes(fold, spread)
-        patch_ref[:, here] = patch.astype(jnp.bfloat16)
-        hidden_all[:, here] = dot_lanes(w_in_spread[...], spread).astype(jnp.bfloat16)
+        spread[here, :] = spread_tile(latent_wide, row, col, half_side, features)
+    patch_ref[...] = dot_lanes(fold, spread[...]).astype(jnp.bfloat16)
+    hidden_all[...] = dot_lanes(weights_ref[:model_width, model_width:], spread[...]).astype(jnp.bfloat16)
+    for tile in range(tiles_here):
+        here = slice(tile * tokens, (tile + 1) * tokens)
+        base = hidden_all[:chunk_rows, here].astype(jnp.float32)[:1]
         total = jnp.zeros((chunk_rows, tokens), jnp.float32)
+        squares = jnp.zeros((chunk_rows, tokens), jnp.float32)
         for at in range(0, model_width, chunk_rows):
-            total = total + hidden_all[at : at + chunk_rows, here].astype(jnp.float32)
-        mean = jnp.sum(total, axis=0, keepdims=True) * (1.0 / model_width)
-        total = jnp.zeros((chunk_rows, tokens), jnp.float32)
-        for at in range(0, model_width, chunk_rows):
-            center = hidden_all[at : at + chunk_rows, here].astype(jnp.float32) - mean
-            total = total + center * center
-        variance = jnp.sum(total, axis=0, keepdims=True) * (1.0 / model_width)
+            moved = hidden_all[at : at + chunk_rows, here].astype(jnp.float32) - base
+            total = total + moved
+            squares = squares + moved * moved
+        offset = jnp.sum(total, axis=0, keepdims=True) * (1.0 / model_width)
+        mean = base + offset
+        variance = jnp.sum(squares, axis=0, keepdims=True) * (1.0 / model_width) - offset * offset
         inv_scale = lax.rsqrt(variance + layer_eps)
         for at in range(0, model_width, chunk_rows):
             center = hidden_all[at : at + chunk_rows, here].astype(jnp.float32) - mean
             left_ref[at : at + chunk_rows, here] = (center * inv_scale).astype(jnp.bfloat16)
-        high, low = split_two(patch * inv_scale)
+        high, low = split_two(patch_ref[:, here].astype(jnp.float32) * inv_scale)
         left_ref[model_width : model_width + features, here] = high
         left_ref[model_width + features :, here] = low
     for tile in range(tiles_here):
         here = slice(tile * tokens, (tile + 1) * tokens)
         unit = left_ref[:model_width, here]
-        value_ref[:, here] = dot_plain(w_both[:units, :], unit)
-        gate_ref[:, here] = dot_plain(w_both[units:, :], unit)
+        value_ref[:, here] = dot_plain(weights_ref[:units, :model_width], unit)
+        gate_ref[:, here] = dot_plain(weights_ref[units : 2 * units, :model_width], unit)
         for at in range(0, units, chunk_rows):
             value = value_ref[at : at + chunk_rows, here]
             gate = gate_ref[at : at + chunk_rows, here]
-            normal = 0.5 * (1.0 + lax.erf(gate * root_half))
+            normal = 0.5 * lax.erf(gate * root_half) + 0.5
             active[at : at + chunk_rows, here] = (value * (gate * normal)).astype(jnp.bfloat16)
-    parts = dot_plain(w_noise[...], active[...])
+    parts = dot_plain(weights_ref[2 * units :, :units], active[...])
     noise[...] = parts[:features] + parts[features:]
     peers = lax.axis_size("mp")
     for group in range(tiles_here // peers):
@@ -496,6 +520,7 @@
     w_gate_ref,
     w_down_ref,
     w_out_ref,
+    w_through,
     value_ref,
     gate_ref,
     left_ref,
@@ -507,12 +532,12 @@
     grad_down_ref,
     small_ref,
     cot_wide,
-    w_through,
     scaled_sum,
     mean_sum,
     active_sum,
     hidden_sum,
     patch_sum,
+    spread,
     cot,
     d_active,
     d_both,
@@ -522,9 +547,9 @@
     step = pl.program_id(0)
     model_width, features = w_out_ref.shape
     units = w_down_ref.shape[0]
-    slabs, two_slabs, cols = reward_ref.shape
-    slab_rows = two_slabs // 2
+    slabs = reward_ref.shape[0]
     panels, rows, width = sum_ref.shape
+    slab_rows = rows // slabs
     tokens = half_side * half_side
     tiles_here = active.shape[1] // tokens
 
@@ -539,16 +564,13 @@
                 [reward_ref[slab, :slab_rows, lanes] for slab in range(slabs)], axis=0
             )
             curvature = jnp.concatenate(
-                [reward_ref[slab, slab_rows:, lanes] for slab in range(slabs)], axis=0
+                [reward_ref[slab, slab_rows : 2 * slab_rows, lanes] for slab in range(slabs)], axis=0
             )
             cot_wide[panel] = (
                 ((reward - curvature * blended) / cover * scale_factor)
                 .astype(jnp.bfloat16)
                 .astype(jnp.float32)
             )
-        w_through[...] = jnp.concatenate(
-            split_two(dot_plain(w_down_ref[...], w_out_ref[...])), axis=1
-        )
         for ref in (
             grad_value_ref,
             grad_gate_ref,
@@ -562,16 +584,16 @@
 
     for tile in range(tiles_here):
         here = slice(tile * tokens, (tile + 1) * tokens)
-        spread = spread_tile(
+        spread[here, :] = spread_tile(
             cot_wide,
             corner_ref[step * tiles_here + tile, 0],
             corner_ref[step * tiles_here + tile, 1],
             half_side,
             features,
         )
-        cots = dot_lanes(fold_matrix(features, half_side), spread).astype(jnp.bfloat16)
-        cot[:, here] = cots
-        d_active[:, here] = dot_plain(w_through[...], jnp.concatenate([cots, cots], axis=0))
+    cots = dot_lanes(fold_matrix(features, half_side), spread[...]).astype(jnp.bfloat16)
+    cot[...] = cots
+    d_active[...] = dot_plain(w_through[...], jnp.concatenate([cots, cots], axis=0))
     for tile in range(tiles_here):
         here = slice(tile * tokens, (tile + 1) * tokens)
         total = jnp.zeros((chunk_rows, tokens), jnp.float32)
@@ -581,14 +603,15 @@
             gate = gate_ref[chunk, here]
             passed = d_active[chunk, here]
             normal = 0.5 * (1.0 + lax.erf(gate * root_half))
+            gelu = gate * normal
             slope = normal + gate * jnp.exp(-0.5 * gate * gate) * inv_root_two_pi
-            active[chunk, here] = (value * (gate * normal)).astype(jnp.bfloat16)
-            d_value = (passed * (gate * normal)).astype(jnp.bfloat16)
-            d_gate = (passed * value * slope).astype(jnp.bfloat16)
-            d_both[chunk, here] = d_value
-            d_both[units + at : units + at + chunk_rows, here] = d_gate
-            total = total + d_value.astype(jnp.float32) * value
-            total = total + d_gate.astype(jnp.float32) * gate
+            active[chunk, here] = (value * gelu).astype(jnp.bfloat16)
+            product = passed * value
+            d_both[chunk, here] = (passed * gelu).astype(jnp.bfloat16)
+            d_both[units + at : units + at + chunk_rows, here] = (product * slope).astype(
+                jnp.bfloat16
+            )
+            total = total + product * (gelu + slope * gate)
         along = jnp.sum(total, axis=0, keepdims=True) * (1.0 / model_width)
         scaled = left_ref[model_width:, here].astype(jnp.float32)
         high, low = split_two((scaled[:features] + scaled[features:]) * along)
@@ -654,7 +677,7 @@
     return total, other
 
 
-chunk_rows = 32
+chunk_rows = 16
 
 
 def some_tokens(height, tokens):
@@ -678,14 +701,15 @@
     return [jax.ShapeDtypeStruct(shape, kind) for shape, kind in shapes]
 
 
-kernel_params = pltpu.CompilerParams(
-    dimension_semantics=("arbitrary",), vmem_limit_bytes=52 * 2**20
-)
+def kernel_params(megabytes):
+    return pltpu.CompilerParams(
+        dimension_semantics=("arbitrary",), vmem_limit_bytes=megabytes * 2**20
+    )
 
 
 def run_forward(corners, latents, weights, half_side, rows):
-    features, model_width = weights[0].shape
-    units = weights[1].shape[1]
+    model_width, features = weights[1].shape
+    units = weights[0].shape[0] // 2 - features
     tiles = corners.shape[0]
     cols = latents.shape[2]
     steps = tiles // step_tiles(tiles)
@@ -705,22 +729,20 @@
             out_specs=[whole(canvas.shape)] * 2 + [some_tokens(k.shape[0], k.shape[1] // steps) for k in kept],
             scratch_shapes=[
                 pltpu.VMEM(canvas.shape, f32),
-                pltpu.VMEM((model_width, 2 * width), b16),
-                pltpu.VMEM((2 * units, model_width), b16),
-                pltpu.VMEM((2 * features, units), b16),
+                pltpu.VMEM((tokens, 2 * width), b16),
                 pltpu.VMEM((model_width, tokens), b16),
                 pltpu.VMEM((units, tokens), b16),
                 pltpu.VMEM((features, tokens), f32),
             ],
         ),
-        compiler_params=kernel_params,
+        compiler_params=kernel_params(52),
         name="forward",
     )(corners, latents, *weights)
 
 
 def run_backward(corners, total, other, rewards, cover, weights, stored, half_side):
-    features, model_width = weights[0].shape
-    units = weights[1].shape[1]
+    model_width, features = weights[3].shape
+    units = weights[0].shape[1]
     tiles = corners.shape[0]
     token_count = half_side * half_side
     steps = tiles // step_tiles(tiles)
@@ -742,7 +764,7 @@
             grid=(steps,),
             in_specs=[whole(total.shape)] * 2
             + [whole(rewards.shape), whole(cover.shape)]
-            + [whole(w.shape) for w in weights[1:]]
+            + [whole(w.shape) for w in weights]
             + [some_tokens(k.shape[0], k.shape[1] // steps) for k in stored],
             out_specs=[
                 whole((rows, panels * width)),
@@ -753,12 +775,12 @@
             ],
             scratch_shapes=[
                 pltpu.VMEM(total.shape, f32),
-                pltpu.VMEM((units, 2 * features), jnp.bfloat16),
                 pltpu.VMEM((2 * features, 2 * units), f32),
                 pltpu.VMEM((model_width, 2 * features), f32),
                 pltpu.VMEM((units, features), f32),
                 pltpu.VMEM((features, model_width), f32),
                 pltpu.VMEM((features, features), f32),
+                pltpu.VMEM((tokens, 2 * width), jnp.bfloat16),
                 pltpu.VMEM((features, tokens), jnp.bfloat16),
                 pltpu.VMEM((units, tokens), f32),
                 pltpu.VMEM((2 * units, tokens), jnp.bfloat16),
@@ -766,9 +788,46 @@
                 pltpu.VMEM((2 * features, tokens), jnp.bfloat16),
             ],
         ),
-        compiler_params=kernel_params,
+        compiler_params=kernel_params(52),
         name="backward",
-    )(corners, total, other, rewards, cover, *weights[1:], *stored)
+    )(corners, total, other, rewards, cover, *weights, *stored)
+
+
+def pack_kernel(offset_ref, latent_ref, reward_ref, curvature_ref, packed_ref, rewards_ref):
+    copies, packed_rows, cols = packed_ref.shape
+    slab_rows = latent_ref.shape[0]
+    tiles_here = offset_ref.shape[0]
+    lane = lax.broadcasted_iota(jnp.int32, (packed_rows - slab_rows, cols), 1)
+    digits = jnp.zeros(lane.shape, jnp.int32)
+    for tile in range(tiles_here):
+        for axis in range(2):
+            value = offset_ref[tile, axis]
+            at = 2 * tile + axis
+            digits = jnp.where(lane == at, value // 256, digits)
+            digits = jnp.where(lane == 2 * tiles_here + at, value % 256, digits)
+    packed = jnp.concatenate(
+        [latent_ref[...].astype(jnp.float32), digits.astype(jnp.float32)], axis=0
+    ).astype(packed_ref.dtype)
+    rewards = jnp.concatenate([reward_ref[...], curvature_ref[...]], axis=0)
+    for copy in range(copies):
+        packed_ref[copy] = packed
+        rewards_ref[copy] = rewards
+
+
+def run_pack(latent, reward_grad, curvature, offsets, slabs):
+    slab_rows, cols = latent.shape
+    packed_rows = -(-(slab_rows + 1) // 16) * 16
+    vmem = pl.BlockSpec(memory_space=pltpu.VMEM)
+    return pl.pallas_call(
+        pack_kernel,
+        out_shape=[
+            jax.ShapeDtypeStruct((slabs, packed_rows, cols), latent.dtype),
+            jax.ShapeDtypeStruct((slabs, 2 * slab_rows, cols), jnp.float32),
+        ],
+        in_specs=[pl.BlockSpec(memory_space=pltpu.SMEM), vmem, vmem, vmem],
+        out_specs=[vmem, vmem],
+        name="pack",
+    )(offsets, latent, reward_grad, curvature)
 
 
 def per_device_replicated(
@@ -783,24 +842,18 @@
     slabs = lax.axis_size("tile")
     tiles = tiles_here * slabs
     rows = slab_rows * slabs
-    digits = jnp.stack([offsets // 256, offsets % 256]).reshape(1, -1).astype(latent.dtype)
-    digit_row = jnp.pad(digits, ((0, 0), (0, cols - digits.shape[1])))
-    spare = -(slab_rows + 1) % 16
-    packed = jnp.pad(jnp.concatenate([latent, digit_row], axis=0), ((0, spare), (0, 0)))
-
-    def to_all(values):
-        return lax.all_to_all(
-            jnp.broadcast_to(values[None], (slabs,) + values.shape), "tile", 0, 0
-        )
-
-    latents = to_all(packed)
-    rewards = to_all(jnp.concatenate([reward_grad, curvature], axis=0))
+    packed, rewards = run_pack(latent, reward_grad, curvature, offsets, slabs)
+    latents = lax.all_to_all(packed, "tile", 0, 0)
+    rewards = lax.all_to_all(rewards, "tile", 0, 0)
     digits = latents[:, slab_rows, : 4 * tiles_here].astype(jnp.int32)
     digits = digits.reshape(slabs, 2, tiles_here, 2)
     corners = (digits[:, 0] * 256 + digits[:, 1]).reshape(tiles, 2)
 
-    weights = (w_in, w_value, w_gate, w_down, w_out)
-    sums, cover, *stored = run_forward(corners, latents, weights, half_side, rows)
+    packed_weights, w_through = run_weights((w_in, w_value, w_gate, w_down, w_out), half_side)
+    sums, cover, *stored = run_forward(
+        corners, latents, (packed_weights, w_out), half_side, rows
+    )
+    weights = (w_value, w_gate, w_down, w_out, w_through)
     total, other = over_mp(sums)
     blended, grad_value, grad_gate, grad_down, small = run_backward(
         corners, total, other, rewards, cover, weights, stored, half_side
@@ -817,7 +870,7 @@
     tiles = offsets.shape[0] * lax.axis_size("tile")
     stored_bytes = tiles * (S // 2) ** 2 * (8 * w_value.shape[1] + 3 * w_in.shape[1])
     peers = lax.axis_size("mp")
-    pairs = peers > 1 and peers & (peers - 1) == 0 and tiles % peers == 0
+    pairs = w_in.shape[1] <= 2 * w_value.shape[1] and peers > 1 and peers & (peers - 1) == 0 and tiles % peers == 0
     replicate = pairs and stored_bytes <= 40 * 2**20
     plan = per_device_replicated if replicate else per_device_sharded
     return plan(

time: 84.2 us -> 82 us (0.974)
  waiting for transfers between devices: 14.9 us -> 10.7 us
  Pallas kernels: 47.5 us -> 50.8 us
  other arithmetic: 2.33 us -> 0.06 us
  starting transfers between devices: 13.8 us -> 15.3 us
    pallas_call x0 -> x2, Pallas kernels: none -> 5.82 us  [the longest x1 4.23 us: run_weights(): pl.pallas_call(functools.partial(weight_kernel, half_side), out_shape=[ja...]
    all_to_all x2, waiting for transfers between devices: 5.47 us -> 1.36 us  [the longest x1 1.36 us: per_device_replicated(): latents = lax.all_to_all(packed, 'tile', 0, 0)]
    concatenate x2 -> x0, other arithmetic: 1.49 us -> none  [the longest x1 0.77 us: per_device_replicated(): rewards = to_all(jnp.concatenate([reward_grad, curvature], axis=0))]
    broadcast_in_dim x2 -> x0, local copies, waits for them, and re-layouts: 1.39 us -> none  [to_all(): jnp.broadcast_to(values[None], (slabs,) + values.shape)]
    all_to_all x2, starting transfers between devices: 10.7 us -> 12 us  [the longest x1 7.25 us: per_device_replicated(): latents = lax.all_to_all(packed, 'tile', 0, 0)]
    pallas_call x1, Pallas kernels: 25.2 us -> 23.9 us  [run_backward(): pl.pallas_call(functools.partial(backward_kernel, half_side, scale_factor...]
    pallas_call x1, Pallas kernels: 22.2 us -> 21.1 us  [run_forward(): pl.pallas_call(functools.partial(forward_kernel, half_side), out_shape=[c...]
    unnamed x5 -> x7, local copies, waits for them, and re-layouts: 1.62 us -> 2.58 us
  transfers between devices with their start and end apart: 6 -> 6, of which waited for: 5 -> 5; matrix products, arithmetic and copies ran while one was open for 3% -> 3% of each run, Pallas kernels for 27% -> 31%
where the time goes in v3:
time: 82 us; the launch traced here: 81.5 us
  Pallas kernels  50.8 us (62%)
  starting transfers between devices  15.3 us (19%)
  waiting for transfers between devices  10.7 us (13%)
  local copies, waits for them, and re-layouts  4 us (5%)
    pallas_call x1, Pallas kernels, run_backward(): pl.pallas_call(functools.partial(backward_kernel, half_side, scale_factor...  23.9 us
    pallas_call x1, Pallas kernels, run_forward(): pl.pallas_call(functools.partial(forward_kernel, half_side), out_shape=[c...  21.1 us
    ppermute x4, waiting for transfers between devices, over_mp(): other = lax.ppermute(total, 'mp', [(i, i ^ by) for i in range(peers)])  9.29 us
    all_to_all x1, starting transfers between devices, per_device_replicated(): latents = lax.all_to_all(packed, 'tile', 0, 0)  7.25 us
    all_to_all x1, starting transfers between devices, per_device_replicated(): rewards = lax.all_to_all(rewards, 'tile', 0, 0)  4.78 us
    pallas_call x1, Pallas kernels, run_weights(): pl.pallas_call(functools.partial(weight_kernel, half_side), out_shape=[ja...  4.23 us
    ppermute x4, starting transfers between devices, over_mp(): other = lax.ppermute(total, 'mp', [(i, i ^ by) for i in range(peers)])  3.28 us
    unnamed x7, local copies, waits for them, and re-layouts  2.58 us
  transfers between devices with their start and end apart: 6, of which 5 were waited for; matrix products, arithmetic and copies ran while one was open for 3% of the time, Pallas kernels for 31%

profile of v3, /device:TPU:0, one launch (start us, length us, event | category | flops | bytes accessed | tf_op | source)
XLA Modules:
  0.0 81.5 jit_solution(17442015051904366202)
XLA Ops:
  0.6 1.6 %pack.1 = (bf16[8,16,384]{2,1,0:T(8,128)(2,1)}, f32[8,24,384]{2,1,0:T(8,128)}) custom-call(s32[2,2]{1,0:T(2,128)} %offset_ref.1, bf16[12,384]{1,0:T(8,128)(2,1)} %latent_ref.1, f32[12,384]{1,0:T(8,128)} %reward_ref.1, f32[12,384]{1,0:T(8,128)} %curvature_ref.1), custom_call_target="tpu_custom_call" | custom-call | tf_op jit(solution)/shard_map/pack/pallas_call | solution.py:821
  2.2 7.3 %all-to-all-start = ((bf16[8,16,384]{2,1,0:T(8,128)(2,1)}), bf16[8,16,384]{2,1,0:T(8,128)(2,1)S(1)}, u32[]{:S(2)}, u32[]{:S(2)}) async-start(bf16[8,16,384]{2,1,0:T(8,128)(2,1)} %get-tuple-element.22), calls=%async_computation | async-start | bytes 196608 | tf_op jit(solution)/shard_map/all_to_all | solution.py:846
  9.5 1.5 %copy.31.w_out_ref = bf16[640,16]{1,0:T(8,128)(2,1)} copy(bf16[640,16]{0,1:T(8,128)(2,1)} %param.18) | data formatting | bytes 40960 | tf_op args[9]
  11.0 0.0 copy-start
  11.0 4.2 %weights.1 = (bf16[1312,896]{1,0:T(8,128)(2,1)}, bf16[640,32]{1,0:T(8,128)(2,1)}) custom-call(bf16[16,640]{1,0:T(8,128)(2,1)} %w_in_ref.1, bf16[640,640]{1,0:T(8,128)(2,1)} %w_value_ref.3, bf16[640,640]{1,0:T(8,128)(2,1)} %w_gate_ref.3, bf16[640,640]{1,0:T(8,128)(2,1)} %w_down_ref.3, bf16[640,16]{1,0:T(8,128)(2,1)} %copy.31.w_out_ref), custom_call_target="tpu_custom_call" | custom-call | tf_op jit(solution)/shard_map/weights/pallas_call | solution.py:361
  15.2 0.0 copy-start.2
  15.2 1.4 %all-to-all-done.latent_ref = bf16[8,16,384]{2,1,0:T(8,128)(2,1)S(1)} async-done(((bf16[8,16,384]{2,1,0:T(8,128)(2,1)}), bf16[8,16,384]{2,1,0:T(8,128)(2,1)S(1)}, u32[]{:S(2)}, u32[]{:S(2)}) %all-to-all-start) | async-done | bytes 98336 | tf_op jit(solution)/shard_map/all_to_all | solution.py:846
  16.6 4.8 %all-to-all-start.1 = ((f32[8,24,384]{2,1,0:T(8,128)}), f32[8,24,384]{2,1,0:T(8,128)S(1)}, u32[]{:S(2)}, u32[]{:S(2)}) async-start(f32[8,24,384]{2,1,0:T(8,128)} %get-tuple-element.25), calls=%async_computation.1 | async-start | bytes 589824 | tf_op jit(solution)/shard_map/all_to_all | solution.py:847
  21.4 0.1 copy.29
  21.5 0.1 copy.36
  21.6 0.0 copy-done
  21.6 21.1 %forward.1 = (f32[3,96,128]{2,1,0:T(8,128)S(1)}, f32[3,96,128]{2,1,0:T(8,128)S(1)}, f32[640,4096]{1,0:T(8,128)}, f32[640,4096]{1,0:T(8,128)}, bf16[672,4096]{1,0...) custom-call(s32[16,2]{1,0:T(8,128)S(1)} %bitcast.4, ...), custom_call_target="tpu_custom_call" | custom-call | tf_op jit(solution)/shard_map/forward/pallas_call | solution.py:722
  42.6 0.0 copy-start.1
  42.6 1.0 %copy-done.1 = bf16[640,1024]{1,0:T(8,128)(2,1)} copy-done((bf16[640,1024]{1,0:T(8,128)(2,1)}, bf16[640,1024]{1,0:T(8,128)(2,1)S(1)}, u32[]{:S(2)}) %copy-start.1) | copy-done | bytes 1310744
  43.7 0.0 collective-permute-start
  43.7 1.4 %collective-permute-done = f32[3,96,128]{2,1,0:T(8,128)S(1)} collective-permute-done((f32[3,96,128]{2,1,0:T(8,128)S(1)}, f32[3,96,128]{2,1,0:T(8,128)S(1)}, u32[]{:S(2)}, u32[]{:S(2)}) %collective-permute-start) | collective-permute-done | bytes 147488 | tf_op jit(solution)/shard_map/ppermute | solution.py:675
  45.1 1.6 %collective-permute-start.1 = (f32[3,96,128]{2,1,0:T(8,128)S(1)}, f32[3,96,128]{2,1,0:T(8,128)S(1)}, u32[]{:S(2)}, u32[]{:S(2)}) collective-permute-start(f32[3,96,128]{2,1,0:T(8,128)S(1)} %add.21.sum_ref), channel_id=1, source_target_pairs={{0,2},{1,3},{2,0},{3,1},{4,6},{5,7},{6,4},{7,5},{8,10},{9,11},{10,... | collective-permute-start | bytes 442376 | tf_op jit(solution)/shard_map/ppermute | solution.py:675
  46.7 4.3 %collective-permute-done.1.other_ref = f32[3,96,128]{2,1,0:T(8,128)S(1)} collective-permute-done((f32[3,96,128]{2,1,0:T(8,128)S(1)}, f32[3,96,128]{2,1,0:T(8,128)S(1)}, u32[]{:S(2)}, u32[]{:S(2)}) %collective-permute-start.1) | collective-permute-done | bytes 147488 | tf_op jit(solution)/shard_map/ppermute | solution.py:675
  51.0 0.0 all-to-all-done.1.reward_ref
  51.0 0.0 copy-done.2
  51.0 23.9 %backward.1 = (f32[96,384]{1,0:T(8,128)S(1)}, f32[640,640]{1,0:T(8,128)}, f32[640,640]{1,0:T(8,128)}, f32[640,640]{1,0:T(8,128)}, f32[32,640]{1,0:T(8,128)S(1)}) custom-call(s32[16,2]{1,0:T(8,128)S(1)} %bitcast.5, f32[3,96,128]{2,1,0:T(8,128)S(1)} %add.21.sum_ref, f32[3,96,128]{2,1,0:T(8,128)S(1)} %collective-permute-done.1.other_ref, ...), custom_call_target="tpu_custom_call" | custom-call | tf_op jit(solution)/shard_map/backward/pallas_call | solution.py:753
  75.0 0.0 collective-permute-start.2
  75.0 1.3 %collective-permute-done.2 = f32[32,640]{1,0:T(8,128)S(1)} collective-permute-done((f32[32,640]{1,0:T(8,128)S(1)}, f32[32,640]{1,0:T(8,128)S(1)}, u32[]{:S(2)}, u32[]{:S(2)}) %collective-permute-start.2) | collective-permute-done | bytes 81952 | tf_op jit(solution)/shard_map/ppermute | solution.py:675
  76.3 1.6 %collective-permute-start.3 = (f32[32,640]{1,0:T(8,128)S(1)}, f32[32,640]{1,0:T(8,128)S(1)}, u32[]{:S(2)}, u32[]{:S(2)}) collective-permute-start(f32[32,640]{1,0:T(8,128)S(1)} %add.23), channel_id=1, source_target_pairs={{0,2},{1,3},{2,0},{3,1},{4,6},{5,7},{6,4},{7,5},{8,10},{9,11},{10,... | collective-permute-start | bytes 245768 | tf_op jit(solution)/shard_map/ppermute | solution.py:675
  77.9 0.6 constant_dynamic-slice_fusion
  78.5 2.3 %collective-permute-done.3 = f32[32,640]{1,0:T(8,128)S(1)} collective-permute-done((f32[32,640]{1,0:T(8,128)S(1)}, f32[32,640]{1,0:T(8,128)S(1)}, u32[]{:S(2)}, u32[]{:S(2)}) %collective-permute-start.3) | collective-permute-done | bytes 81952 | tf_op jit(solution)/shard_map/ppermute | solution.py:675
  80.9 0.6 slice_bitcast_fusion
  (5 shorter events, 0.1 us)
Async XLA Ops:
  2.2 14.4 %all-to-all-start = ((bf16[8,16,384]{2,1,0:T(8,128)(2,1)}), bf16[8,16,384]{2,1,0:T(8,128)(2,1)S(1)}, u32[]{:S(2)}, u32[]{:S(2)}) async-start(bf16[8,16,384]{2,1,0:T(8,128)(2,1)} %get-tuple-element.22), calls=%async_computation | async-start | bytes 196608 | tf_op jit(solution)/shard_map/all_to_all | solution.py:846
  11.0 10.6 %copy-start = (bf16[640,16]{1,0:T(8,128)(2,1)S(1)}, bf16[640,16]{1,0:T(8,128)(2,1)}, u32[]{:S(2)}) copy-start(bf16[640,16]{1,0:T(8,128)(2,1)} %copy.31.w_out_ref) | copy-start | bytes 61444
  15.2 35.8 %copy-start.2 = (bf16[640,32]{1,0:T(8,128)(2,1)S(1)}, bf16[640,32]{1,0:T(8,128)(2,1)}, u32[]{:S(2)}) copy-start(bf16[640,32]{1,0:T(8,128)(2,1)} %get-tuple-element.27.w_through) | copy-start | bytes 122884
  16.6 34.4 %all-to-all-start.1 = ((f32[8,24,384]{2,1,0:T(8,128)}), f32[8,24,384]{2,1,0:T(8,128)S(1)}, u32[]{:S(2)}, u32[]{:S(2)}) async-start(f32[8,24,384]{2,1,0:T(8,128)} %get-tuple-element.25), calls=%async_computation.1 | async-start | bytes 589824 | tf_op jit(solution)/shard_map/all_to_all | solution.py:847
  42.6 1.0 %copy-start.1 = (bf16[640,1024]{1,0:T(8,128)(2,1)}, bf16[640,1024]{1,0:T(8,128)(2,1)S(1)}, u32[]{:S(2)}) copy-start(bf16[640,1024]{1,0:T(8,128)(2,1)S(1)} %get-tuple-element.32.hidden_ref) | copy-start | bytes 3932164
  43.7 1.4 %collective-permute-start = (f32[3,96,128]{2,1,0:T(8,128)S(1)}, f32[3,96,128]{2,1,0:T(8,128)S(1)}, u32[]{:S(2)}, u32[]{:S(2)}) collective-permute-start(f32[3,96,128]{2,1,0:T(8,128)S(1)} %get-tuple-element.24), channel_id=1, source_target_pairs={{0,1},{1,0},{2,3},{3,2},{4,5},{5,4},{6,7},{7,6},{8,9},{9,8},{10,11... | collective-permute-start | bytes 442376 | tf_op jit(solution)/shard_map/ppermute | solution.py:675
  45.1 6.0 %collective-permute-start.1 = (f32[3,96,128]{2,1,0:T(8,128)S(1)}, f32[3,96,128]{2,1,0:T(8,128)S(1)}, u32[]{:S(2)}, u32[]{:S(2)}) collective-permute-start(f32[3,96,128]{2,1,0:T(8,128)S(1)} %add.21.sum_ref), channel_id=1, source_target_pairs={{0,2},{1,3},{2,0},{3,1},{4,6},{5,7},{6,4},{7,5},{8,10},{9,11},{10,... | collective-permute-start | bytes 442376 | tf_op jit(solution)/shard_map/ppermute | solution.py:675
  75.0 1.3 %collective-permute-start.2 = (f32[32,640]{1,0:T(8,128)S(1)}, f32[32,640]{1,0:T(8,128)S(1)}, u32[]{:S(2)}, u32[]{:S(2)}) collective-permute-start(f32[32,640]{1,0:T(8,128)S(1)} %get-tuple-element.34), channel_id=1, source_target_pairs={{0,1},{1,0},{2,3},{3,2},{4,5},{5,4},{6,7},{7,6},{8,9},{9,8},{10,11... | collective-permute-start | bytes 245768 | tf_op jit(solution)/shard_map/ppermute | solution.py:675
  76.3 4.6 %collective-permute-start.3 = (f32[32,640]{1,0:T(8,128)S(1)}, f32[32,640]{1,0:T(8,128)S(1)}, u32[]{:S(2)}, u32[]{:S(2)}) collective-permute-start(f32[32,640]{1,0:T(8,128)S(1)} %add.23), channel_id=1, source_target_pairs={{0,2},{1,3},{2,0},{3,1},{4,6},{5,7},{6,4},{7,5},{8,10},{9,11},{10,... | collective-permute-start | bytes 245768 | tf_op jit(solution)/shard_map/ppermute | solution.py:675

commit v4 on v3

--- a/solution.py
+++ b/solution.py
@@ -378,8 +378,6 @@
     value_ref,
     gate_ref,
     left_ref,
-    patch_ref,
-    hidden_ref,
     latent_wide,
     spread,
     hidden_all,
@@ -398,7 +396,7 @@
     @pl.when(step == 0)
     def _prepare():
         for slab in range(slabs):
-            own = latent_ref[slab].astype(jnp.float32)[:own_rows]
+            own = latent_ref[slab, : latent_rows(own_rows)].astype(jnp.float32)[:own_rows]
             for panel in range(panels):
                 latent_wide[panel, slab * own_rows : (slab + 1) * own_rows, :] = own[
                     :, panel * width : (panel + 1) * width
@@ -419,7 +417,8 @@
     for tile, (row, col) in enumerate(corners):
         here = slice(tile * tokens, (tile + 1) * tokens)
         spread[here, :] = spread_tile(latent_wide, row, col, half_side, features)
-    patch_ref[...] = dot_lanes(fold, spread[...]).astype(jnp.bfloat16)
+    patch_rows = slice(model_width + 2 * features, None)
+    left_ref[patch_rows, : active.shape[1]] = dot_lanes(fold, spread[...]).astype(jnp.bfloat16)
     hidden_all[...] = dot_lanes(weights_ref[:model_width, model_width:], spread[...]).astype(jnp.bfloat16)
     for tile in range(tiles_here):
         here = slice(tile * tokens, (tile + 1) * tokens)
@@ -437,9 +436,9 @@
         for at in range(0, model_width, chunk_rows):
             center = hidden_all[at : at + chunk_rows, here].astype(jnp.float32) - mean
             left_ref[at : at + chunk_rows, here] = (center * inv_scale).astype(jnp.bfloat16)
-        high, low = split_two(patch_ref[:, here].astype(jnp.float32) * inv_scale)
+        high, low = split_two(left_ref[patch_rows, here].astype(jnp.float32) * inv_scale)
         left_ref[model_width : model_width + features, here] = high
-        left_ref[model_width + features :, here] = low
+        left_ref[model_width + features : model_width + 2 * features, here] = low
     for tile in range(tiles_here):
         here = slice(tile * tokens, (tile + 1) * tokens)
         unit = left_ref[:model_width, here]
@@ -456,7 +455,8 @@
     for group in range(tiles_here // peers):
         own = token_at(group * peers + lax.axis_index("mp"), tokens)
         hidden = hidden_all[:, own]
-        hidden_ref[:, group * tokens : (group + 1) * tokens] = hidden
+        at = active.shape[1] + group * tokens
+        left_ref[:model_width, at : at + tokens] = hidden
         noise[:, own] = noise[:, own] + lax.dot_general(
             w_out_ref[...], hidden, (((0,), (0,)), ((), ())), preferred_element_type=jnp.float32
         )
@@ -516,16 +516,14 @@
     other_ref,
     reward_ref,
     cover_ref,
-    w_value_ref,
-    w_gate_ref,
-    w_down_ref,
+    w_value_far,
+    w_gate_far,
+    w_down_far,
     w_out_ref,
     w_through,
     value_ref,
     gate_ref,
     left_ref,
-    patch_ref,
-    hidden_ref,
     blended_ref,
     grad_value_ref,
     grad_gate_ref,
@@ -543,10 +541,28 @@
     d_both,
     active,
     along_scaled,
+    grad_value,
+    grad_gate,
+    grad_down,
+    w_value_ref,
+    w_gate_ref,
+    w_down_ref,
+    out_sems,
+    in_sems,
 ):
     step = pl.program_id(0)
     model_width, features = w_out_ref.shape
     units = w_down_ref.shape[0]
+    arrivals = [
+        pltpu.make_async_copy(far, near, in_sems.at[index])
+        for index, (far, near) in enumerate(
+            (
+                (w_value_far, w_value_ref),
+                (w_gate_far, w_gate_ref),
+                (w_down_far, w_down_ref),
+            )
+        )
+    ]
     slabs = reward_ref.shape[0]
     panels, rows, width = sum_ref.shape
     slab_rows = rows // slabs
@@ -555,25 +571,30 @@
 
     @pl.when(step == 0)
     def _prepare():
+        for copy in arrivals:
+            copy.start()
         for panel in range(panels):
             lanes = slice(panel * width, (panel + 1) * width)
             cover = cover_ref[panel]
             blended = (sum_ref[panel] + other_ref[panel]) / cover
             blended_ref[:, lanes] = blended
-            reward = jnp.concatenate(
-                [reward_ref[slab, :slab_rows, lanes] for slab in range(slabs)], axis=0
+            parts = []
+            for slab in range(slabs):
+                rewards = reward_ref[slab, :, lanes].astype(jnp.float32)[latent_rows(slab_rows) :]
+                parts.append([rewards[term * slab_rows : (term + 1) * slab_rows] for term in range(4)])
+            high, low, curved_high, curved_low = (
+                jnp.concatenate([part[term] for part in parts], axis=0) for term in range(4)
             )
-            curvature = jnp.concatenate(
-                [reward_ref[slab, slab_rows : 2 * slab_rows, lanes] for slab in range(slabs)], axis=0
-            )
+            reward = high + low
+            curvature = curved_high + curved_low
             cot_wide[panel] = (
                 ((reward - curvature * blended) / cover * scale_factor)
                 .astype(jnp.bfloat16)
                 .astype(jnp.float32)
             )
         for ref in (
-            grad_value_ref,
-            grad_gate_ref,
+            grad_value,
+            grad_gate,
             scaled_sum,
             mean_sum,
             active_sum,
@@ -613,33 +634,48 @@
             )
             total = total + product * (gelu + slope * gate)
         along = jnp.sum(total, axis=0, keepdims=True) * (1.0 / model_width)
-        scaled = left_ref[model_width:, here].astype(jnp.float32)
+        scaled = left_ref[model_width : model_width + 2 * features, here].astype(jnp.float32)
         high, low = split_two((scaled[:features] + scaled[features:]) * along)
         along_scaled[:features, here] = high
         along_scaled[features:, here] = low
-    grads = dot_lanes(left_ref[...], d_both[...])
-    grad_value_ref[...] += grads[:model_width, :units]
-    grad_gate_ref[...] += grads[:model_width, units:]
+    left = left_ref[: model_width + 2 * features, : cot.shape[1]]
+    grads = dot_lanes(left, d_both[...])
+    grad_value[...] += grads[:model_width, :units]
+    grad_gate[...] += grads[:model_width, units:]
     scaled_sum[...] += grads[model_width:]
-    mean_sum[...] += dot_lanes(left_ref[:model_width, :], along_scaled[...])
+    mean_sum[...] += dot_lanes(left[:model_width], along_scaled[...])
     active_sum[...] += dot_lanes(active[...], cot[...])
     peers = lax.axis_size("mp")
     for group in range(tiles_here // peers):
         own = token_at(group * peers + lax.axis_index("mp"), tokens)
         own_cot = cot[:, own]
-        hidden_sum[...] += dot_lanes(
-            own_cot, hidden_ref[:, group * tokens : (group + 1) * tokens]
-        )
-        patch_sum[...] += dot_lanes(patch_ref[:, own], own_cot)
+        at = cot.shape[1] + group * tokens
+        hidden_sum[...] += dot_lanes(own_cot, left_ref[:model_width, at : at + tokens])
+        patch_sum[...] += dot_lanes(left_ref[model_width + 2 * features :, own], own_cot)
 
     @pl.when(step == pl.num_programs(0) - 1)
     def _finish():
+        outs = [
+            pltpu.make_async_copy(buffer, ref, out_sems.at[index])
+            for index, (buffer, ref) in enumerate(
+                (
+                    (grad_value, grad_value_ref),
+                    (grad_gate, grad_gate_ref),
+                    (grad_down, grad_down_ref),
+                )
+            )
+        ]
+        outs[0].start()
+        outs[1].start()
         active_two = jnp.concatenate(split_two(active_sum[...].T), axis=0)
         mean_both = mean_sum[...].T
         w_out_two = jnp.concatenate([w_out_ref[...], w_out_ref[...]], axis=1)
-        grad_down_ref[...] = lax.dot_general(
+        grad_down[...] = lax.dot_general(
             active_two, w_out_two, (((0,), (1,)), ((), ())), preferred_element_type=jnp.float32
         )
+        outs[2].start()
+        for copy in arrivals:
+            copy.wait()
         through = dot_plain(active_two, w_down_ref[...])
         small_ref[features:] = hidden_sum[...] + through[:features] + through[features:]
         scaled_both = scaled_sum[:features] + scaled_sum[features:]
@@ -658,6 +694,8 @@
             - mean_both[:features]
             - mean_both[features:]
         )
+        for copy in outs:
+            copy.wait()
 
 
 def whole(shape):
@@ -691,12 +729,11 @@
 
 def saved_arrays(tiles, token_count, features, model_width, units):
     every = tiles * token_count
+    wide = every + every // lax.axis_size("mp")
     shapes = [
         ((units, every), jnp.float32),
         ((units, every), jnp.float32),
-        ((model_width + 2 * features, every), jnp.bfloat16),
-        ((features, every), jnp.bfloat16),
-        ((model_width, every // lax.axis_size("mp")), jnp.bfloat16),
+        ((model_width + 3 * features, wide), jnp.bfloat16),
     ]
     return [jax.ShapeDtypeStruct(shape, kind) for shape, kind in shapes]
 
@@ -764,13 +801,14 @@
             grid=(steps,),
             in_specs=[whole(total.shape)] * 2
             + [whole(rewards.shape), whole(cover.shape)]
-            + [whole(w.shape) for w in weights]
+            + [pl.BlockSpec(memory_space=pl.ANY)] * 3
+            + [whole(w.shape) for w in weights[3:]]
             + [some_tokens(k.shape[0], k.shape[1] // steps) for k in stored],
             out_specs=[
                 whole((rows, panels * width)),
-                whole((model_width, units)),
-                whole((model_width, units)),
-                whole((units, model_width)),
+                pl.BlockSpec(memory_space=pl.ANY),
+                pl.BlockSpec(memory_space=pl.ANY),
+                pl.BlockSpec(memory_space=pl.ANY),
                 whole((2 * features, model_width)),
             ],
             scratch_shapes=[
@@ -786,6 +824,12 @@
                 pltpu.VMEM((2 * units, tokens), jnp.bfloat16),
                 pltpu.VMEM((units, tokens), jnp.bfloat16),
                 pltpu.VMEM((2 * features, tokens), jnp.bfloat16),
+                pltpu.VMEM((model_width, units), f32),
+                pltpu.VMEM((model_width, units), f32),
+                pltpu.VMEM((units, model_width), f32),
+                *[pltpu.VMEM(w.shape, w.dtype) for w in weights[:3]],
+                pltpu.SemaphoreType.DMA((3,)),
+                pltpu.SemaphoreType.DMA((3,)),
             ],
         ),
         compiler_params=kernel_params(52),
@@ -793,8 +837,9 @@
     )(corners, total, other, rewards, cover, *weights, *stored)
 
 
-def pack_kernel(offset_ref, latent_ref, reward_ref, curvature_ref, packed_ref, rewards_ref):
-    copies, packed_rows, cols = packed_ref.shape
+def pack_kernel(offset_ref, latent_ref, reward_ref, curvature_ref, packed_ref):
+    copies, unused, cols = packed_ref.shape
+    packed_rows = latent_rows(latent_ref.shape[0])
     slab_rows = latent_ref.shape[0]
     tiles_here = offset_ref.shape[0]
     lane = lax.broadcasted_iota(jnp.int32, (packed_rows - slab_rows, cols), 1)
@@ -805,27 +850,29 @@
             at = 2 * tile + axis
             digits = jnp.where(lane == at, value // 256, digits)
             digits = jnp.where(lane == 2 * tiles_here + at, value % 256, digits)
+    rewards = split_two(reward_ref[...]) + split_two(curvature_ref[...])
     packed = jnp.concatenate(
-        [latent_ref[...].astype(jnp.float32), digits.astype(jnp.float32)], axis=0
+        [latent_ref[...].astype(jnp.float32), digits.astype(jnp.float32)]
+        + [part.astype(jnp.float32) for part in rewards],
+        axis=0,
     ).astype(packed_ref.dtype)
-    rewards = jnp.concatenate([reward_ref[...], curvature_ref[...]], axis=0)
     for copy in range(copies):
-        packed_ref[copy] = packed
-        rewards_ref[copy] = rewards
+        packed_ref[copy, : packed.shape[0]] = packed
+
+
+def latent_rows(slab_rows):
+    return -(-(slab_rows + 1) // 16) * 16
 
 
 def run_pack(latent, reward_grad, curvature, offsets, slabs):
     slab_rows, cols = latent.shape
-    packed_rows = -(-(slab_rows + 1) // 16) * 16
+    packed_rows = latent_rows(slab_rows) + 4 * slab_rows
     vmem = pl.BlockSpec(memory_space=pltpu.VMEM)
     return pl.pallas_call(
         pack_kernel,
-        out_shape=[
-            jax.ShapeDtypeStruct((slabs, packed_rows, cols), latent.dtype),
-            jax.ShapeDtypeStruct((slabs, 2 * slab_rows, cols), jnp.float32),
-        ],
+        out_shape=jax.ShapeDtypeStruct((slabs, packed_rows, cols), latent.dtype),
         in_specs=[pl.BlockSpec(memory_space=pltpu.SMEM), vmem, vmem, vmem],
-        out_specs=[vmem, vmem],
+        out_specs=vmem,
         name="pack",
     )(offsets, latent, reward_grad, curvature)
 
@@ -842,9 +889,8 @@
     slabs = lax.axis_size("tile")
     tiles = tiles_here * slabs
     rows = slab_rows * slabs
-    packed, rewards = run_pack(latent, reward_grad, curvature, offsets, slabs)
+    packed = run_pack(latent, reward_grad, curvature, offsets, slabs)
     latents = lax.all_to_all(packed, "tile", 0, 0)
-    rewards = lax.all_to_all(rewards, "tile", 0, 0)
     digits = latents[:, slab_rows, : 4 * tiles_here].astype(jnp.int32)
     digits = digits.reshape(slabs, 2, tiles_here, 2)
     corners = (digits[:, 0] * 256 + digits[:, 1]).reshape(tiles, 2)
@@ -856,7 +902,7 @@
     weights = (w_value, w_gate, w_down, w_out, w_through)
     total, other = over_mp(sums)
     blended, grad_value, grad_gate, grad_down, small = run_backward(
-        corners, total, other, rewards, cover, weights, stored, half_side
+        corners, total, other, latents, cover, weights, stored, half_side
     )
     own = lax.dynamic_slice_in_dim(blended, lax.axis_index("tile") * slab_rows, slab_rows, 0)
     mine, theirs = over_mp(small)

time: 82 us -> 78.8 us (0.961)
  starting transfers between devices: 15.3 us -> 10.6 us
  waiting for transfers between devices: 10.7 us -> 15.1 us
  Pallas kernels: 50.8 us -> 49.1 us
  local copies, waits for them, and re-layouts: 4 us -> 2.95 us
    all_to_all x1 -> x0, starting transfers between devices: 4.78 us -> none  [per_device_replicated(): rewards = lax.all_to_all(rewards, 'tile', 0, 0)]
    all_to_all x1, waiting for transfers between devices: 1.36 us -> 5.8 us  [per_device_replicated(): latents = lax.all_to_all(packed, 'tile', 0, 0)]
    pallas_call x1, Pallas kernels: 23.9 us -> 22.1 us  [run_backward(): pl.pallas_call(functools.partial(backward_kernel, half_side, scale_factor...]
    unnamed x7 -> x5, local copies, waits for them, and re-layouts: 2.58 us -> 1.54 us
  transfers between devices with their start and end apart: 6 -> 5, of which waited for: 5 -> 5; matrix products, arithmetic and copies ran while one was open for 3% -> 3% of each run, Pallas kernels for 31% -> 6%
where the time goes in v4:
time: 78.8 us; the launch traced here: 78.4 us
  Pallas kernels  49.1 us (62%)
  waiting for transfers between devices  15.1 us (19%)
  starting transfers between devices  10.6 us (13%)
  local copies, waits for them, and re-layouts  2.95 us (4%)
    pallas_call x1, Pallas kernels, run_backward(): pl.pallas_call(functools.partial(backward_kernel, half_side, scale_factor...  22.1 us
    pallas_call x1, Pallas kernels, run_forward(): pl.pallas_call(functools.partial(forward_kernel, half_side), out_shape=[c...  21 us
    ppermute x4, waiting for transfers between devices, over_mp(): other = lax.ppermute(total, 'mp', [(i, i ^ by) for i in range(peers)])  9.26 us
    all_to_all x1, starting transfers between devices, per_device_replicated(): latents = lax.all_to_all(packed, 'tile', 0, 0)  7.25 us
    all_to_all x1, waiting for transfers between devices, per_device_replicated(): latents = lax.all_to_all(packed, 'tile', 0, 0)  5.8 us
    pallas_call x1, Pallas kernels, run_weights(): pl.pallas_call(functools.partial(weight_kernel, half_side), out_shape=[ja...  4.36 us
    ppermute x4, starting transfers between devices, over_mp(): other = lax.ppermute(total, 'mp', [(i, i ^ by) for i in range(peers)])  3.36 us
    pallas_call x1, Pallas kernels, run_pack(): pl.pallas_call(pack_kernel, out_shape=jax.ShapeDtypeStruct((slabs, packed...  1.6 us
  transfers between devices with their start and end apart: 5, of which 5 were waited for; matrix products, arithmetic and copies ran while one was open for 3% of the time, Pallas kernels for 6%

profile of v4, /device:TPU:0, one launch (start us, length us, event | category | flops | bytes accessed | tf_op | source)
XLA Modules:
  0.0 78.4 jit_solution(6873372820174036266)
XLA Ops:
  0.6 1.6 %pack.1 = bf16[8,64,384]{2,1,0:T(8,128)(2,1)} custom-call(s32[2,2]{1,0:T(2,128)} %offset_ref.1, bf16[12,384]{1,0:T(8,128)(2,1)} %latent_ref.1, f32[12,384]{1,0:T(8,128)} %reward_ref.1, f32[12,384]{1,0:T(8,128)} %curvature_ref.1), custom_call_target="tpu_custom_call" | custom-call | tf_op jit(solution)/shard_map/pack/pallas_call | solution.py:871
  2.2 7.3 %all-to-all-start = ((bf16[8,64,384]{2,1,0:T(8,128)(2,1)}), bf16[8,64,384]{2,1,0:T(8,128)(2,1)S(1)}, u32[]{:S(2)}, u32[]{:S(2)}) async-start(bf16[8,64,384]{2,1,0:T(8,128)(2,1)} %pack.1), calls=%async_computation | async-start | bytes 786432 | tf_op jit(solution)/shard_map/all_to_all | solution.py:893
  9.5 1.5 %copy.31.w_out_ref = bf16[640,16]{1,0:T(8,128)(2,1)} copy(bf16[640,16]{0,1:T(8,128)(2,1)} %param.18) | data formatting | bytes 40960 | tf_op args[9]
  11.0 0.0 copy-start
  11.0 4.4 %weights.1 = (bf16[1312,896]{1,0:T(8,128)(2,1)}, bf16[640,32]{1,0:T(8,128)(2,1)}) custom-call(bf16[16,640]{1,0:T(8,128)(2,1)} %w_in_ref.1, bf16[640,640]{1,0:T(8,128)(2,1)} %w_value_far.1, bf16[640,640]{1,0:T(8,128)(2,1)} %w_gate_far.1, bf16[640,640]{1,0:T(8,128)(2,1)} %w_down_far.1, bf16[640,16]{1,0:T(8,128)(2,1)} %copy.31.w_out_ref), custom_call_target="tpu_custom_call" | custom-call | tf_op jit(solution)/shard_map/weights/pallas_call | solution.py:361
  15.4 0.0 copy-start.1
  15.4 5.8 %all-to-all-done.latent_ref.reward_ref = bf16[8,64,384]{2,1,0:T(8,128)(2,1)S(1)} async-done(((bf16[8,64,384]{2,1,0:T(8,128)(2,1)}), bf16[8,64,384]{2,1,0:T(8,128)(2,1)S(1)}, u32[]{:S(2)}, u32[]{:S(2)}) %all-to-all-start) | async-done | bytes 393248 | tf_op jit(solution)/shard_map/all_to_all | solution.py:893
  21.2 0.1 copy.29
  21.3 0.1 copy.36
  21.4 0.0 copy-done
  21.4 21.0 %forward.1 = (f32[3,96,128]{2,1,0:T(8,128)S(1)}, f32[3,96,128]{2,1,0:T(8,128)S(1)}, f32[640,4096]{1,0:T(8,128)}, f32[640,4096]{1,0:T(8,128)}, bf16[688,5120]{1,0:T(8,128)(2,1)}) custom-call(s32[16,2]{1,0:T(8,128)S(1)} %bitcast.4, bf16[8,64,384]{2,1,0:T(8,128)(2,1)S(1)} %all-to-all-done.latent_ref.reward_ref, ...), custom_call_target="tpu_custom_call" | custom-call | tf_op jit(solution)/shard_map/forward/pallas_call | solution.py:759
  42.4 0.0 collective-permute-start
  42.4 1.4 %collective-permute-done = f32[3,96,128]{2,1,0:T(8,128)S(1)} collective-permute-done((f32[3,96,128]{2,1,0:T(8,128)S(1)}, f32[3,96,128]{2,1,0:T(8,128)S(1)}, u32[]{:S(2)}, u32[]{:S(2)}) %collective-permute-start) | collective-permute-done | bytes 147488 | tf_op jit(solution)/shard_map/ppermute | solution.py:713
  43.7 1.6 %collective-permute-start.1 = (f32[3,96,128]{2,1,0:T(8,128)S(1)}, f32[3,96,128]{2,1,0:T(8,128)S(1)}, u32[]{:S(2)}, u32[]{:S(2)}) collective-permute-start(f32[3,96,128]{2,1,0:T(8,128)S(1)} %add.21.sum_ref), channel_id=1, source_target_pairs={{0,2},{1,3},{2,0},{3,1},{4,6},{5,7},{6,4},{7,5},{8,10},{9,11},{10,... | collective-permute-start | bytes 442376 | tf_op jit(solution)/shard_map/ppermute | solution.py:713
  45.4 4.3 %collective-permute-done.1.other_ref = f32[3,96,128]{2,1,0:T(8,128)S(1)} collective-permute-done((f32[3,96,128]{2,1,0:T(8,128)S(1)}, f32[3,96,128]{2,1,0:T(8,128)S(1)}, u32[]{:S(2)}, u32[]{:S(2)}) %collective-permute-start.1) | collective-permute-done | bytes 147488 | tf_op jit(solution)/shard_map/ppermute | solution.py:713
  49.7 0.0 copy-done.1
  49.7 22.1 %backward.1 = (f32[96,384]{1,0:T(8,128)S(1)}, f32[640,640]{1,0:T(8,128)}, f32[640,640]{1,0:T(8,128)}, f32[640,640]{1,0:T(8,128)}, f32[32,640]{1,0:T(8,128)S(1)}) custom-call(s32[16,2]{1,0:T(8,128)S(1)} %bitcast.5, f32[3,96,128]{2,1,0:T(8,128)S(1)} %add.21.sum_ref, f32[3,96,128]{2,1,0:T(8,128)S(1)} %collective-permute-done.1.other_ref, ...), custom_call_target="tpu_custom_call" | custom-call | tf_op jit(solution)/shard_map/backward/pallas_call | solution.py:790
  71.9 0.1 collective-permute-start.2
  71.9 1.3 %collective-permute-done.2 = f32[32,640]{1,0:T(8,128)S(1)} collective-permute-done((f32[32,640]{1,0:T(8,128)S(1)}, f32[32,640]{1,0:T(8,128)S(1)}, u32[]{:S(2)}, u32[]{:S(2)}) %collective-permute-start.2) | collective-permute-done | bytes 81952 | tf_op jit(solution)/shard_map/ppermute | solution.py:713
  73.2 1.7 %collective-permute-start.3 = (f32[32,640]{1,0:T(8,128)S(1)}, f32[32,640]{1,0:T(8,128)S(1)}, u32[]{:S(2)}, u32[]{:S(2)}) collective-permute-start(f32[32,640]{1,0:T(8,128)S(1)} %add.23), channel_id=1, source_target_pairs={{0,2},{1,3},{2,0},{3,1},{4,6},{5,7},{6,4},{7,5},{8,10},{9,11},{10,... | collective-permute-start | bytes 245768 | tf_op jit(solution)/shard_map/ppermute | solution.py:713
  74.9 0.6 constant_dynamic-slice_fusion
  75.5 2.3 %collective-permute-done.3 = f32[32,640]{1,0:T(8,128)S(1)} collective-permute-done((f32[32,640]{1,0:T(8,128)S(1)}, f32[32,640]{1,0:T(8,128)S(1)}, u32[]{:S(2)}, u32[]{:S(2)}) %collective-permute-start.3) | collective-permute-done | bytes 81952 | tf_op jit(solution)/shard_map/ppermute | solution.py:713
  77.8 0.6 slice_bitcast_fusion
  (5 shorter events, 0.1 us)
Async XLA Ops:
  2.2 18.9 %all-to-all-start = ((bf16[8,64,384]{2,1,0:T(8,128)(2,1)}), bf16[8,64,384]{2,1,0:T(8,128)(2,1)S(1)}, u32[]{:S(2)}, u32[]{:S(2)}) async-start(bf16[8,64,384]{2,1,0:T(8,128)(2,1)} %pack.1), calls=%async_computation | async-start | bytes 786432 | tf_op jit(solution)/shard_map/all_to_all | solution.py:893
  11.0 10.4 %copy-start = (bf16[640,16]{1,0:T(8,128)(2,1)S(1)}, bf16[640,16]{1,0:T(8,128)(2,1)}, u32[]{:S(2)}) copy-start(bf16[640,16]{1,0:T(8,128)(2,1)} %copy.31.w_out_ref) | copy-start | bytes 61444
  15.4 34.3 %copy-start.1 = (bf16[640,32]{1,0:T(8,128)(2,1)S(1)}, bf16[640,32]{1,0:T(8,128)(2,1)}, u32[]{:S(2)}) copy-start(bf16[640,32]{1,0:T(8,128)(2,1)} %get-tuple-element.21.w_through) | copy-start | bytes 122884
  42.4 1.4 %collective-permute-start = (f32[3,96,128]{2,1,0:T(8,128)S(1)}, f32[3,96,128]{2,1,0:T(8,128)S(1)}, u32[]{:S(2)}, u32[]{:S(2)}) collective-permute-start(f32[3,96,128]{2,1,0:T(8,128)S(1)} %get-tuple-element.19), channel_id=1, source_target_pairs={{0,1},{1,0},{2,3},{3,2},{4,5},{5,4},{6,7},{7,6},{8,9},{9,8},{10,11... | collective-permute-start | bytes 442376 | tf_op jit(solution)/shard_map/ppermute | solution.py:713
  43.7 6.0 %collective-permute-start.1 = (f32[3,96,128]{2,1,0:T(8,128)S(1)}, f32[3,96,128]{2,1,0:T(8,128)S(1)}, u32[]{:S(2)}, u32[]{:S(2)}) collective-permute-start(f32[3,96,128]{2,1,0:T(8,128)S(1)} %add.21.sum_ref), channel_id=1, source_target_pairs={{0,2},{1,3},{2,0},{3,1},{4,6},{5,7},{6,4},{7,5},{8,10},{9,11},{10,... | collective-permute-start | bytes 442376 | tf_op jit(solution)/shard_map/ppermute | solution.py:713
  71.9 1.3 %collective-permute-start.2 = (f32[32,640]{1,0:T(8,128)S(1)}, f32[32,640]{1,0:T(8,128)S(1)}, u32[]{:S(2)}, u32[]{:S(2)}) collective-permute-start(f32[32,640]{1,0:T(8,128)S(1)} %get-tuple-element.26), channel_id=1, source_target_pairs={{0,1},{1,0},{2,3},{3,2},{4,5},{5,4},{6,7},{7,6},{8,9},{9,8},{10,11... | collective-permute-start | bytes 245768 | tf_op jit(solution)/shard_map/ppermute | solution.py:713
  73.2 4.6 %collective-permute-start.3 = (f32[32,640]{1,0:T(8,128)S(1)}, f32[32,640]{1,0:T(8,128)S(1)}, u32[]{:S(2)}, u32[]{:S(2)}) collective-permute-start(f32[32,640]{1,0:T(8,128)S(1)} %add.23), channel_id=1, source_target_pairs={{0,2},{1,3},{2,0},{3,1},{4,6},{5,7},{6,4},{7,5},{8,10},{9,11},{10,... | collective-permute-start | bytes 245768 | tf_op jit(solution)/shard_map/ppermute | solution.py:713

commit v5 on v4

--- a/solution.py
+++ b/solution.py
@@ -301,7 +301,13 @@
     return token % half_side == place // run % half_side
 
 
-def spread_tile(canvas_ref, row, col, half_side, features):
+def repeat_matrix(half_side):
+    token = lax.broadcasted_iota(jnp.int32, (half_side * half_side, half_side), 0)
+    patch_row = lax.broadcasted_iota(jnp.int32, (half_side * half_side, half_side), 1)
+    return jnp.where(token // half_side == patch_row, 1.0, 0.0).astype(jnp.bfloat16)
+
+
+def spread_tile(canvas_ref, row, col, half_side, features, mask, repeat):
     run = features // 2
     width = half_side * run
     panels = canvas_ref.shape[0]
@@ -314,11 +320,7 @@
         rolled = pltpu.roll(rows, lax.rem(cols - lanes, cols), 1)
         halves.append(rolled[:, :width])
     pair = jnp.concatenate(halves, axis=1).astype(jnp.bfloat16)
-    token = lax.broadcasted_iota(jnp.int32, (half_side * half_side, half_side), 0)
-    patch_row = lax.broadcasted_iota(jnp.int32, (half_side * half_side, half_side), 1)
-    repeat = jnp.where(token // half_side == patch_row, 1.0, 0.0).astype(jnp.bfloat16)
-    repeated = dot_plain(repeat, pair)
-    return jnp.where(column_mask(features, half_side), repeated, 0.0).astype(jnp.bfloat16)
+    return (dot_plain(repeat[...], pair) * mask[...]).astype(jnp.bfloat16)
 
 
 def token_at(tile, tokens):
@@ -383,6 +385,8 @@
     hidden_all,
     active,
     noise,
+    mask,
+    repeat,
 ):
     step = pl.program_id(0)
     model_width, features = w_out_ref.shape
@@ -404,6 +408,8 @@
         canvas_ref[...] = jnp.zeros_like(canvas_ref)
         cover_ref[...] = jnp.zeros_like(cover_ref)
         noise[...] = jnp.zeros_like(noise)
+        mask[...] = jnp.where(column_mask(features, half_side), 1.0, 0.0)
+        repeat[...] = repeat_matrix(half_side)
 
     def corners_of(group):
         return [
@@ -412,11 +418,15 @@
         ]
 
     corners = corners_of(step)
-    add_noise(canvas_ref, noise[...], corners_of(jnp.maximum(step - 1, 0)), half_side, features)
+    add_noise(
+        canvas_ref, noise[...], corners_of(jnp.maximum(step - 1, 0)), half_side, features, mask
+    )
     fold = fold_matrix(features, half_side)
     for tile, (row, col) in enumerate(corners):
         here = slice(tile * tokens, (tile + 1) * tokens)
-        spread[here, :] = spread_tile(latent_wide, row, col, half_side, features)
+        spread[here, :] = spread_tile(
+            latent_wide, row, col, half_side, features, mask, repeat
+        )
     patch_rows = slice(model_width + 2 * features, None)
     left_ref[patch_rows, : active.shape[1]] = dot_lanes(fold, spread[...]).astype(jnp.bfloat16)
     hidden_all[...] = dot_lanes(weights_ref[:model_width, model_width:], spread[...]).astype(jnp.bfloat16)
@@ -463,7 +473,7 @@
 
     @pl.when(step == pl.num_programs(0) - 1)
     def _last():
-        add_noise(canvas_ref, noise[...], corners, half_side, features)
+        add_noise(canvas_ref, noise[...], corners, half_side, features, mask)
 
     shape = cover_ref.shape
     row_at = lax.broadcasted_iota(jnp.int32, shape, 1)
@@ -483,7 +493,7 @@
     cover_ref[...] = cover
 
 
-def add_noise(canvas_ref, noise, corners, half_side, features):
+def add_noise(canvas_ref, noise, corners, half_side, features, mask):
     run = features // 2
     width = half_side * run
     panels = canvas_ref.shape[0]
@@ -495,7 +505,7 @@
         preferred_element_type=jnp.float32,
     )
     tall = tall.reshape(len(corners), half_side * half_side, 2 * width)
-    kept = jnp.where(column_mask(features, half_side)[None], tall, 0.0)
+    kept = tall * mask[...][None]
     pairs = jnp.sum(kept.reshape(len(corners), half_side, half_side, 2 * width), axis=2)
     blank = jnp.zeros((half_side, (panels - 1) * width), jnp.float32)
     for tile, (row, col) in enumerate(corners):
@@ -547,6 +557,8 @@
     w_value_ref,
     w_gate_ref,
     w_down_ref,
+    mask,
+    repeat,
     out_sems,
     in_sems,
 ):
@@ -573,6 +585,8 @@
     def _prepare():
         for copy in arrivals:
             copy.start()
+        mask[...] = jnp.where(column_mask(features, half_side), 1.0, 0.0)
+        repeat[...] = repeat_matrix(half_side)
         for panel in range(panels):
             lanes = slice(panel * width, (panel + 1) * width)
             cover = cover_ref[panel]
@@ -611,6 +625,8 @@
             corner_ref[step * tiles_here + tile, 1],
             half_side,
             features,
+            mask,
+            repeat,
         )
     cots = dot_lanes(fold_matrix(features, half_side), spread[...]).astype(jnp.bfloat16)
     cot[...] = cots
@@ -644,7 +660,7 @@
     grad_gate[...] += grads[:model_width, units:]
     scaled_sum[...] += grads[model_width:]
     mean_sum[...] += dot_lanes(left[:model_width], along_scaled[...])
-    active_sum[...] += dot_lanes(active[...], cot[...])
+    active_sum[...] += dot_lanes(cot[...], active[...])
     peers = lax.axis_size("mp")
     for group in range(tiles_here // peers):
         own = token_at(group * peers + lax.axis_index("mp"), tokens)
@@ -667,7 +683,7 @@
         ]
         outs[0].start()
         outs[1].start()
-        active_two = jnp.concatenate(split_two(active_sum[...].T), axis=0)
+        active_two = jnp.concatenate(split_two(active_sum[...]), axis=0)
         mean_both = mean_sum[...].T
         w_out_two = jnp.concatenate([w_out_ref[...], w_out_ref[...]], axis=1)
         grad_down[...] = lax.dot_general(
@@ -770,6 +786,8 @@
                 pltpu.VMEM((model_width, tokens), b16),
                 pltpu.VMEM((units, tokens), b16),
                 pltpu.VMEM((features, tokens), f32),
+                pltpu.VMEM((half_side * half_side, 2 * width), f32),
+                pltpu.VMEM((half_side * half_side, half_side), b16),
             ],
         ),
         compiler_params=kernel_params(52),
@@ -815,7 +833,7 @@
                 pltpu.VMEM(total.shape, f32),
                 pltpu.VMEM((2 * features, 2 * units), f32),
                 pltpu.VMEM((model_width, 2 * features), f32),
-                pltpu.VMEM((units, features), f32),
+                pltpu.VMEM((features, units), f32),
                 pltpu.VMEM((features, model_width), f32),
                 pltpu.VMEM((features, features), f32),
                 pltpu.VMEM((tokens, 2 * width), jnp.bfloat16),
@@ -828,6 +846,8 @@
                 pltpu.VMEM((model_width, units), f32),
                 pltpu.VMEM((units, model_width), f32),
                 *[pltpu.VMEM(w.shape, w.dtype) for w in weights[:3]],
+                pltpu.VMEM((half_side * half_side, 2 * width), f32),
+                pltpu.VMEM((half_side * half_side, half_side), jnp.bfloat16),
                 pltpu.SemaphoreType.DMA((3,)),
                 pltpu.SemaphoreType.DMA((3,)),
             ],

time: 78.8 us -> 78.1 us (level)
  no operation moved by 1% of the time
where the time goes in v5:
time: 78.1 us; the launch traced here: 77.7 us
  Pallas kernels  48.4 us (62%)
  waiting for transfers between devices  15.1 us (19%)
  starting transfers between devices  10.6 us (14%)
  local copies, waits for them, and re-layouts  2.95 us (4%)
    pallas_call x1, Pallas kernels, run_backward(): pl.pallas_call(functools.partial(backward_kernel, half_side, scale_factor...  21.5 us
    pallas_call x1, Pallas kernels, run_forward(): pl.pallas_call(functools.partial(forward_kernel, half_side), out_shape=[c...  20.9 us
    ppermute x4, waiting for transfers between devices, over_mp(): other = lax.ppermute(total, 'mp', [(i, i ^ by) for i in range(peers)])  9.27 us
    all_to_all x1, starting transfers between devices, per_device_replicated(): latents = lax.all_to_all(packed, 'tile', 0, 0)  7.25 us
    all_to_all x1, waiting for transfers between devices, per_device_replicated(): latents = lax.all_to_all(packed, 'tile', 0, 0)  5.8 us
    pallas_call x1, Pallas kernels, run_weights(): pl.pallas_call(functools.partial(weight_kernel, half_side), out_shape=[ja...  4.36 us
    ppermute x4, starting transfers between devices, over_mp(): other = lax.ppermute(total, 'mp', [(i, i ^ by) for i in range(peers)])  3.35 us
    pallas_call x1, Pallas kernels, run_pack(): pl.pallas_call(pack_kernel, out_shape=jax.ShapeDtypeStruct((slabs, packed...  1.6 us
  transfers between devices with their start and end apart: 5, of which 5 were waited for; matrix products, arithmetic and copies ran while one was open for 3% of the time, Pallas kernels for 6%

profile of v5, /device:TPU:0, one launch (start us, length us, event | category | flops | bytes accessed | tf_op | source)
XLA Modules:
  0.0 77.7 jit_solution(15547976654702033524)
XLA Ops:
  0.6 1.6 %pack.1 = bf16[8,64,384]{2,1,0:T(8,128)(2,1)} custom-call(s32[2,2]{1,0:T(2,128)} %offset_ref.1, bf16[12,384]{1,0:T(8,128)(2,1)} %latent_ref.1, f32[12,384]{1,0:T(8,128)} %reward_ref.1, f32[12,384]{1,0:T(8,128)} %curvature_ref.1), custom_call_target="tpu_custom_call" | custom-call | tf_op jit(solution)/shard_map/pack/pallas_call | solution.py:891
  2.2 7.3 %all-to-all-start = ((bf16[8,64,384]{2,1,0:T(8,128)(2,1)}), bf16[8,64,384]{2,1,0:T(8,128)(2,1)S(1)}, u32[]{:S(2)}, u32[]{:S(2)}) async-start(bf16[8,64,384]{2,1,0:T(8,128)(2,1)} %pack.1), calls=%async_computation | async-start | bytes 786432 | tf_op jit(solution)/shard_map/all_to_all | solution.py:913
  9.5 1.5 %copy.31.w_out_ref = bf16[640,16]{1,0:T(8,128)(2,1)} copy(bf16[640,16]{0,1:T(8,128)(2,1)} %param.18) | data formatting | bytes 40960 | tf_op args[9]
  11.0 0.0 copy-start
  11.0 4.4 %weights.1 = (bf16[1312,896]{1,0:T(8,128)(2,1)}, bf16[640,32]{1,0:T(8,128)(2,1)}) custom-call(bf16[16,640]{1,0:T(8,128)(2,1)} %w_in_ref.1, bf16[640,640]{1,0:T(8,128)(2,1)} %w_value_far.1, bf16[640,640]{1,0:T(8,128)(2,1)} %w_gate_far.1, bf16[640,640]{1,0:T(8,128)(2,1)} %w_down_far.1, bf16[640,16]{1,0:T(8,128)(2,1)} %copy.31.w_out_ref), custom_call_target="tpu_custom_call" | custom-call | tf_op jit(solution)/shard_map/weights/pallas_call | solution.py:363
  15.4 0.0 copy-start.1
  15.4 5.8 %all-to-all-done.latent_ref.reward_ref = bf16[8,64,384]{2,1,0:T(8,128)(2,1)S(1)} async-done(((bf16[8,64,384]{2,1,0:T(8,128)(2,1)}), bf16[8,64,384]{2,1,0:T(8,128)(2,1)S(1)}, u32[]{:S(2)}, u32[]{:S(2)}) %all-to-all-start) | async-done | bytes 393248 | tf_op jit(solution)/shard_map/all_to_all | solution.py:913
  21.2 0.1 copy.29
  21.3 0.1 copy.36
  21.4 0.0 copy-done
  21.4 20.9 %forward.1 = (f32[3,96,128]{2,1,0:T(8,128)S(1)}, f32[3,96,128]{2,1,0:T(8,128)S(1)}, f32[640,4096]{1,0:T(8,128)}, f32[640,4096]{1,0:T(8,128)}, bf16[688,5120]{1,0:T(8,128)(2,1)}) custom-call(s32[16,2]{1,0:T(8,128)S(1)} %bitcast.4, bf16[8,64,384]{2,1,0:T(8,128)(2,1)S(1)} %all-to-all-done.latent_ref.reward_ref, ...), custom_call_target="tpu_custom_call" | custom-call | tf_op jit(solution)/shard_map/forward/pallas_call | solution.py:775
  42.3 0.0 collective-permute-start
  42.3 1.4 %collective-permute-done = f32[3,96,128]{2,1,0:T(8,128)S(1)} collective-permute-done((f32[3,96,128]{2,1,0:T(8,128)S(1)}, f32[3,96,128]{2,1,0:T(8,128)S(1)}, u32[]{:S(2)}, u32[]{:S(2)}) %collective-permute-start) | collective-permute-done | bytes 147488 | tf_op jit(solution)/shard_map/ppermute | solution.py:729
  43.6 1.6 %collective-permute-start.1 = (f32[3,96,128]{2,1,0:T(8,128)S(1)}, f32[3,96,128]{2,1,0:T(8,128)S(1)}, u32[]{:S(2)}, u32[]{:S(2)}) collective-permute-start(f32[3,96,128]{2,1,0:T(8,128)S(1)} %add.21.sum_ref), channel_id=1, source_target_pairs={{0,2},{1,3},{2,0},{3,1},{4,6},{5,7},{6,4},{7,5},{8,10},{9,11},{10,... | collective-permute-start | bytes 442376 | tf_op jit(solution)/shard_map/ppermute | solution.py:729
  45.3 4.3 %collective-permute-done.1.other_ref = f32[3,96,128]{2,1,0:T(8,128)S(1)} collective-permute-done((f32[3,96,128]{2,1,0:T(8,128)S(1)}, f32[3,96,128]{2,1,0:T(8,128)S(1)}, u32[]{:S(2)}, u32[]{:S(2)}) %collective-permute-start.1) | collective-permute-done | bytes 147488 | tf_op jit(solution)/shard_map/ppermute | solution.py:729
  49.6 0.0 copy-done.1
  49.6 21.5 %backward.1 = (f32[96,384]{1,0:T(8,128)S(1)}, f32[640,640]{1,0:T(8,128)}, f32[640,640]{1,0:T(8,128)}, f32[640,640]{1,0:T(8,128)}, f32[32,640]{1,0:T(8,128)S(1)}) custom-call(s32[16,2]{1,0:T(8,128)S(1)} %bitcast.5, f32[3,96,128]{2,1,0:T(8,128)S(1)} %add.21.sum_ref, f32[3,96,128]{2,1,0:T(8,128)S(1)} %collective-permute-done.1.other_ref, ...), custom_call_target="tpu_custom_call" | custom-call | tf_op jit(solution)/shard_map/backward/pallas_call | solution.py:808
  71.1 0.1 collective-permute-start.2
  71.2 1.3 %collective-permute-done.2 = f32[32,640]{1,0:T(8,128)S(1)} collective-permute-done((f32[32,640]{1,0:T(8,128)S(1)}, f32[32,640]{1,0:T(8,128)S(1)}, u32[]{:S(2)}, u32[]{:S(2)}) %collective-permute-start.2) | collective-permute-done | bytes 81952 | tf_op jit(solution)/shard_map/ppermute | solution.py:729
  72.5 1.6 %collective-permute-start.3 = (f32[32,640]{1,0:T(8,128)S(1)}, f32[32,640]{1,0:T(8,128)S(1)}, u32[]{:S(2)}, u32[]{:S(2)}) collective-permute-start(f32[32,640]{1,0:T(8,128)S(1)} %add.23), channel_id=1, source_target_pairs={{0,2},{1,3},{2,0},{3,1},{4,6},{5,7},{6,4},{7,5},{8,10},{9,11},{10,... | collective-permute-start | bytes 245768 | tf_op jit(solution)/shard_map/ppermute | solution.py:729
  74.1 0.6 constant_dynamic-slice_fusion
  74.7 2.3 %collective-permute-done.3 = f32[32,640]{1,0:T(8,128)S(1)} collective-permute-done((f32[32,640]{1,0:T(8,128)S(1)}, f32[32,640]{1,0:T(8,128)S(1)}, u32[]{:S(2)}, u32[]{:S(2)}) %collective-permute-start.3) | collective-permute-done | bytes 81952 | tf_op jit(solution)/shard_map/ppermute | solution.py:729
  77.1 0.6 slice_bitcast_fusion
  (5 shorter events, 0.1 us)
Async XLA Ops:
  2.2 18.9 %all-to-all-start = ((bf16[8,64,384]{2,1,0:T(8,128)(2,1)}), bf16[8,64,384]{2,1,0:T(8,128)(2,1)S(1)}, u32[]{:S(2)}, u32[]{:S(2)}) async-start(bf16[8,64,384]{2,1,0:T(8,128)(2,1)} %pack.1), calls=%async_computation | async-start | bytes 786432 | tf_op jit(solution)/shard_map/all_to_all | solution.py:913
  11.0 10.4 %copy-start = (bf16[640,16]{1,0:T(8,128)(2,1)S(1)}, bf16[640,16]{1,0:T(8,128)(2,1)}, u32[]{:S(2)}) copy-start(bf16[640,16]{1,0:T(8,128)(2,1)} %copy.31.w_out_ref) | copy-start | bytes 61444
  15.4 34.2 %copy-start.1 = (bf16[640,32]{1,0:T(8,128)(2,1)S(1)}, bf16[640,32]{1,0:T(8,128)(2,1)}, u32[]{:S(2)}) copy-start(bf16[640,32]{1,0:T(8,128)(2,1)} %get-tuple-element.21.w_through) | copy-start | bytes 122884
  42.3 1.4 %collective-permute-start = (f32[3,96,128]{2,1,0:T(8,128)S(1)}, f32[3,96,128]{2,1,0:T(8,128)S(1)}, u32[]{:S(2)}, u32[]{:S(2)}) collective-permute-start(f32[3,96,128]{2,1,0:T(8,128)S(1)} %get-tuple-element.19), channel_id=1, source_target_pairs={{0,1},{1,0},{2,3},{3,2},{4,5},{5,4},{6,7},{7,6},{8,9},{9,8},{10,11... | collective-permute-start | bytes 442376 | tf_op jit(solution)/shard_map/ppermute | solution.py:729
  43.6 6.0 %collective-permute-start.1 = (f32[3,96,128]{2,1,0:T(8,128)S(1)}, f32[3,96,128]{2,1,0:T(8,128)S(1)}, u32[]{:S(2)}, u32[]{:S(2)}) collective-permute-start(f32[3,96,128]{2,1,0:T(8,128)S(1)} %add.21.sum_ref), channel_id=1, source_target_pairs={{0,2},{1,3},{2,0},{3,1},{4,6},{5,7},{6,4},{7,5},{8,10},{9,11},{10,... | collective-permute-start | bytes 442376 | tf_op jit(solution)/shard_map/ppermute | solution.py:729
  71.1 1.3 %collective-permute-start.2 = (f32[32,640]{1,0:T(8,128)S(1)}, f32[32,640]{1,0:T(8,128)S(1)}, u32[]{:S(2)}, u32[]{:S(2)}) collective-permute-start(f32[32,640]{1,0:T(8,128)S(1)} %get-tuple-element.26), channel_id=1, source_target_pairs={{0,1},{1,0},{2,3},{3,2},{4,5},{5,4},{6,7},{7,6},{8,9},{9,8},{10,11... | collective-permute-start | bytes 245768 | tf_op jit(solution)/shard_map/ppermute | solution.py:729
  72.5 4.6 %collective-permute-start.3 = (f32[32,640]{1,0:T(8,128)S(1)}, f32[32,640]{1,0:T(8,128)S(1)}, u32[]{:S(2)}, u32[]{:S(2)}) collective-permute-start(f32[32,640]{1,0:T(8,128)S(1)} %add.23), channel_id=1, source_target_pairs={{0,2},{1,3},{2,0},{3,1},{4,6},{5,7},{6,4},{7,5},{8,10},{9,11},{10,... | collective-permute-start | bytes 245768 | tf_op jit(solution)/shard_map/ppermute | solution.py:729

commit v6 on v5

--- a/solution.py
+++ b/solution.py
@@ -387,6 +387,7 @@
     noise,
     mask,
     repeat,
+    canvas_sum,
 ):
     step = pl.program_id(0)
     model_width, features = w_out_ref.shape
@@ -405,7 +406,7 @@
                 latent_wide[panel, slab * own_rows : (slab + 1) * own_rows, :] = own[
                     :, panel * width : (panel + 1) * width
                 ]
-        canvas_ref[...] = jnp.zeros_like(canvas_ref)
+        canvas_sum[...] = jnp.zeros_like(canvas_sum)
         cover_ref[...] = jnp.zeros_like(cover_ref)
         noise[...] = jnp.zeros_like(noise)
         mask[...] = jnp.where(column_mask(features, half_side), 1.0, 0.0)
@@ -419,7 +420,7 @@
 
     corners = corners_of(step)
     add_noise(
-        canvas_ref, noise[...], corners_of(jnp.maximum(step - 1, 0)), half_side, features, mask
+        canvas_sum, noise[...], corners_of(jnp.maximum(step - 1, 0)), half_side, features, mask
     )
     fold = fold_matrix(features, half_side)
     for tile, (row, col) in enumerate(corners):
@@ -473,7 +474,8 @@
 
     @pl.when(step == pl.num_programs(0) - 1)
     def _last():
-        add_noise(canvas_ref, noise[...], corners, half_side, features, mask)
+        add_noise(canvas_sum, noise[...], corners, half_side, features, mask)
+        canvas_ref[...] = canvas_sum[:, :rows, :]
 
     shape = cover_ref.shape
     row_at = lax.broadcasted_iota(jnp.int32, shape, 1)
@@ -601,7 +603,7 @@
             )
             reward = high + low
             curvature = curved_high + curved_low
-            cot_wide[panel] = (
+            cot_wide[panel, :rows] = (
                 ((reward - curvature * blended) / cover * scale_factor)
                 .astype(jnp.bfloat16)
                 .astype(jnp.float32)
@@ -781,13 +783,14 @@
             in_specs=[whole(latents.shape)] + [whole(w.shape) for w in weights],
             out_specs=[whole(canvas.shape)] * 2 + [some_tokens(k.shape[0], k.shape[1] // steps) for k in kept],
             scratch_shapes=[
-                pltpu.VMEM(canvas.shape, f32),
+                pltpu.VMEM((cols // width, rows + 8, width), f32),
                 pltpu.VMEM((tokens, 2 * width), b16),
                 pltpu.VMEM((model_width, tokens), b16),
                 pltpu.VMEM((units, tokens), b16),
                 pltpu.VMEM((features, tokens), f32),
                 pltpu.VMEM((half_side * half_side, 2 * width), f32),
                 pltpu.VMEM((half_side * half_side, half_side), b16),
+                pltpu.VMEM((cols // width, rows + 8, width), f32),
             ],
         ),
         compiler_params=kernel_params(52),
@@ -830,7 +833,7 @@
                 whole((2 * features, model_width)),
             ],
             scratch_shapes=[
-                pltpu.VMEM(total.shape, f32),
+                pltpu.VMEM((panels, rows + 8, width), f32),
                 pltpu.VMEM((2 * features, 2 * units), f32),
                 pltpu.VMEM((model_width, 2 * features), f32),
                 pltpu.VMEM((features, units), f32),

time: 78.1 us -> 78.2 us (level)
  no operation moved by 1% of the time
where the time goes in v6:
time: 78.2 us; the launch traced here: 77.8 us
  Pallas kernels  48.4 us (62%)
  waiting for transfers between devices  15.1 us (19%)
  starting transfers between devices  10.5 us (13%)
  local copies, waits for them, and re-layouts  2.95 us (4%)
    pallas_call x1, Pallas kernels, run_backward(): pl.pallas_call(functools.partial(backward_kernel, half_side, scale_factor...  21.5 us
    pallas_call x1, Pallas kernels, run_forward(): pl.pallas_call(functools.partial(forward_kernel, half_side), out_shape=[c...  21 us
    ppermute x4, waiting for transfers between devices, over_mp(): other = lax.ppermute(total, 'mp', [(i, i ^ by) for i in range(peers)])  9.35 us
    all_to_all x1, starting transfers between devices, per_device_replicated(): latents = lax.all_to_all(packed, 'tile', 0, 0)  7.25 us
    all_to_all x1, waiting for transfers between devices, per_device_replicated(): latents = lax.all_to_all(packed, 'tile', 0, 0)  5.8 us
    pallas_call x1, Pallas kernels, run_weights(): pl.pallas_call(functools.partial(weight_kernel, half_side), out_shape=[ja...  4.36 us
    ppermute x4, starting transfers between devices, over_mp(): other = lax.ppermute(total, 'mp', [(i, i ^ by) for i in range(peers)])  3.27 us
    pallas_call x1, Pallas kernels, run_pack(): pl.pallas_call(pack_kernel, out_shape=jax.ShapeDtypeStruct((slabs, packed...  1.6 us
  transfers between devices with their start and end apart: 5, of which 5 were waited for; matrix products, arithmetic and copies ran while one was open for 3% of the time, Pallas kernels for 6%

profile of v6, /device:TPU:0, one launch (start us, length us, event | category | flops | bytes accessed | tf_op | source)
XLA Modules:
  0.0 77.8 jit_solution(13827179035175781941)
XLA Ops:
  0.6 1.6 %pack.1 = bf16[8,64,384]{2,1,0:T(8,128)(2,1)} custom-call(s32[2,2]{1,0:T(2,128)} %offset_ref.1, bf16[12,384]{1,0:T(8,128)(2,1)} %latent_ref.1, f32[12,384]{1,0:T(8,128)} %reward_ref.1, f32[12,384]{1,0:T(8,128)} %curvature_ref.1), custom_call_target="tpu_custom_call" | custom-call | tf_op jit(solution)/shard_map/pack/pallas_call | solution.py:894
  2.2 7.3 %all-to-all-start = ((bf16[8,64,384]{2,1,0:T(8,128)(2,1)}), bf16[8,64,384]{2,1,0:T(8,128)(2,1)S(1)}, u32[]{:S(2)}, u32[]{:S(2)}) async-start(bf16[8,64,384]{2,1,0:T(8,128)(2,1)} %pack.1), calls=%async_computation | async-start | bytes 786432 | tf_op jit(solution)/shard_map/all_to_all | solution.py:916
  9.5 1.5 %copy.31.w_out_ref = bf16[640,16]{1,0:T(8,128)(2,1)} copy(bf16[640,16]{0,1:T(8,128)(2,1)} %param.18) | data formatting | bytes 40960 | tf_op args[9]
  11.0 0.0 copy-start
  11.0 4.4 %weights.1 = (bf16[1312,896]{1,0:T(8,128)(2,1)}, bf16[640,32]{1,0:T(8,128)(2,1)}) custom-call(bf16[16,640]{1,0:T(8,128)(2,1)} %w_in_ref.1, bf16[640,640]{1,0:T(8,128)(2,1)} %w_value_far.1, bf16[640,640]{1,0:T(8,128)(2,1)} %w_gate_far.1, bf16[640,640]{1,0:T(8,128)(2,1)} %w_down_far.1, bf16[640,16]{1,0:T(8,128)(2,1)} %copy.31.w_out_ref), custom_call_target="tpu_custom_call" | custom-call | tf_op jit(solution)/shard_map/weights/pallas_call | solution.py:363
  15.4 0.0 copy-start.1
  15.4 5.8 %all-to-all-done.latent_ref.reward_ref = bf16[8,64,384]{2,1,0:T(8,128)(2,1)S(1)} async-done(((bf16[8,64,384]{2,1,0:T(8,128)(2,1)}), bf16[8,64,384]{2,1,0:T(8,128)(2,1)S(1)}, u32[]{:S(2)}, u32[]{:S(2)}) %all-to-all-start) | async-done | bytes 393248 | tf_op jit(solution)/shard_map/all_to_all | solution.py:916
  21.2 0.1 copy.29
  21.3 0.1 copy.36
  21.4 0.0 copy-done
  21.4 21.0 %forward.1 = (f32[3,96,128]{2,1,0:T(8,128)S(1)}, f32[3,96,128]{2,1,0:T(8,128)S(1)}, f32[640,4096]{1,0:T(8,128)}, f32[640,4096]{1,0:T(8,128)}, bf16[688,5120]{1,0:T(8,128)(2,1)}) custom-call(s32[16,2]{1,0:T(8,128)S(1)} %bitcast.4, bf16[8,64,384]{2,1,0:T(8,128)(2,1)S(1)} %all-to-all-done.latent_ref.reward_ref, ...), custom_call_target="tpu_custom_call" | custom-call | tf_op jit(solution)/shard_map/forward/pallas_call | solution.py:777
  42.3 0.0 collective-permute-start
  42.3 1.4 %collective-permute-done = f32[3,96,128]{2,1,0:T(8,128)S(1)} collective-permute-done((f32[3,96,128]{2,1,0:T(8,128)S(1)}, f32[3,96,128]{2,1,0:T(8,128)S(1)}, u32[]{:S(2)}, u32[]{:S(2)}) %collective-permute-start) | collective-permute-done | bytes 147488 | tf_op jit(solution)/shard_map/ppermute | solution.py:731
  43.7 1.6 %collective-permute-start.1 = (f32[3,96,128]{2,1,0:T(8,128)S(1)}, f32[3,96,128]{2,1,0:T(8,128)S(1)}, u32[]{:S(2)}, u32[]{:S(2)}) collective-permute-start(f32[3,96,128]{2,1,0:T(8,128)S(1)} %add.21.sum_ref), channel_id=1, source_target_pairs={{0,2},{1,3},{2,0},{3,1},{4,6},{5,7},{6,4},{7,5},{8,10},{9,11},{10,... | collective-permute-start | bytes 442376 | tf_op jit(solution)/shard_map/ppermute | solution.py:731
  45.3 4.4 %collective-permute-done.1.other_ref = f32[3,96,128]{2,1,0:T(8,128)S(1)} collective-permute-done((f32[3,96,128]{2,1,0:T(8,128)S(1)}, f32[3,96,128]{2,1,0:T(8,128)S(1)}, u32[]{:S(2)}, u32[]{:S(2)}) %collective-permute-start.1) | collective-permute-done | bytes 147488 | tf_op jit(solution)/shard_map/ppermute | solution.py:731
  49.7 0.0 copy-done.1
  49.7 21.5 %backward.1 = (f32[96,384]{1,0:T(8,128)S(1)}, f32[640,640]{1,0:T(8,128)}, f32[640,640]{1,0:T(8,128)}, f32[640,640]{1,0:T(8,128)}, f32[32,640]{1,0:T(8,128)S(1)}) custom-call(s32[16,2]{1,0:T(8,128)S(1)} %bitcast.5, f32[3,96,128]{2,1,0:T(8,128)S(1)} %add.21.sum_ref, f32[3,96,128]{2,1,0:T(8,128)S(1)} %collective-permute-done.1.other_ref, ...), custom_call_target="tpu_custom_call" | custom-call | tf_op jit(solution)/shard_map/backward/pallas_call | solution.py:811
  71.2 0.1 collective-permute-start.2
  71.3 1.3 %collective-permute-done.2 = f32[32,640]{1,0:T(8,128)S(1)} collective-permute-done((f32[32,640]{1,0:T(8,128)S(1)}, f32[32,640]{1,0:T(8,128)S(1)}, u32[]{:S(2)}, u32[]{:S(2)}) %collective-permute-start.2) | collective-permute-done | bytes 81952 | tf_op jit(solution)/shard_map/ppermute | solution.py:731
  72.6 1.6 %collective-permute-start.3 = (f32[32,640]{1,0:T(8,128)S(1)}, f32[32,640]{1,0:T(8,128)S(1)}, u32[]{:S(2)}, u32[]{:S(2)}) collective-permute-start(f32[32,640]{1,0:T(8,128)S(1)} %add.23), channel_id=1, source_target_pairs={{0,2},{1,3},{2,0},{3,1},{4,6},{5,7},{6,4},{7,5},{8,10},{9,11},{10,... | collective-permute-start | bytes 245768 | tf_op jit(solution)/shard_map/ppermute | solution.py:731
  74.2 0.6 constant_dynamic-slice_fusion
  74.8 2.4 %collective-permute-done.3 = f32[32,640]{1,0:T(8,128)S(1)} collective-permute-done((f32[32,640]{1,0:T(8,128)S(1)}, f32[32,640]{1,0:T(8,128)S(1)}, u32[]{:S(2)}, u32[]{:S(2)}) %collective-permute-start.3) | collective-permute-done | bytes 81952 | tf_op jit(solution)/shard_map/ppermute | solution.py:731
  77.2 0.6 slice_bitcast_fusion
  (5 shorter events, 0.1 us)
Async XLA Ops:
  2.2 18.9 %all-to-all-start = ((bf16[8,64,384]{2,1,0:T(8,128)(2,1)}), bf16[8,64,384]{2,1,0:T(8,128)(2,1)S(1)}, u32[]{:S(2)}, u32[]{:S(2)}) async-start(bf16[8,64,384]{2,1,0:T(8,128)(2,1)} %pack.1), calls=%async_computation | async-start | bytes 786432 | tf_op jit(solution)/shard_map/all_to_all | solution.py:916
  11.0 10.4 %copy-start = (bf16[640,16]{1,0:T(8,128)(2,1)S(1)}, bf16[640,16]{1,0:T(8,128)(2,1)}, u32[]{:S(2)}) copy-start(bf16[640,16]{1,0:T(8,128)(2,1)} %copy.31.w_out_ref) | copy-start | bytes 61444
  15.4 34.3 %copy-start.1 = (bf16[640,32]{1,0:T(8,128)(2,1)S(1)}, bf16[640,32]{1,0:T(8,128)(2,1)}, u32[]{:S(2)}) copy-start(bf16[640,32]{1,0:T(8,128)(2,1)} %get-tuple-element.21.w_through) | copy-start | bytes 122884
  42.3 1.4 %collective-permute-start = (f32[3,96,128]{2,1,0:T(8,128)S(1)}, f32[3,96,128]{2,1,0:T(8,128)S(1)}, u32[]{:S(2)}, u32[]{:S(2)}) collective-permute-start(f32[3,96,128]{2,1,0:T(8,128)S(1)} %get-tuple-element.19), channel_id=1, source_target_pairs={{0,1},{1,0},{2,3},{3,2},{4,5},{5,4},{6,7},{7,6},{8,9},{9,8},{10,11... | collective-permute-start | bytes 442376 | tf_op jit(solution)/shard_map/ppermute | solution.py:731
  43.7 6.0 %collective-permute-start.1 = (f32[3,96,128]{2,1,0:T(8,128)S(1)}, f32[3,96,128]{2,1,0:T(8,128)S(1)}, u32[]{:S(2)}, u32[]{:S(2)}) collective-permute-start(f32[3,96,128]{2,1,0:T(8,128)S(1)} %add.21.sum_ref), channel_id=1, source_target_pairs={{0,2},{1,3},{2,0},{3,1},{4,6},{5,7},{6,4},{7,5},{8,10},{9,11},{10,... | collective-permute-start | bytes 442376 | tf_op jit(solution)/shard_map/ppermute | solution.py:731
  71.2 1.3 %collective-permute-start.2 = (f32[32,640]{1,0:T(8,128)S(1)}, f32[32,640]{1,0:T(8,128)S(1)}, u32[]{:S(2)}, u32[]{:S(2)}) collective-permute-start(f32[32,640]{1,0:T(8,128)S(1)} %get-tuple-element.26), channel_id=1, source_target_pairs={{0,1},{1,0},{2,3},{3,2},{4,5},{5,4},{6,7},{7,6},{8,9},{9,8},{10,11... | collective-permute-start | bytes 245768 | tf_op jit(solution)/shard_map/ppermute | solution.py:731
  72.6 4.6 %collective-permute-start.3 = (f32[32,640]{1,0:T(8,128)S(1)}, f32[32,640]{1,0:T(8,128)S(1)}, u32[]{:S(2)}, u32[]{:S(2)}) collective-permute-start(f32[32,640]{1,0:T(8,128)S(1)} %add.23), channel_id=1, source_target_pairs={{0,2},{1,3},{2,0},{3,1},{4,6},{5,7},{6,4},{7,5},{8,10},{9,11},{10,... | collective-permute-start | bytes 245768 | tf_op jit(solution)/shard_map/ppermute | solution.py:731
